TPU v7x, 32 devices: a whole 2x2x4 slice. The times are simulated.
32 devices in a mesh: gx: 4 (over z), gy: 8 (over y, x, core).
Axes of the slice: x: 2, y: 2, z: 4, core: 2. Of those that a mesh axis runs over, the one named last changes fastest.
Arguments:
- particles: float32 [384, 6, 128], P(('gx', 'gy')), may hold values from -6 to 6
- occupancy: int32 [384], P(('gx', 'gy')), may hold values from 32 to 128, as said below
- neighbours: int32 [384, 16], P(('gx', 'gy')), may hold values from 0 to 383, as said below
- curve_cuts: int32 [2, 32], replicated, may hold values from 0 to 378, as said below
Outputs:
- after_first: float32 [768, 6, 128], P(('gx', 'gy'))
- after_second: float32 [768, 6, 128], P(('gx', 'gy'))
Inputs may be any that keep to these rules, and one draw needn't show every extreme that they name: `occupancy`: each tile holds at least 32 live particles, and some tile in every draw holds 128. `neighbours`: tile t lists 16 different tiles among the curve positions t + 1 to t + 24, counted modulo 384. `curve_cuts`: entry d of each row is d * 12 + e with e between -6 and 6, and e is 0 for device 0; so each device owns 0 to 24 tiles, and in every step some device owns exactly 24.
All inputs are finite; a program needn't handle non-finite values.
Results may differ from a plain program's by a relative error of at most 0.0001.
Values sent between devices are 32-bit elements; how exact they have to be, the bound alone decides.
No kernel may reach another device: no remote copies, remote signals or barrier semaphores. Data moves between devices by JAX's collectives and lax.ppermute only.
A program may use at most 64 MiB of HBM per device.

v0:
```python
import jax
import jax.numpy as jnp
from jax import lax
from jax.sharding import PartitionSpec as P

TILE_P = 128
STEPS = 2


soften = 0.05
time_step = 0.5
group_tiles = 2


def shifted(value, axis, steps):
    count = lax.axis_size(axis)
    pairs = [(source, (source + steps) % count) for source in range(count)]
    return lax.ppermute(value, axis, pairs)


def shifted_2(value, axis, steps):
    count = lax.axis_size(axis)
    first, last = (max(0, -steps), min(count, count - steps))
    return lax.ppermute(value, axis, [(source, source + steps) for source in range(first, last)])


def pair_terms(targets, sources):
    target_pos = targets[:, None, :3, :, None]
    source_pos = sources[:, :, :3, None, :]
    separation = source_pos - target_pos
    distance_sq = jnp.sum(separation * separation, axis=2) + soften
    kernel = distance_sq ** (-1.5)
    action = jnp.sum(
        kernel[:, :, None] * sources[:, :, 3][:, :, None, None, :] * separation, axis=(1, 4)
    )
    reaction = -jnp.sum(
        kernel[:, :, None] * targets[:, 3][:, None, None, :, None] * separation, axis=3
    )
    return (action, reaction)


def pair_scan(own_pos, tile_pool, source_index):
    tile_count = own_pos.shape[0]
    slot_count = own_pos.shape[2]
    group_count = tile_count // group_tiles

    def block_pass(react_pool, inputs):
        targets, source_ids = inputs
        sources = jnp.concatenate(
            [targets[:, None], jnp.take(tile_pool, source_ids, axis=0)], axis=1
        )
        action, reaction = pair_terms(targets, sources)
        react_pool = react_pool.at[source_ids.reshape(-1)].add(
            reaction[:, 1:].reshape(-1, 3, slot_count)
        )
        return (react_pool, action)

    start_pool = jnp.zeros((tile_pool.shape[0], 3, slot_count), jnp.float32)
    react_pool, actions = lax.scan(
        block_pass,
        start_pool,
        (
            own_pos.reshape(group_count, group_tiles, 4, slot_count),
            source_index.reshape(group_count, group_tiles, -1),
        ),
    )
    return (actions.reshape(tile_count, 3, slot_count), react_pool)


def home_forces(own_pos, home_offsets, tiles_home):
    windows = [own_pos]
    for distance in range(1, 3):
        windows.append(shifted(own_pos, ("gx", "gy"), -distance))
    tile_pool = jnp.concatenate(windows, axis=0)
    source_index = jnp.arange(tiles_home, dtype=jnp.int32)[:, None] + home_offsets
    actions, react_pool = pair_scan(own_pos, tile_pool, source_index)
    acceleration = actions + react_pool[:tiles_home]
    for distance in range(1, 3):
        returned = shifted(
            react_pool[distance * tiles_home : (distance + 1) * tiles_home], ("gx", "gy"), distance
        )
        acceleration = acceleration + returned
    return acceleration


def place_home(state_rows, new_starts, device, tiles_home, capacity):
    half_tiles = tiles_home // 2
    lower_rows = shifted_2(state_rows[tiles_home - half_tiles :], ("gx", "gy"), 1)
    upper_rows = shifted_2(state_rows[:half_tiles], ("gx", "gy"), -1)
    pool_rows = jnp.concatenate([lower_rows, state_rows, upper_rows], axis=0)
    own_new = new_starts[device]
    next_new = new_starts[device + 1]
    wanted = own_new + jnp.arange(capacity, dtype=jnp.int32)
    filled = (wanted < next_new).astype(jnp.float32)
    source_index = jnp.clip(wanted - (device * tiles_home - half_tiles), 0, 2 * tiles_home - 1)
    return jnp.take(pool_rows, source_index, axis=0) * filled[:, None, None]


def body(particles, occupancy, neighbours, curve_cuts):
    device = lax.axis_index(("gx", "gy"))
    mesh_size = lax.axis_size(("gx", "gy"))
    tiles_home = particles.shape[0]
    slot_count = particles.shape[2]
    total_tiles = tiles_home * mesh_size
    capacity = 2 * tiles_home
    slot_ids = jnp.arange(slot_count, dtype=jnp.int32)
    weight = (slot_ids[None, :] < occupancy[:, None]).astype(jnp.float32)
    home_tiles = device * tiles_home + jnp.arange(tiles_home, dtype=jnp.int32)
    home_offsets = (neighbours - home_tiles[:, None]) % total_tiles
    tail_entry = jnp.array([total_tiles], jnp.int32)
    snapshots = []
    live_weight = weight[:, None]
    position = particles[:, :3]
    velocity = particles[:, 3:]
    for step_index in range(STEPS):
        new_starts = jnp.concatenate([curve_cuts[step_index], tail_entry])
        own_pos = jnp.concatenate([position, live_weight], axis=1)
        acceleration = home_forces(own_pos, home_offsets, tiles_home)
        velocity = live_weight * (velocity + time_step * acceleration / TILE_P)
        position = live_weight * (position + time_step * velocity)
        state_rows = jnp.concatenate([position, velocity], axis=1)
        snapshots.append(place_home(state_rows, new_starts, device, tiles_home, capacity))
    return (snapshots[0], snapshots[1])


def solution(mesh):
    in_specs = (P(("gx", "gy"), None, None), P(("gx", "gy")), P(("gx", "gy"), None), P())
    out_specs = (P(("gx", "gy"), None, None), P(("gx", "gy"), None, None))
    return jax.shard_map(body, mesh=mesh, in_specs=in_specs, out_specs=out_specs, check_vma=False)
```

profile of v0, /device:TPU:1, one launch (start us, length us, event | category | flops | bytes accessed | tf_op | source)
XLA Modules:
  0.0 124.7 jit_solution(650095179593546269)
XLA Ops:
  2.3 6.7 %collective-permute-start.1 = (f32[12,4,128]{2,1,0:T(4,128)S(1)}, f32[12,4,128]{2,1,0:T(4,128)S(1)}, u32[]{:S(2)}, u32[]{:S(2)}) collective-permute-start(f32[12,4,128]{2,1,0:T(4,128)S(1)} %pad_maximum_fusion.9), channel_id=1, source_target_pairs={{0,30},{1,31},{2,0},{3,1},{4,2},{5,3},{6,4},{7,5},{8,6},{9,7},{10,... | collective-permute-start | bytes 73736 | tf_op jit(solution)/shard_map/ppermute | solution.py:18
  14.6 1.2 compare_convert_fusion.2
  16.0 39.0 %while.24 = (s32[]{:T(128)}, f32[36,3,128]{2,1,0:T(4,128)S(1)}, f32[6,2,3,128]{3,2,1,0:T(4,128)S(1)}, s32[6,2,16]{2,1,0:T(2,128)S(1)}, f32[6,2,4,128]{3,2,1,0:T(...) while((s32[]{:T(128)}, f32[36,3,128]{2,1,0:T(4,128)S(1)}, f32[6,2,3,128]{3,2,1,0:T(4,128)S(1)}, ...), condition=%wide.region_5.7_spmd, body=%wide.region_0.6_spmd.sunk | while | flops 14529410 | bytes 14446425 | solution.py:59
  17.9 1.0 fusion.56
  18.9 1.8 %fusion.57 = (f32[2,3,128]{2,1,0:T(4,128)S(1)}, f32[2,17,3,128]{3,2,1,0:T(4,128)S(1)}) fusion(f32[2,17,128,128]{3,2,1,0:T(8,128)S(1)} %get-tuple-element.234, f32[2,3,128]{2,1,0:T(4,128)S(1)} %bitcast.118, f32[2,17,3,128]{3,2,1,0:T(4,128)S(1)} %copy.70, f32[2,17,128,128]{3,2,1,0:T(8,128)S(1)} %get-tuple-element.235), kind=kLoop, calls=%fused_computation.11.clone.1 | loop fusion | flops 8342016 | bytes 4567040 | tf_op jit(solution)/shard_map/while/body/eval_jaxpr/reduce_sum | solution.py:33
  20.8 1.6 %scatter_fusion = f32[36,3,128]{2,1,0:T(4,128)S(1)} fusion(f32[36,3,128]{2,1,0:T(4,128)S(1)} %get-tuple-element.260, s32[32]{0:T(128)S(1)} %fusion.52, f32[32,3,128]{2,1,0:T(4,128)S(1)} %bitcast.112), kind=kCustom, calls=%fused_computation.4.clone.1 | custom fusion | flops 12288 | bytes 147584 | tf_op jit(solution)/shard_map/while/body/eval_jaxpr/scatter-add | solution.py:53
  24.4 1.0 fusion.56
  25.4 1.8 %fusion.57 = (f32[2,3,128]{2,1,0:T(4,128)S(1)}, f32[2,17,3,128]{3,2,1,0:T(4,128)S(1)}) fusion(f32[2,17,128,128]{3,2,1,0:T(8,128)S(1)} %get-tuple-element.234, f32[2,3,128]{2,1,0:T(4,128)S(1)} %bitcast.118, f32[2,17,3,128]{3,2,1,0:T(4,128)S(1)} %copy.70, f32[2,17,128,128]{3,2,1,0:T(8,128)S(1)} %get-tuple-element.235), kind=kLoop, calls=%fused_computation.11.clone.1 | loop fusion | flops 8342016 | bytes 4567040 | tf_op jit(solution)/shard_map/while/body/eval_jaxpr/reduce_sum | solution.py:33
  27.3 1.6 %scatter_fusion = f32[36,3,128]{2,1,0:T(4,128)S(1)} fusion(f32[36,3,128]{2,1,0:T(4,128)S(1)} %get-tuple-element.260, s32[32]{0:T(128)S(1)} %fusion.52, f32[32,3,128]{2,1,0:T(4,128)S(1)} %bitcast.112), kind=kCustom, calls=%fused_computation.4.clone.1 | custom fusion | flops 12288 | bytes 147584 | tf_op jit(solution)/shard_map/while/body/eval_jaxpr/scatter-add | solution.py:53
  30.9 1.0 fusion.56
  31.9 1.8 %fusion.57 = (f32[2,3,128]{2,1,0:T(4,128)S(1)}, f32[2,17,3,128]{3,2,1,0:T(4,128)S(1)}) fusion(f32[2,17,128,128]{3,2,1,0:T(8,128)S(1)} %get-tuple-element.234, f32[2,3,128]{2,1,0:T(4,128)S(1)} %bitcast.118, f32[2,17,3,128]{3,2,1,0:T(4,128)S(1)} %copy.70, f32[2,17,128,128]{3,2,1,0:T(8,128)S(1)} %get-tuple-element.235), kind=kLoop, calls=%fused_computation.11.clone.1 | loop fusion | flops 8342016 | bytes 4567040 | tf_op jit(solution)/shard_map/while/body/eval_jaxpr/reduce_sum | solution.py:33
  33.8 1.6 %scatter_fusion = f32[36,3,128]{2,1,0:T(4,128)S(1)} fusion(f32[36,3,128]{2,1,0:T(4,128)S(1)} %get-tuple-element.260, s32[32]{0:T(128)S(1)} %fusion.52, f32[32,3,128]{2,1,0:T(4,128)S(1)} %bitcast.112), kind=kCustom, calls=%fused_computation.4.clone.1 | custom fusion | flops 12288 | bytes 147584 | tf_op jit(solution)/shard_map/while/body/eval_jaxpr/scatter-add | solution.py:53
  37.4 1.0 fusion.56
  38.4 1.8 %fusion.57 = (f32[2,3,128]{2,1,0:T(4,128)S(1)}, f32[2,17,3,128]{3,2,1,0:T(4,128)S(1)}) fusion(f32[2,17,128,128]{3,2,1,0:T(8,128)S(1)} %get-tuple-element.234, f32[2,3,128]{2,1,0:T(4,128)S(1)} %bitcast.118, f32[2,17,3,128]{3,2,1,0:T(4,128)S(1)} %copy.70, f32[2,17,128,128]{3,2,1,0:T(8,128)S(1)} %get-tuple-element.235), kind=kLoop, calls=%fused_computation.11.clone.1 | loop fusion | flops 8342016 | bytes 4567040 | tf_op jit(solution)/shard_map/while/body/eval_jaxpr/reduce_sum | solution.py:33
  40.3 1.6 %scatter_fusion = f32[36,3,128]{2,1,0:T(4,128)S(1)} fusion(f32[36,3,128]{2,1,0:T(4,128)S(1)} %get-tuple-element.260, s32[32]{0:T(128)S(1)} %fusion.52, f32[32,3,128]{2,1,0:T(4,128)S(1)} %bitcast.112), kind=kCustom, calls=%fused_computation.4.clone.1 | custom fusion | flops 12288 | bytes 147584 | tf_op jit(solution)/shard_map/while/body/eval_jaxpr/scatter-add | solution.py:53
  43.9 1.0 fusion.56
  44.8 1.8 %fusion.57 = (f32[2,3,128]{2,1,0:T(4,128)S(1)}, f32[2,17,3,128]{3,2,1,0:T(4,128)S(1)}) fusion(f32[2,17,128,128]{3,2,1,0:T(8,128)S(1)} %get-tuple-element.234, f32[2,3,128]{2,1,0:T(4,128)S(1)} %bitcast.118, f32[2,17,3,128]{3,2,1,0:T(4,128)S(1)} %copy.70, f32[2,17,128,128]{3,2,1,0:T(8,128)S(1)} %get-tuple-element.235), kind=kLoop, calls=%fused_computation.11.clone.1 | loop fusion | flops 8342016 | bytes 4567040 | tf_op jit(solution)/shard_map/while/body/eval_jaxpr/reduce_sum | solution.py:33
  46.8 1.6 %scatter_fusion = f32[36,3,128]{2,1,0:T(4,128)S(1)} fusion(f32[36,3,128]{2,1,0:T(4,128)S(1)} %get-tuple-element.260, s32[32]{0:T(128)S(1)} %fusion.52, f32[32,3,128]{2,1,0:T(4,128)S(1)} %bitcast.112), kind=kCustom, calls=%fused_computation.4.clone.1 | custom fusion | flops 12288 | bytes 147584 | tf_op jit(solution)/shard_map/while/body/eval_jaxpr/scatter-add | solution.py:53
  50.4 1.0 fusion.56
  51.3 1.8 %fusion.57 = (f32[2,3,128]{2,1,0:T(4,128)S(1)}, f32[2,17,3,128]{3,2,1,0:T(4,128)S(1)}) fusion(f32[2,17,128,128]{3,2,1,0:T(8,128)S(1)} %get-tuple-element.234, f32[2,3,128]{2,1,0:T(4,128)S(1)} %bitcast.118, f32[2,17,3,128]{3,2,1,0:T(4,128)S(1)} %copy.70, f32[2,17,128,128]{3,2,1,0:T(8,128)S(1)} %get-tuple-element.235), kind=kLoop, calls=%fused_computation.11.clone.1 | loop fusion | flops 8342016 | bytes 4567040 | tf_op jit(solution)/shard_map/while/body/eval_jaxpr/reduce_sum | solution.py:33
  53.3 1.6 %scatter_fusion = f32[36,3,128]{2,1,0:T(4,128)S(1)} fusion(f32[36,3,128]{2,1,0:T(4,128)S(1)} %get-tuple-element.260, s32[32]{0:T(128)S(1)} %fusion.52, f32[32,3,128]{2,1,0:T(4,128)S(1)} %bitcast.112), kind=kCustom, calls=%fused_computation.4.clone.1 | custom fusion | flops 12288 | bytes 147584 | tf_op jit(solution)/shard_map/while/body/eval_jaxpr/scatter-add | solution.py:53
  55.0 1.4 %collective-permute-start.2 = (f32[12,3,128]{2,1,0:T(4,128)S(1)}, f32[12,3,128]{2,1,0:T(4,128)S(1)}, u32[]{:S(2)}, u32[]{:S(2)}) collective-permute-start(f32[12,3,128]{2,1,0:T(4,128)S(1)} %get-tuple-element.132), channel_id=1, source_target_pairs={{0,1},{1,2},{2,3},{3,4},{4,5},{5,6},{6,7},{7,8},{8,9},{9,10},{10,1... | collective-permute-start | bytes 55304 | tf_op jit(solution)/shard_map/ppermute | solution.py:18
  56.4 1.3 %compare_convert_fusion.3 = f32[24]{0:T(128)S(1)} fusion(s32[]{:T(128)} %bitcast.22, s32[]{:T(128)} %bitcast.19), kind=kLoop, calls=%fused_computation.106 | loop fusion | flops 72 | bytes 104 | tf_op jit(solution)/shard_map/convert_element_type | solution.py:94
  57.7 5.0 %collective-permute-done.3 = f32[12,3,128]{2,1,0:T(4,128)S(1)} collective-permute-done((f32[12,3,128]{2,1,0:T(4,128)S(1)}, f32[12,3,128]{2,1,0:T(4,128)S(1)}, u32[]{:S(2)}, u32[]{:S(2)}) %collective-permute-start.3) | collective-permute-done | bytes 18464 | tf_op jit(solution)/shard_map/ppermute | solution.py:18
  63.2 3.9 %collective-permute-start.4 = (f32[6,6,128]{2,1,0:T(8,128)S(1)}, f32[6,6,128]{2,1,0:T(8,128)S(1)}, u32[]{:S(2)}, u32[]{:S(2)}) collective-permute-start(f32[6,6,128]{2,1,0:T(8,128)S(1)} %get-tuple-element.136), channel_id=1, source_target_pairs={{0,1},{1,2},{2,3},{3,4},{4,5},{5,6},{6,7},{7,8},{8,9},{9,10},{10,1... | collective-permute-start | bytes 55304 | tf_op jit(solution)/shard_map/ppermute | solution.py:24
  67.1 1.9 %collective-permute-start.5 = (f32[6,6,128]{2,1,0:T(8,128)S(1)}, f32[6,6,128]{2,1,0:T(8,128)S(1)}, u32[]{:S(2)}, u32[]{:S(2)}) collective-permute-start(f32[6,6,128]{2,1,0:T(8,128)S(1)} %get-tuple-element.137), channel_id=1, source_target_pairs={{1,0},{2,1},{3,2},{4,3},{5,4},{6,5},{7,6},{8,7},{9,8},{10,9},{11,1... | collective-permute-start | bytes 55304 | tf_op jit(solution)/shard_map/ppermute | solution.py:24
  69.1 39.0 %while.25 = (s32[]{:T(128)}, f32[36,3,128]{2,1,0:T(4,128)S(1)}, f32[6,2,3,128]{3,2,1,0:T(4,128)S(1)}, s32[6,2,16]{2,1,0:T(2,128)S(1)}, f32[6,2,4,128]{3,2,1,0:T(...) while((s32[]{:T(128)}, f32[36,3,128]{2,1,0:T(4,128)S(1)}, f32[6,2,3,128]{3,2,1,0:T(4,128)S(1)}, ...), condition=%wide.region_11.14_spmd, body=%wide.region_6.13_spmd.sunk | while | flops 14529410 | bytes 14446425 | solution.py:59
  71.0 1.0 fusion.62
  72.0 1.8 %fusion.63 = (f32[2,3,128]{2,1,0:T(4,128)S(1)}, f32[2,17,3,128]{3,2,1,0:T(4,128)S(1)}) fusion(f32[2,17,128,128]{3,2,1,0:T(8,128)S(1)} %get-tuple-element.248, f32[2,3,128]{2,1,0:T(4,128)S(1)} %bitcast.120, f32[2,17,3,128]{3,2,1,0:T(4,128)S(1)} %copy.75, f32[2,17,128,128]{3,2,1,0:T(8,128)S(1)} %get-tuple-element.249), kind=kLoop, calls=%fused_computation.36.clone.1 | loop fusion | flops 8342016 | bytes 4567040 | tf_op jit(solution)/shard_map/while/body/eval_jaxpr/reduce_sum | solution.py:33
  73.9 1.6 %scatter_fusion.1 = f32[36,3,128]{2,1,0:T(4,128)S(1)} fusion(f32[36,3,128]{2,1,0:T(4,128)S(1)} %get-tuple-element.281, s32[32]{0:T(128)S(1)} %fusion.58, f32[32,3,128]{2,1,0:T(4,128)S(1)} %bitcast.113), kind=kCustom, calls=%fused_computation.5.clone.1 | custom fusion | flops 12288 | bytes 147584 | tf_op jit(solution)/shard_map/while/body/eval_jaxpr/scatter-add | solution.py:53
  77.5 1.0 fusion.62
  78.5 1.8 %fusion.63 = (f32[2,3,128]{2,1,0:T(4,128)S(1)}, f32[2,17,3,128]{3,2,1,0:T(4,128)S(1)}) fusion(f32[2,17,128,128]{3,2,1,0:T(8,128)S(1)} %get-tuple-element.248, f32[2,3,128]{2,1,0:T(4,128)S(1)} %bitcast.120, f32[2,17,3,128]{3,2,1,0:T(4,128)S(1)} %copy.75, f32[2,17,128,128]{3,2,1,0:T(8,128)S(1)} %get-tuple-element.249), kind=kLoop, calls=%fused_computation.36.clone.1 | loop fusion | flops 8342016 | bytes 4567040 | tf_op jit(solution)/shard_map/while/body/eval_jaxpr/reduce_sum | solution.py:33
  80.4 1.6 %scatter_fusion.1 = f32[36,3,128]{2,1,0:T(4,128)S(1)} fusion(f32[36,3,128]{2,1,0:T(4,128)S(1)} %get-tuple-element.281, s32[32]{0:T(128)S(1)} %fusion.58, f32[32,3,128]{2,1,0:T(4,128)S(1)} %bitcast.113), kind=kCustom, calls=%fused_computation.5.clone.1 | custom fusion | flops 12288 | bytes 147584 | tf_op jit(solution)/shard_map/while/body/eval_jaxpr/scatter-add | solution.py:53
  85.0 1.8 %fusion.63 = (f32[2,3,128]{2,1,0:T(4,128)S(1)}, f32[2,17,3,128]{3,2,1,0:T(4,128)S(1)}) fusion(f32[2,17,128,128]{3,2,1,0:T(8,128)S(1)} %get-tuple-element.248, f32[2,3,128]{2,1,0:T(4,128)S(1)} %bitcast.120, f32[2,17,3,128]{3,2,1,0:T(4,128)S(1)} %copy.75, f32[2,17,128,128]{3,2,1,0:T(8,128)S(1)} %get-tuple-element.249), kind=kLoop, calls=%fused_computation.36.clone.1 | loop fusion | flops 8342016 | bytes 4567040 | tf_op jit(solution)/shard_map/while/body/eval_jaxpr/reduce_sum | solution.py:33
  86.9 1.6 %scatter_fusion.1 = f32[36,3,128]{2,1,0:T(4,128)S(1)} fusion(f32[36,3,128]{2,1,0:T(4,128)S(1)} %get-tuple-element.281, s32[32]{0:T(128)S(1)} %fusion.58, f32[32,3,128]{2,1,0:T(4,128)S(1)} %bitcast.113), kind=kCustom, calls=%fused_computation.5.clone.1 | custom fusion | flops 12288 | bytes 147584 | tf_op jit(solution)/shard_map/while/body/eval_jaxpr/scatter-add | solution.py:53
  90.5 1.0 fusion.62
  91.5 1.8 %fusion.63 = (f32[2,3,128]{2,1,0:T(4,128)S(1)}, f32[2,17,3,128]{3,2,1,0:T(4,128)S(1)}) fusion(f32[2,17,128,128]{3,2,1,0:T(8,128)S(1)} %get-tuple-element.248, f32[2,3,128]{2,1,0:T(4,128)S(1)} %bitcast.120, f32[2,17,3,128]{3,2,1,0:T(4,128)S(1)} %copy.75, f32[2,17,128,128]{3,2,1,0:T(8,128)S(1)} %get-tuple-element.249), kind=kLoop, calls=%fused_computation.36.clone.1 | loop fusion | flops 8342016 | bytes 4567040 | tf_op jit(solution)/shard_map/while/body/eval_jaxpr/reduce_sum | solution.py:33
  93.4 1.6 %scatter_fusion.1 = f32[36,3,128]{2,1,0:T(4,128)S(1)} fusion(f32[36,3,128]{2,1,0:T(4,128)S(1)} %get-tuple-element.281, s32[32]{0:T(128)S(1)} %fusion.58, f32[32,3,128]{2,1,0:T(4,128)S(1)} %bitcast.113), kind=kCustom, calls=%fused_computation.5.clone.1 | custom fusion | flops 12288 | bytes 147584 | tf_op jit(solution)/shard_map/while/body/eval_jaxpr/scatter-add | solution.py:53
  98.0 1.8 %fusion.63 = (f32[2,3,128]{2,1,0:T(4,128)S(1)}, f32[2,17,3,128]{3,2,1,0:T(4,128)S(1)}) fusion(f32[2,17,128,128]{3,2,1,0:T(8,128)S(1)} %get-tuple-element.248, f32[2,3,128]{2,1,0:T(4,128)S(1)} %bitcast.120, f32[2,17,3,128]{3,2,1,0:T(4,128)S(1)} %copy.75, f32[2,17,128,128]{3,2,1,0:T(8,128)S(1)} %get-tuple-element.249), kind=kLoop, calls=%fused_computation.36.clone.1 | loop fusion | flops 8342016 | bytes 4567040 | tf_op jit(solution)/shard_map/while/body/eval_jaxpr/reduce_sum | solution.py:33
  99.9 1.6 %scatter_fusion.1 = f32[36,3,128]{2,1,0:T(4,128)S(1)} fusion(f32[36,3,128]{2,1,0:T(4,128)S(1)} %get-tuple-element.281, s32[32]{0:T(128)S(1)} %fusion.58, f32[32,3,128]{2,1,0:T(4,128)S(1)} %bitcast.113), kind=kCustom, calls=%fused_computation.5.clone.1 | custom fusion | flops 12288 | bytes 147584 | tf_op jit(solution)/shard_map/while/body/eval_jaxpr/scatter-add | solution.py:53
  104.5 1.8 %fusion.63 = (f32[2,3,128]{2,1,0:T(4,128)S(1)}, f32[2,17,3,128]{3,2,1,0:T(4,128)S(1)}) fusion(f32[2,17,128,128]{3,2,1,0:T(8,128)S(1)} %get-tuple-element.248, f32[2,3,128]{2,1,0:T(4,128)S(1)} %bitcast.120, f32[2,17,3,128]{3,2,1,0:T(4,128)S(1)} %copy.75, f32[2,17,128,128]{3,2,1,0:T(8,128)S(1)} %get-tuple-element.249), kind=kLoop, calls=%fused_computation.36.clone.1 | loop fusion | flops 8342016 | bytes 4567040 | tf_op jit(solution)/shard_map/while/body/eval_jaxpr/reduce_sum | solution.py:33
  106.4 1.6 %scatter_fusion.1 = f32[36,3,128]{2,1,0:T(4,128)S(1)} fusion(f32[36,3,128]{2,1,0:T(4,128)S(1)} %get-tuple-element.281, s32[32]{0:T(128)S(1)} %fusion.58, f32[32,3,128]{2,1,0:T(4,128)S(1)} %bitcast.113), kind=kCustom, calls=%fused_computation.5.clone.1 | custom fusion | flops 12288 | bytes 147584 | tf_op jit(solution)/shard_map/while/body/eval_jaxpr/scatter-add | solution.py:53
  108.1 1.8 %collective-permute-start.8 = (f32[12,3,128]{2,1,0:T(4,128)S(1)}, f32[12,3,128]{2,1,0:T(4,128)S(1)}, u32[]{:S(2)}, u32[]{:S(2)}) collective-permute-start(f32[12,3,128]{2,1,0:T(4,128)S(1)} %get-tuple-element.130), channel_id=1, source_target_pairs={{0,1},{1,2},{2,3},{3,4},{4,5},{5,6},{6,7},{7,8},{8,9},{9,10},{10,1... | collective-permute-start | bytes 55304 | tf_op jit(solution)/shard_map/ppermute | solution.py:18
  109.9 3.0 %collective-permute-start.9 = (f32[12,3,128]{2,1,0:T(4,128)S(1)}, f32[12,3,128]{2,1,0:T(4,128)S(1)}, u32[]{:S(2)}, u32[]{:S(2)}) collective-permute-start(f32[12,3,128]{2,1,0:T(4,128)S(1)} %get-tuple-element.131), channel_id=1, source_target_pairs={{0,2},{1,3},{2,4},{3,5},{4,6},{5,7},{6,8},{7,9},{8,10},{9,11},{10,... | collective-permute-start | bytes 55304 | tf_op jit(solution)/shard_map/ppermute | solution.py:18
  113.5 2.7 %collective-permute-done.9 = f32[12,3,128]{2,1,0:T(4,128)S(1)} collective-permute-done((f32[12,3,128]{2,1,0:T(4,128)S(1)}, f32[12,3,128]{2,1,0:T(4,128)S(1)}, u32[]{:S(2)}, u32[]{:S(2)}) %collective-permute-start.9) | collective-permute-done | bytes 18464 | tf_op jit(solution)/shard_map/ppermute | solution.py:18
  116.2 1.9 %collective-permute-start.10 = (f32[6,6,128]{2,1,0:T(8,128)S(1)}, f32[6,6,128]{2,1,0:T(8,128)S(1)}, u32[]{:S(2)}, u32[]{:S(2)}) collective-permute-start(f32[6,6,128]{2,1,0:T(8,128)S(1)} %get-tuple-element.134), channel_id=1, source_target_pairs={{0,1},{1,2},{2,3},{3,4},{4,5},{5,6},{6,7},{7,8},{8,9},{9,10},{10,1... | collective-permute-start | bytes 55304 | tf_op jit(solution)/shard_map/ppermute | solution.py:24
  118.2 2.4 %collective-permute-start.11 = (f32[6,6,128]{2,1,0:T(8,128)S(1)}, f32[6,6,128]{2,1,0:T(8,128)S(1)}, u32[]{:S(2)}, u32[]{:S(2)}) collective-permute-start(f32[6,6,128]{2,1,0:T(8,128)S(1)} %get-tuple-element.135), channel_id=1, source_target_pairs={{1,0},{2,1},{3,2},{4,3},{5,4},{6,5},{7,6},{8,7},{9,8},{10,9},{11,1... | collective-permute-start | bytes 55304 | tf_op jit(solution)/shard_map/ppermute | solution.py:24
  121.3 2.0 %collective-permute-done.11 = f32[6,6,128]{2,1,0:T(8,128)S(1)} collective-permute-done((f32[6,6,128]{2,1,0:T(8,128)S(1)}, f32[6,6,128]{2,1,0:T(8,128)S(1)}, u32[]{:S(2)}, u32[]{:S(2)}) %collective-permute-start.11) | collective-permute-done | bytes 18464 | tf_op jit(solution)/shard_map/ppermute | solution.py:24
  (286 shorter events, 36.8 us)
Async XLA Ops:
  2.2 13.7 %collective-permute-start = (f32[12,4,128]{2,1,0:T(4,128)S(1)}, f32[12,4,128]{2,1,0:T(4,128)S(1)}, u32[]{:S(2)}, u32[]{:S(2)}) collective-permute-start(f32[12,4,128]{2,1,0:T(4,128)S(1)} %pad_maximum_fusion.9), channel_id=1, source_target_pairs={{0,31},{1,0},{2,1},{3,2},{4,3},{5,4},{6,5},{7,6},{8,7},{9,8},{10,9... | collective-permute-start | bytes 73736 | tf_op jit(solution)/shard_map/ppermute | solution.py:18
  2.3 13.6 %collective-permute-start.1 = (f32[12,4,128]{2,1,0:T(4,128)S(1)}, f32[12,4,128]{2,1,0:T(4,128)S(1)}, u32[]{:S(2)}, u32[]{:S(2)}) collective-permute-start(f32[12,4,128]{2,1,0:T(4,128)S(1)} %pad_maximum_fusion.9), channel_id=1, source_target_pairs={{0,30},{1,31},{2,0},{3,1},{4,2},{5,3},{6,4},{7,5},{8,6},{9,7},{10,... | collective-permute-start | bytes 73736 | tf_op jit(solution)/shard_map/ppermute | solution.py:18
  16.0 46.7 %copy-start = (f32[12,6,128]{2,1,0:T(8,128)S(1)}, f32[12,6,128]{2,1,0:T(8,128)}, u32[]{:S(2)}) copy-start(f32[12,6,128]{2,1,0:T(8,128)} %param.13) | copy-start | bytes 110596
  55.0 2.7 %collective-permute-start.2 = (f32[12,3,128]{2,1,0:T(4,128)S(1)}, f32[12,3,128]{2,1,0:T(4,128)S(1)}, u32[]{:S(2)}, u32[]{:S(2)}) collective-permute-start(f32[12,3,128]{2,1,0:T(4,128)S(1)} %get-tuple-element.132), channel_id=1, source_target_pairs={{0,1},{1,2},{2,3},{3,4},{4,5},{5,6},{6,7},{7,8},{8,9},{9,10},{10,1... | collective-permute-start | bytes 55304 | tf_op jit(solution)/shard_map/ppermute | solution.py:18
  56.4 6.3 %collective-permute-start.3 = (f32[12,3,128]{2,1,0:T(4,128)S(1)}, f32[12,3,128]{2,1,0:T(4,128)S(1)}, u32[]{:S(2)}, u32[]{:S(2)}) collective-permute-start(f32[12,3,128]{2,1,0:T(4,128)S(1)} %get-tuple-element.133), channel_id=1, source_target_pairs={{0,2},{1,3},{2,4},{3,5},{4,6},{5,7},{6,8},{7,9},{8,10},{9,11},{10,... | collective-permute-start | bytes 55304 | tf_op jit(solution)/shard_map/ppermute | solution.py:18
  62.8 6.3 %collective-permute-start.6 = (f32[12,4,128]{2,1,0:T(4,128)S(1)}, f32[12,4,128]{2,1,0:T(4,128)S(1)}, u32[]{:S(2)}, u32[]{:S(2)}) collective-permute-start(f32[12,4,128]{2,1,0:T(4,128)S(1)} %pad_maximum_fusion.8), channel_id=1, source_target_pairs={{0,31},{1,0},{2,1},{3,2},{4,3},{5,4},{6,5},{7,6},{8,7},{9,8},{10,9... | collective-permute-start | bytes 73736 | tf_op jit(solution)/shard_map/ppermute | solution.py:18
  63.1 5.9 %collective-permute-start.7 = (f32[12,4,128]{2,1,0:T(4,128)S(1)}, f32[12,4,128]{2,1,0:T(4,128)S(1)}, u32[]{:S(2)}, u32[]{:S(2)}) collective-permute-start(f32[12,4,128]{2,1,0:T(4,128)S(1)} %pad_maximum_fusion.8), channel_id=1, source_target_pairs={{0,30},{1,31},{2,0},{3,1},{4,2},{5,3},{6,4},{7,5},{8,6},{9,7},{10,... | collective-permute-start | bytes 73736 | tf_op jit(solution)/shard_map/ppermute | solution.py:18
  63.2 49.6 %collective-permute-start.4 = (f32[6,6,128]{2,1,0:T(8,128)S(1)}, f32[6,6,128]{2,1,0:T(8,128)S(1)}, u32[]{:S(2)}, u32[]{:S(2)}) collective-permute-start(f32[6,6,128]{2,1,0:T(8,128)S(1)} %get-tuple-element.136), channel_id=1, source_target_pairs={{0,1},{1,2},{2,3},{3,4},{4,5},{5,6},{6,7},{7,8},{8,9},{9,10},{10,1... | collective-permute-start | bytes 55304 | tf_op jit(solution)/shard_map/ppermute | solution.py:24
  67.1 45.8 %collective-permute-start.5 = (f32[6,6,128]{2,1,0:T(8,128)S(1)}, f32[6,6,128]{2,1,0:T(8,128)S(1)}, u32[]{:S(2)}, u32[]{:S(2)}) collective-permute-start(f32[6,6,128]{2,1,0:T(8,128)S(1)} %get-tuple-element.137), channel_id=1, source_target_pairs={{1,0},{2,1},{3,2},{4,3},{5,4},{6,5},{7,6},{8,7},{9,8},{10,9},{11,1... | collective-permute-start | bytes 55304 | tf_op jit(solution)/shard_map/ppermute | solution.py:24
  108.1 5.4 %collective-permute-start.8 = (f32[12,3,128]{2,1,0:T(4,128)S(1)}, f32[12,3,128]{2,1,0:T(4,128)S(1)}, u32[]{:S(2)}, u32[]{:S(2)}) collective-permute-start(f32[12,3,128]{2,1,0:T(4,128)S(1)} %get-tuple-element.130), channel_id=1, source_target_pairs={{0,1},{1,2},{2,3},{3,4},{4,5},{5,6},{6,7},{7,8},{8,9},{9,10},{10,1... | collective-permute-start | bytes 55304 | tf_op jit(solution)/shard_map/ppermute | solution.py:18
  109.9 6.3 %collective-permute-start.9 = (f32[12,3,128]{2,1,0:T(4,128)S(1)}, f32[12,3,128]{2,1,0:T(4,128)S(1)}, u32[]{:S(2)}, u32[]{:S(2)}) collective-permute-start(f32[12,3,128]{2,1,0:T(4,128)S(1)} %get-tuple-element.131), channel_id=1, source_target_pairs={{0,2},{1,3},{2,4},{3,5},{4,6},{5,7},{6,8},{7,9},{8,10},{9,11},{10,... | collective-permute-start | bytes 55304 | tf_op jit(solution)/shard_map/ppermute | solution.py:18
  116.2 5.1 %collective-permute-start.10 = (f32[6,6,128]{2,1,0:T(8,128)S(1)}, f32[6,6,128]{2,1,0:T(8,128)S(1)}, u32[]{:S(2)}, u32[]{:S(2)}) collective-permute-start(f32[6,6,128]{2,1,0:T(8,128)S(1)} %get-tuple-element.134), channel_id=1, source_target_pairs={{0,1},{1,2},{2,3},{3,4},{4,5},{5,6},{6,7},{7,8},{8,9},{9,10},{10,1... | collective-permute-start | bytes 55304 | tf_op jit(solution)/shard_map/ppermute | solution.py:24
  118.2 5.1 %collective-permute-start.11 = (f32[6,6,128]{2,1,0:T(8,128)S(1)}, f32[6,6,128]{2,1,0:T(8,128)S(1)}, u32[]{:S(2)}, u32[]{:S(2)}) collective-permute-start(f32[6,6,128]{2,1,0:T(8,128)S(1)} %get-tuple-element.135), channel_id=1, source_target_pairs={{1,0},{2,1},{3,2},{4,3},{5,4},{6,5},{7,6},{8,7},{9,8},{10,9},{11,1... | collective-permute-start | bytes 55304 | tf_op jit(solution)/shard_map/ppermute | solution.py:24
where the time goes:
time: 125 us
  other arithmetic  71.8 us (57%)
  starting transfers between devices  23.5 us (19%)
  local copies, waits for them, and re-layouts  17.1 us (14%)
  waiting for transfers between devices  9.71 us (8%)
  loops' own time  1.59 us (1%)
    reduce_sum x12, other arithmetic, pair_terms(): jnp.sum(kernel[:, :, None] * sources[:, :, 3][:, :, None, None, :] * sepa...  21.9 us
    scatter-add x12, other arithmetic, block_pass(): react_pool.at[source_ids.reshape(-1)]  19.6 us
    ppermute x8, starting transfers between devices, shifted(): return lax.ppermute(value, axis, pairs)  13.3 us
    mul x12, other arithmetic, pair_terms(): kernel[:, :, None] * targets[:, 3][:, None, None, :, None] * separation  11.8 us
    ppermute x4, starting transfers between devices, shifted_2(): lax.ppermute(value, axis, [(source, source + steps) for source in range(f...  10.1 us
    reduce_sum x12, other arithmetic, pair_terms(): distance_sq = jnp.sum(separation * separation, axis=2) + soften  9.68 us
    ppermute x8, waiting for transfers between devices, shifted(): return lax.ppermute(value, axis, pairs)  7.74 us
    gather x12, local copies, waits for them, and re-layouts, block_pass(): jnp.take(tile_pool, source_ids, axis=0)  7.28 us
  transfers between devices with their start and end apart: 12, of which 3 were waited for; matrix products, arithmetic and copies ran while one was open for 38% of the time, Pallas kernels for 0%

commit v1 on v0

v1 whole, which is shorter than its diff:
```python
import functools

import jax
import jax.numpy as jnp
from jax import lax
from jax.experimental import pallas as pl
from jax.experimental.pallas import tpu as pltpu
from jax.sharding import PartitionSpec as P

AXES = ("gx", "gy")
STEPS = 2

soften = 0.05
time_step = 0.5
reach = 2
chunk = 4
feature_rows = 32
moment_rows = 16
lanes = 128


def shifted(value, steps):
    count = lax.axis_size(AXES)
    pairs = [(source, (source + steps) % count) for source in range(count)]
    return lax.ppermute(value, AXES, pairs)


def shifted_open(value, steps):
    count = lax.axis_size(AXES)
    first, last = (max(0, -steps), min(count, count - steps))
    return lax.ppermute(value, AXES, [(source, source + steps) for source in range(first, last)])


def round_up(value, step):
    return -(-value // step) * step


def device_index():
    return lax.axis_index("gx") * lax.axis_size("gy") + lax.axis_index("gy")


def pieces(value, count):
    parts = []
    rest = value
    for _ in range(count - 1):
        part = rest.astype(jnp.bfloat16).astype(jnp.float32)
        parts.append(part)
        rest = rest - part
    parts.append(rest.astype(jnp.bfloat16).astype(jnp.float32))
    return parts


def pack_kernel(total_tiles, particles_ref, occupancy_ref, neighbours_ref, packed_ref):
    tiles, slots = packed_ref.shape[1:]
    listed = neighbours_ref.shape[1]
    for row in range(3):
        packed_ref[row] = particles_ref[:, row, :]
    tile_ids = lax.broadcasted_iota(jnp.int32, (tiles, listed), 0)
    offsets = neighbours_ref[...] - (device_index() * tiles + tile_ids)
    offsets = jnp.where(offsets < 0, offsets + total_tiles, offsets)
    packed_ref[3] = jnp.zeros((tiles, slots), jnp.float32)
    packed_ref[3, :, :listed] = offsets.astype(jnp.float32)
    for tile in range(tiles):
        live = occupancy_ref[tile].astype(jnp.float32)
        packed_ref[3, tile : tile + 1, listed : listed + 1] = jnp.full((1, 1), live)


def build_lists(aux, window, tiles, listed, rows):
    center = reach * tiles
    place = lax.broadcasted_iota(jnp.int32, (rows, lanes), 0).astype(jnp.float32)
    lane = lax.broadcasted_iota(jnp.int32, (rows, lanes), 1).astype(jnp.float32)
    mask = place == lane + center
    for entry in range(listed):
        mask = mask | (place + aux[:, entry : entry + 1] == lane + center)
    own_rows = round_up(tiles, 8)
    own = aux[center : center + own_rows]
    own_place = lax.broadcasted_iota(jnp.int32, (own_rows, lanes), 0).astype(jnp.float32) + center
    own_lane = lax.broadcasted_iota(jnp.int32, (own_rows, lanes), 1).astype(jnp.float32)
    listing = own_place + own[:, 0:1] == own_lane
    for entry in range(1, listed):
        listing = listing | (own_place + own[:, entry : entry + 1] == own_lane)
    listing = jnp.where(listing, 1.0, 0.0)
    listing = jnp.concatenate([listing, jnp.zeros((lanes - own_rows, lanes), jnp.float32)], axis=0)
    listing = jnp.transpose(listing)[:rows]
    mask = jnp.where(lane < tiles, jnp.maximum(jnp.where(mask, 1.0, 0.0), listing), 0.0)
    earlier = lax.broadcasted_iota(jnp.int32, (rows, rows), 1) < lax.broadcasted_iota(jnp.int32, (rows, rows), 0)
    rank = jnp.dot(
        jnp.where(earlier, 1.0, 0.0).astype(jnp.bfloat16),
        mask.astype(jnp.bfloat16),
        preferred_element_type=jnp.float32,
    )
    key = jnp.where(mask > 0.5, rank, -1.0)
    counts = jnp.sum(mask, axis=0, keepdims=True)
    lists = []
    for tile in range(tiles):
        hit = key[:, tile : tile + 1] == lane
        lists.append(jnp.sum(jnp.where(hit, place - window, 0.0), axis=0, keepdims=True) + window)
    lists.append(jnp.full((1, lanes), float(window)))
    lists.append(counts)
    return [row.astype(jnp.int32) for row in lists]


def build_features(place_of, weight, tiles, rows, refs):
    feature_ref, moment_ref, source_ref, target_ref, moments_ref = refs
    center = reach * tiles
    middle = [jnp.mean(axis[center : center + 8], keepdims=True) for axis in place_of]
    centred = [axis - mid for axis, mid in zip(place_of, middle)]
    norm = centred[0] * centred[0] + centred[1] * centred[1] + centred[2] * centred[2]
    ones = jnp.ones_like(norm)
    source_rows = []
    target_rows = []
    moments = []
    for axis in centred:
        near, mid, far = pieces(axis, 3)
        near_2, mid_2, far_2 = (-2.0 * near, -2.0 * mid, -2.0 * far)
        source_rows += [near, near, mid, mid, near, far]
        target_rows += [near_2, mid_2, near_2, mid_2, far_2, near_2]
        moments += [weight * near, weight * mid, weight * far]
    source_rows += pieces(norm, 3) + [ones] * 3
    target_rows += [ones] * 3 + pieces(norm + soften, 3)
    moments.append(weight)
    zeros = jnp.zeros_like(norm)
    source_rows += [zeros] * (feature_rows - len(source_rows))
    moments += [zeros] * (moment_rows - len(moments))
    for row, value in enumerate(source_rows):
        feature_ref[:, row, :] = value
    for row, value in enumerate(moments):
        moment_ref[:, row, :] = value
    per_group = lanes // feature_rows
    for group in range(rows // per_group):
        block = feature_ref[group * per_group : (group + 1) * per_group].reshape(lanes, lanes)
        source_ref[group] = jnp.transpose(block).astype(jnp.bfloat16)
    for tile in range(rows):
        moment = moment_ref[tile].astype(jnp.bfloat16)
        moments_ref[tile] = jnp.concatenate([moment, moment], axis=1)
    target_rows += [zeros] * (feature_rows - len(target_rows))
    own_rows = round_up(tiles, 8)
    for row, value in enumerate(target_rows):
        feature_ref[:own_rows, row, :] = value[center : center + own_rows]
    blank = jnp.zeros((feature_rows, lanes), jnp.bfloat16)
    for tile in range(tiles + 1):
        target = feature_ref[tile].astype(jnp.bfloat16)
        for variant in range(per_group):
            for part in range(per_group):
                target_ref[tile, variant, part * feature_rows : (part + 1) * feature_rows, :] = (
                    target if part == variant else blank
                )
    return centred


def accumulate(tiles, lists_ref, source_ref, target_ref, moments_ref, distance_ref, kernel_ref, total_ref):
    per_group = lanes // feature_rows
    total_ref[...] = jnp.zeros(total_ref.shape, jnp.float32)
    chunk_counts = [(lists_ref[tiles + 1, tile] + chunk - 1) // chunk for tile in range(tiles)]
    chunk_total = functools.reduce(lambda left, right: left + right, chunk_counts)

    def step(_, carry):
        tile, part, tile_1, part_1, tile_2, part_2 = carry
        moment = jnp.concatenate(
            [moments_ref[lists_ref[tile_2, part_2 * chunk + entry]] for entry in range(chunk)], axis=1
        )
        total_ref[tile_2] += jnp.dot(moment, kernel_ref[...], preferred_element_type=jnp.float32)
        for entry in range(chunk):
            inverse = lax.rsqrt(distance_ref[entry])
            kernel = inverse * inverse * inverse
            high = kernel.astype(jnp.bfloat16)
            low = (kernel - high.astype(jnp.float32)).astype(jnp.bfloat16)
            kernel_ref[entry * 2 * lanes : entry * 2 * lanes + lanes, :] = high
            kernel_ref[entry * 2 * lanes + lanes : (entry + 1) * 2 * lanes, :] = low
        for entry in range(chunk):
            source = lists_ref[tile, part * chunk + entry]
            distance_ref[entry] = jnp.dot(
                source_ref[source // per_group],
                target_ref[tile, source % per_group],
                preferred_element_type=jnp.float32,
            )
        filled = lists_ref[tiles + 1, tile]
        more = (part + 1) * chunk < filled
        next_tile = jnp.where(more, tile, jnp.minimum(tile + 1, tiles))
        next_part = jnp.where(more, part + 1, 0)
        return (next_tile, next_part, tile, part, tile_1, part_1)

    zero = jnp.int32(0)
    spare = jnp.int32(tiles)
    lax.fori_loop(0, chunk_total + 2, step, (zero, zero, spare, zero, spare, zero))


def advance(tiles, centred, place_own, speed_own, weight_own, total_ref, state_ref):
    center = reach * tiles
    zeroth = total_ref[:tiles, 9, :]
    for axis in range(3):
        first = total_ref[:tiles, 3 * axis, :] + total_ref[:tiles, 3 * axis + 1, :] + total_ref[:tiles, 3 * axis + 2, :]
        force = first - centred[axis][center : center + tiles] * zeroth
        speed = weight_own * (speed_own[axis] + time_step * force / lanes)
        state_ref[axis] = weight_own * (place_own[axis] + time_step * speed)
        state_ref[3 + axis] = speed


def first_kernel(
    listed, before_2, before_1, own_ref, after_1, after_2, particles_ref, state_ref, weight_ref, lists_ref, *scratch
):
    planes, scalars, copy_sem, feature_ref, moment_ref, source_ref, target_ref, moments_ref, *loop_refs = scratch
    tiles, slots = own_ref.shape[1:]
    rows = planes.shape[1]
    window = (2 * reach + 1) * tiles
    planes[:, window:, :] = jnp.zeros((4, rows - window, slots), jnp.float32)
    for block, ref in enumerate((before_2, before_1, own_ref, after_1, after_2)):
        planes[:, block * tiles : (block + 1) * tiles, :] = ref[...]
    aux = planes[3]
    for row, value in enumerate(build_lists(aux, window, tiles, listed, rows)):
        lists_ref[row : row + 1, :] = value
    copy = pltpu.make_async_copy(lists_ref, scalars, copy_sem)
    copy.start()
    slot = lax.broadcasted_iota(jnp.int32, (rows, slots), 1).astype(jnp.float32)
    weight = jnp.where(slot < aux[:, listed : listed + 1], 1.0, 0.0)
    weight_ref[...] = weight
    refs = (feature_ref, moment_ref, source_ref, target_ref, moments_ref)
    centred = build_features([planes[axis] for axis in range(3)], weight, tiles, rows, refs)
    copy.wait()
    accumulate(tiles, scalars, source_ref, target_ref, moments_ref, *loop_refs)
    center = reach * tiles
    advance(
        tiles,
        centred,
        [own_ref[axis] for axis in range(3)],
        [particles_ref[:, 3 + axis, :] for axis in range(3)],
        weight[center : center + tiles],
        loop_refs[-1],
        state_ref,
    )


def place_rows(step, total_tiles, cuts_ref, lower, own, upper, pool_ref, out_ref):
    tiles = own[0].shape[0]
    half = tiles // 2
    capacity = out_ref.shape[0]
    device = device_index()
    last = cuts_ref.shape[1] - 1
    first_tile = cuts_ref[step, device]
    next_tile = jnp.where(device == last, total_tiles, cuts_ref[step, jnp.minimum(device + 1, last)])
    owned = next_tile - first_tile
    start = first_tile - (device * tiles - half)
    for row in range(6):
        pool_ref[:half, row, :] = lower[row]
        pool_ref[half : half + tiles, row, :] = own[row]
        pool_ref[half + tiles : 2 * tiles, row, :] = upper[row]
    for slot in range(capacity):
        source = jnp.minimum(start + slot, 2 * tiles - 1)
        out_ref[slot] = jnp.where(slot < owned, pool_ref[source], 0.0)


def second_kernel(
    total_tiles, lists_ref, cuts_ref, before_2, before_1, own_ref, after_1, after_2, weight_ref, state_ref, out_ref, *scratch
):
    planes, pool_ref, feature_ref, moment_ref, source_ref, target_ref, moments_ref, *loop_refs = scratch
    tiles, slots = own_ref.shape[1:]
    half = tiles // 2
    rows = planes.shape[1]
    window = (2 * reach + 1) * tiles
    planes[:, window:, :] = jnp.zeros((3, rows - window, slots), jnp.float32)
    for block, ref in enumerate((before_2, before_1, own_ref, after_1, after_2)):
        planes[:, block * tiles : (block + 1) * tiles, :] = ref[:3]
    weight = weight_ref[...]
    refs = (feature_ref, moment_ref, source_ref, target_ref, moments_ref)
    centred = build_features([planes[axis] for axis in range(3)], weight, tiles, rows, refs)
    accumulate(tiles, lists_ref, source_ref, target_ref, moments_ref, *loop_refs)
    center = reach * tiles
    advance(
        tiles,
        centred,
        [own_ref[axis] for axis in range(3)],
        [own_ref[3 + axis] for axis in range(3)],
        weight[center : center + tiles],
        loop_refs[-1],
        state_ref,
    )
    place_rows(
        0,
        total_tiles,
        cuts_ref,
        [before_1[row, tiles - half :, :] for row in range(6)],
        [own_ref[row] for row in range(6)],
        [after_1[row, :half, :] for row in range(6)],
        pool_ref,
        out_ref,
    )


def third_kernel(total_tiles, cuts_ref, lower_ref, own_ref, upper_ref, out_ref, pool_ref):
    place_rows(
        1,
        total_tiles,
        cuts_ref,
        [lower_ref[row] for row in range(6)],
        [own_ref[row] for row in range(6)],
        [upper_ref[row] for row in range(6)],
        pool_ref,
        out_ref,
    )


def body(particles, occupancy, neighbours, curve_cuts):
    tiles, _, slots = particles.shape
    listed = neighbours.shape[1]
    total_tiles = tiles * lax.axis_size(AXES)
    half = tiles // 2
    rows = round_up((2 * reach + 1) * tiles + 1, 8)
    vmem = pl.BlockSpec(memory_space=pltpu.VMEM)
    smem = pl.BlockSpec(memory_space=pltpu.SMEM)

    def shape(*sizes, dtype=jnp.float32):
        return jax.ShapeDtypeStruct(sizes, dtype)

    packed = pl.pallas_call(
        functools.partial(pack_kernel, total_tiles),
        out_shape=shape(4, tiles, slots),
        in_specs=[vmem, smem, vmem],
        out_specs=vmem,
        name="pack",
    )(particles, occupancy, neighbours)
    feature_scratch = [
        pltpu.VMEM((rows, feature_rows, lanes), jnp.float32),
        pltpu.VMEM((rows, moment_rows, lanes), jnp.float32),
        pltpu.VMEM((rows * feature_rows // lanes, lanes, lanes), jnp.bfloat16),
        pltpu.VMEM((tiles + 1, lanes // feature_rows, lanes, lanes), jnp.bfloat16),
        pltpu.VMEM((rows, moment_rows, 2 * lanes), jnp.bfloat16),
        pltpu.VMEM((chunk, lanes, lanes), jnp.float32),
        pltpu.VMEM((chunk * 2 * lanes, lanes), jnp.bfloat16),
        pltpu.VMEM((round_up(tiles + 1, 8), moment_rows, lanes), jnp.float32),
    ]
    pool_scratch = pltpu.VMEM((2 * tiles, 6, slots), jnp.float32)
    list_rows = round_up(tiles + 2, 8)
    state, weight, lists = pl.pallas_call(
        functools.partial(first_kernel, listed),
        out_shape=(shape(6, tiles, slots), shape(rows, slots), shape(list_rows, lanes, dtype=jnp.int32)),
        in_specs=[vmem] * 6,
        out_specs=(vmem, vmem, vmem),
        scratch_shapes=[
            pltpu.VMEM((4, rows, slots), jnp.float32),
            pltpu.SMEM((list_rows, lanes), jnp.int32),
            pltpu.SemaphoreType.DMA,
        ]
        + feature_scratch,
        name="first_step",
    )(shifted(packed, 2), shifted(packed, 1), packed, shifted(packed, -1), shifted(packed, -2), particles)
    state_2, after_first = pl.pallas_call(
        functools.partial(second_kernel, total_tiles),
        out_shape=(shape(6, tiles, slots), shape(2 * tiles, 6, slots)),
        in_specs=[smem, smem] + [vmem] * 6,
        out_specs=(vmem, vmem),
        scratch_shapes=[pltpu.VMEM((3, rows, slots), jnp.float32), pool_scratch] + feature_scratch,
        name="second_step",
    )(
        lists,
        curve_cuts,
        shifted(state, 2),
        shifted(state, 1),
        state,
        shifted(state, -1),
        shifted(state, -2),
        weight,
    )
    lower = shifted_open(state_2[:, tiles - half :, :], 1)
    upper = shifted_open(state_2[:, :half, :], -1)
    after_second = pl.pallas_call(
        functools.partial(third_kernel, total_tiles),
        out_shape=shape(2 * tiles, 6, slots),
        in_specs=[smem, vmem, vmem, vmem],
        out_specs=vmem,
        scratch_shapes=[pool_scratch],
        name="place",
    )(curve_cuts, lower, state_2, upper)
    return (after_first, after_second)


def solution(mesh):
    in_specs = (P(AXES, None, None), P(AXES), P(AXES, None), P())
    out_specs = (P(AXES, None, None), P(AXES, None, None))
    return jax.shard_map(body, mesh=mesh, in_specs=in_specs, out_specs=out_specs, check_vma=False)
```

time: 125 us -> 91.1 us (0.73)
  other arithmetic: 71.8 us -> 0 us
  Pallas kernels: 0 us -> 54.2 us
  local copies, waits for them, and re-layouts: 17.1 us -> 5.25 us
  starting transfers between devices: 23.5 us -> 17.5 us
  waiting for transfers between devices: 9.71 us -> 12.8 us
  loops' own time: 1.59 us -> 0 us
    pallas_call x0 -> x4, Pallas kernels: none -> 54.2 us  [the longest x1 26.2 us: body(): pl.pallas_call(functools.partial(first_kernel, listed), out_shape=(shape(...]
    reduce_sum x24 -> x0, other arithmetic: 31.5 us -> none  [the longest x12 21.9 us: pair_terms(): jnp.sum(kernel[:, :, None] * sources[:, :, 3][:, :, None, None, :] * sepa...]
    scatter-add x12 -> x0, other arithmetic: 19.6 us -> none  [block_pass(): react_pool.at[source_ids.reshape(-1)]]
    mul x28 -> x0, other arithmetic: 12.2 us -> none  [the longest x12 11.8 us: pair_terms(): kernel[:, :, None] * targets[:, 3][:, None, None, :, None] * separation]
    gather x14 -> x0, local copies, waits for them, and re-layouts: 8.44 us -> none  [the longest x12 7.28 us: block_pass(): jnp.take(tile_pool, source_ids, axis=0)]
    ppermute x12 -> x10, starting transfers between devices: 23.5 us -> 17.5 us  [the longest x8 11.9 us: shifted(): return lax.ppermute(value, AXES, pairs)]
    convert_element_type x5 -> x0, other arithmetic: 4.01 us -> none  [the longest x2 2.47 us: place_home(): filled = (wanted < next_new).astype(jnp.float32)]
    unnamed x4 -> x24, local copies, waits for them, and re-layouts: 1.3 us -> 4.37 us
  transfers between devices with their start and end apart: 12 -> 10, of which waited for: 3 -> 5; matrix products, arithmetic and copies ran while one was open for 38% -> 1% of each run, Pallas kernels for 0% -> 0%
where the time goes in v1:
time: 91.1 us; the launch traced here: 90.4 us
  Pallas kernels  54.2 us (59%)
  starting transfers between devices  17.5 us (19%)
  waiting for transfers between devices  12.8 us (14%)
  local copies, waits for them, and re-layouts  5.25 us (6%)
    pallas_call x1, Pallas kernels, body(): pl.pallas_call(functools.partial(first_kernel, listed), out_shape=(shape(...  26.2 us
    pallas_call x1, Pallas kernels, body(): pl.pallas_call(functools.partial(second_kernel, total_tiles), out_shape=(...  25 us
    ppermute x8, waiting for transfers between devices, shifted(): return lax.ppermute(value, AXES, pairs)  12.5 us
    ppermute x8, starting transfers between devices, shifted(): return lax.ppermute(value, AXES, pairs)  11.9 us
    ppermute x2, starting transfers between devices, shifted_open(): lax.ppermute(value, AXES, [(source, source + steps) for source in range(f...  5.55 us
    unnamed x24, local copies, waits for them, and re-layouts  4.37 us
  transfers between devices with their start and end apart: 10, of which 5 were waited for; matrix products, arithmetic and copies ran while one was open for 1% of the time, Pallas kernels for 0%

profile of v1, /device:TPU:1, one launch (start us, length us, event | category | flops | bytes accessed | tf_op | source)
XLA Modules:
  0.0 90.4 jit_solution(2311442704744493551)
XLA Ops:
  0.6 1.4 %pack.1.own_ref = f32[4,12,128]{2,1,0:T(8,128)} custom-call(f32[12,6,128]{2,1,0:T(8,128)} %particles_ref.3, s32[12]{0:T(128)} %occupancy_ref.1, s32[12,16]{1,0:T(8,128)} %neighbours_ref.1), custom_call_target="tpu_custom_call" | custom-call | tf_op jit(solution)/shard_map/pack/pallas_call | solution.py:314
  2.1 6.0 %collective-permute-start.3 = (f32[4,12,128]{2,1,0:T(8,128)}, f32[4,12,128]{2,1,0:T(8,128)S(1)}, u32[]{:S(2)}, u32[]{:S(2)}) collective-permute-start(f32[4,12,128]{2,1,0:T(8,128)} %pack.1.own_ref), channel_id=1, source_target_pairs={{0,30},{1,31},{2,0},{3,1},{4,2},{5,3},{6,4},{7,5},{8,6},{9,7},{10,... | collective-permute-start | bytes 73736 | tf_op jit(solution)/shard_map/ppermute | solution.py:25
  8.1 1.0 %collective-permute-start.2 = (f32[4,12,128]{2,1,0:T(8,128)}, f32[4,12,128]{2,1,0:T(8,128)S(1)}, u32[]{:S(2)}, u32[]{:S(2)}) collective-permute-start(f32[4,12,128]{2,1,0:T(8,128)} %pack.1.own_ref), channel_id=1, source_target_pairs={{0,31},{1,0},{2,1},{3,2},{4,3},{5,4},{6,5},{7,6},{8,7},{9,8},{10,9... | collective-permute-start | bytes 73736 | tf_op jit(solution)/shard_map/ppermute | solution.py:25
  9.1 0.8 collective-permute-start.1
  9.9 0.0 collective-permute-start
  9.9 0.0 collective-permute-done.3.after_2
  9.9 0.0 copy-start.5
  9.9 1.8 %collective-permute-done.2.after_1 = f32[4,12,128]{2,1,0:T(8,128)S(1)} collective-permute-done((f32[4,12,128]{2,1,0:T(8,128)}, f32[4,12,128]{2,1,0:T(8,128)S(1)}, u32[]{:S(2)}, u32[]{:S(2)}) %collective-permute-start.2) | collective-permute-done | bytes 24608 | tf_op jit(solution)/shard_map/ppermute | solution.py:25
  11.7 0.0 copy-start.6
  11.7 0.0 collective-permute-done.1.before_1
  11.7 0.0 copy-start.7
  11.7 5.2 %collective-permute-done.before_2 = f32[4,12,128]{2,1,0:T(8,128)S(1)} collective-permute-done((f32[4,12,128]{2,1,0:T(8,128)}, f32[4,12,128]{2,1,0:T(8,128)S(1)}, u32[]{:S(2)}, u32[]{:S(2)}) %collective-permute-start) | collective-permute-done | bytes 24608 | tf_op jit(solution)/shard_map/ppermute | solution.py:25
  16.9 0.0 copy-done.5
  16.9 0.0 copy-done.6
  16.9 0.0 copy-done.7
  16.9 0.0 copy-start.8
  16.9 0.6 copy-done.8
  17.5 26.2 %first_step.1 = (f32[6,12,128]{2,1,0:T(8,128)}, f32[64,128]{1,0:T(8,128)}, s32[16,128]{1,0:T(8,128)}) custom-call(f32[4,12,128]{2,1,0:T(8,128)} %copy-done.8, f32[4,12,128]{2,1,0:T(8,128)} %copy-done.7, f32[4,12,128]{2,1,0:T(8,128)} %pack.1.own_ref, f32[4,12,128]{2,1,0:T(8,128)} %copy-done.6, f32[4,12,128]{2,1,0:T(8,128)} %copy-done.5, ...), custom_call_target="tpu_custom_call" | custom-call | tf_op jit(solution)/shard_map/first_step/pallas_call | solution.py:333
  43.7 0.8 collective-permute-start.7
  44.5 0.5 collective-permute-start.6
  45.0 1.6 %collective-permute-start.5 = (f32[6,12,128]{2,1,0:T(8,128)}, f32[6,12,128]{2,1,0:T(8,128)S(1)}, u32[]{:S(2)}, u32[]{:S(2)}) collective-permute-start(f32[6,12,128]{2,1,0:T(8,128)} %get-tuple-element.8.own_ref), channel_id=1, source_target_pairs={{0,1},{1,2},{2,3},{3,4},{4,5},{5,6},{6,7},{7,8},{8,9},{9,10},{10,1... | collective-permute-start | bytes 110600 | tf_op jit(solution)/shard_map/ppermute | solution.py:25
  46.6 1.3 %collective-permute-start.4 = (f32[6,12,128]{2,1,0:T(8,128)}, f32[6,12,128]{2,1,0:T(8,128)S(1)}, u32[]{:S(2)}, u32[]{:S(2)}) collective-permute-start(f32[6,12,128]{2,1,0:T(8,128)} %get-tuple-element.8.own_ref), channel_id=1, source_target_pairs={{0,2},{1,3},{2,4},{3,5},{4,6},{5,7},{6,8},{7,9},{8,10},{9,11},{10,... | collective-permute-start | bytes 110600 | tf_op jit(solution)/shard_map/ppermute | solution.py:25
  47.9 0.0 collective-permute-done.7.after_2
  47.9 0.0 copy-start.1
  47.9 1.3 %collective-permute-done.6.after_1 = f32[6,12,128]{2,1,0:T(8,128)S(1)} collective-permute-done((f32[6,12,128]{2,1,0:T(8,128)}, f32[6,12,128]{2,1,0:T(8,128)S(1)}, u32[]{:S(2)}, u32[]{:S(2)}) %collective-permute-start.6) | collective-permute-done | bytes 36896 | tf_op jit(solution)/shard_map/ppermute | solution.py:25
  49.2 0.0 copy-start.2
  49.2 0.0 collective-permute-done.5.before_1
  49.2 0.0 copy-start.3
  49.2 4.2 %collective-permute-done.4.before_2 = f32[6,12,128]{2,1,0:T(8,128)S(1)} collective-permute-done((f32[6,12,128]{2,1,0:T(8,128)}, f32[6,12,128]{2,1,0:T(8,128)S(1)}, u32[]{:S(2)}, u32[]{:S(2)}) %collective-permute-start.4) | collective-permute-done | bytes 36896 | tf_op jit(solution)/shard_map/ppermute | solution.py:25
  53.4 0.0 copy-start.4
  53.4 0.0 copy-done.1
  53.4 0.0 copy-done.2
  53.4 0.0 copy-done.3
  53.4 0.6 copy-done.4
  54.0 25.0 %second_step.1 = (f32[6,12,128]{2,1,0:T(8,128)}, f32[24,6,128]{2,1,0:T(8,128)}) custom-call(s32[16,128]{1,0:T(8,128)} %get-tuple-element.7.lists_ref, s32[2,32]{1,0:T(2,128)} %cuts_ref.3, f32[6,12,128]{2,1,0:T(8,128)} %copy-done.4, f32[6,12,128]{2,1,0:T(8,128)} %copy-done.3, f32[6,12,128]{2,1,0:T(8,128)} %get-tuple-element.8.own_ref, ...), custom_call_target="tpu_custom_call" | custom-call | tf_op jit(solution)/shard_map/second_step/pallas_call | solution.py:346
  79.0 0.0 copy-start
  79.0 0.9 fusion
  79.9 2.6 %collective-permute-start.9 = (f32[6,6,128]{2,1,0:T(8,128)S(1)}, f32[6,6,128]{2,1,0:T(8,128)S(1)}, u32[]{:S(2)}, u32[]{:S(2)}) collective-permute-start(f32[6,6,128]{2,1,0:T(8,128)S(1)} %get-tuple-element.14), channel_id=1, source_target_pairs={{1,0},{2,1},{3,2},{4,3},{5,4},{6,5},{7,6},{8,7},{9,8},{10,9},{11,1... | collective-permute-start | bytes 55304 | tf_op jit(solution)/shard_map/ppermute | solution.py:31
  82.5 2.9 %collective-permute-start.8 = (f32[6,6,128]{2,1,0:T(8,128)S(1)}, f32[6,6,128]{2,1,0:T(8,128)S(1)}, u32[]{:S(2)}, u32[]{:S(2)}) collective-permute-start(f32[6,6,128]{2,1,0:T(8,128)S(1)} %get-tuple-element.15), channel_id=1, source_target_pairs={{0,1},{1,2},{2,3},{3,4},{4,5},{5,6},{6,7},{7,8},{8,9},{9,10},{10,1... | collective-permute-start | bytes 55304 | tf_op jit(solution)/shard_map/ppermute | solution.py:31
  85.4 0.0 copy-done
  85.5 0.6 copy.6
  86.1 0.0 collective-permute-done.9.upper_ref
  86.1 0.0 copy-start.9
  86.1 0.3 collective-permute-done.8.lower_ref
  86.4 0.3 copy-done.9
  86.7 0.6 copy-done.10
  87.3 1.6 %place.1 = f32[24,6,128]{2,1,0:T(8,128)} custom-call(s32[2,32]{1,0:T(2,128)} %cuts_ref.3, f32[6,6,128]{2,1,0:T(8,128)} %copy-done.10, f32[6,12,128]{2,1,0:T(8,128)} %get-tuple-element.11.own_ref, f32[6,6,128]{2,1,0:T(8,128)} %copy-done.9), custom_call_target="tpu_custom_call" | custom-call | tf_op jit(solution)/shard_map/place/pallas_call | solution.py:365
  88.9 1.5 %copy.7 = f32[24,6,128]{2,0,1:T(8,128)} copy(f32[24,6,128]{2,1,0:T(8,128)} %place.1) | data formatting | bytes 147456
  (1 shorter events, 0.0 us)
Async XLA Ops:
  2.1 7.8 %collective-permute-start.3 = (f32[4,12,128]{2,1,0:T(8,128)}, f32[4,12,128]{2,1,0:T(8,128)S(1)}, u32[]{:S(2)}, u32[]{:S(2)}) collective-permute-start(f32[4,12,128]{2,1,0:T(8,128)} %pack.1.own_ref), channel_id=1, source_target_pairs={{0,30},{1,31},{2,0},{3,1},{4,2},{5,3},{6,4},{7,5},{8,6},{9,7},{10,... | collective-permute-start | bytes 73736 | tf_op jit(solution)/shard_map/ppermute | solution.py:25
  8.1 3.6 %collective-permute-start.2 = (f32[4,12,128]{2,1,0:T(8,128)}, f32[4,12,128]{2,1,0:T(8,128)S(1)}, u32[]{:S(2)}, u32[]{:S(2)}) collective-permute-start(f32[4,12,128]{2,1,0:T(8,128)} %pack.1.own_ref), channel_id=1, source_target_pairs={{0,31},{1,0},{2,1},{3,2},{4,3},{5,4},{6,5},{7,6},{8,7},{9,8},{10,9... | collective-permute-start | bytes 73736 | tf_op jit(solution)/shard_map/ppermute | solution.py:25
  9.1 2.6 %collective-permute-start.1 = (f32[4,12,128]{2,1,0:T(8,128)}, f32[4,12,128]{2,1,0:T(8,128)S(1)}, u32[]{:S(2)}, u32[]{:S(2)}) collective-permute-start(f32[4,12,128]{2,1,0:T(8,128)} %pack.1.own_ref), channel_id=1, source_target_pairs={{0,1},{1,2},{2,3},{3,4},{4,5},{5,6},{6,7},{7,8},{8,9},{9,10},{10,1... | collective-permute-start | bytes 73736 | tf_op jit(solution)/shard_map/ppermute | solution.py:25
  9.9 7.0 %collective-permute-start = (f32[4,12,128]{2,1,0:T(8,128)}, f32[4,12,128]{2,1,0:T(8,128)S(1)}, u32[]{:S(2)}, u32[]{:S(2)}) collective-permute-start(f32[4,12,128]{2,1,0:T(8,128)} %pack.1.own_ref), channel_id=1, source_target_pairs={{0,2},{1,3},{2,4},{3,5},{4,6},{5,7},{6,8},{7,9},{8,10},{9,11},{10,... | collective-permute-start | bytes 73736 | tf_op jit(solution)/shard_map/ppermute | solution.py:25
  9.9 7.0 %copy-start.5 = (f32[4,12,128]{2,1,0:T(8,128)}, f32[4,12,128]{2,1,0:T(8,128)S(1)}, u32[]{:S(2)}) copy-start(f32[4,12,128]{2,1,0:T(8,128)S(1)} %collective-permute-done.3.after_2) | copy-start | bytes 73732
  11.7 5.2 %copy-start.6 = (f32[4,12,128]{2,1,0:T(8,128)}, f32[4,12,128]{2,1,0:T(8,128)S(1)}, u32[]{:S(2)}) copy-start(f32[4,12,128]{2,1,0:T(8,128)S(1)} %collective-permute-done.2.after_1) | copy-start | bytes 73732
  11.7 5.2 %copy-start.7 = (f32[4,12,128]{2,1,0:T(8,128)}, f32[4,12,128]{2,1,0:T(8,128)S(1)}, u32[]{:S(2)}) copy-start(f32[4,12,128]{2,1,0:T(8,128)S(1)} %collective-permute-done.1.before_1) | copy-start | bytes 73732
  16.9 0.6 copy-start.8
  43.7 4.2 %collective-permute-start.7 = (f32[6,12,128]{2,1,0:T(8,128)}, f32[6,12,128]{2,1,0:T(8,128)S(1)}, u32[]{:S(2)}, u32[]{:S(2)}) collective-permute-start(f32[6,12,128]{2,1,0:T(8,128)} %get-tuple-element.8.own_ref), channel_id=1, source_target_pairs={{0,30},{1,31},{2,0},{3,1},{4,2},{5,3},{6,4},{7,5},{8,6},{9,7},{10,... | collective-permute-start | bytes 110600 | tf_op jit(solution)/shard_map/ppermute | solution.py:25
  44.5 4.7 %collective-permute-start.6 = (f32[6,12,128]{2,1,0:T(8,128)}, f32[6,12,128]{2,1,0:T(8,128)S(1)}, u32[]{:S(2)}, u32[]{:S(2)}) collective-permute-start(f32[6,12,128]{2,1,0:T(8,128)} %get-tuple-element.8.own_ref), channel_id=1, source_target_pairs={{0,31},{1,0},{2,1},{3,2},{4,3},{5,4},{6,5},{7,6},{8,7},{9,8},{10,9... | collective-permute-start | bytes 110600 | tf_op jit(solution)/shard_map/ppermute | solution.py:25
  45.0 4.1 %collective-permute-start.5 = (f32[6,12,128]{2,1,0:T(8,128)}, f32[6,12,128]{2,1,0:T(8,128)S(1)}, u32[]{:S(2)}, u32[]{:S(2)}) collective-permute-start(f32[6,12,128]{2,1,0:T(8,128)} %get-tuple-element.8.own_ref), channel_id=1, source_target_pairs={{0,1},{1,2},{2,3},{3,4},{4,5},{5,6},{6,7},{7,8},{8,9},{9,10},{10,1... | collective-permute-start | bytes 110600 | tf_op jit(solution)/shard_map/ppermute | solution.py:25
  46.6 6.7 %collective-permute-start.4 = (f32[6,12,128]{2,1,0:T(8,128)}, f32[6,12,128]{2,1,0:T(8,128)S(1)}, u32[]{:S(2)}, u32[]{:S(2)}) collective-permute-start(f32[6,12,128]{2,1,0:T(8,128)} %get-tuple-element.8.own_ref), channel_id=1, source_target_pairs={{0,2},{1,3},{2,4},{3,5},{4,6},{5,7},{6,8},{7,9},{8,10},{9,11},{10,... | collective-permute-start | bytes 110600 | tf_op jit(solution)/shard_map/ppermute | solution.py:25
  47.9 5.5 %copy-start.1 = (f32[6,12,128]{2,1,0:T(8,128)}, f32[6,12,128]{2,1,0:T(8,128)S(1)}, u32[]{:S(2)}) copy-start(f32[6,12,128]{2,1,0:T(8,128)S(1)} %collective-permute-done.7.after_2) | copy-start | bytes 110596
  49.2 4.2 %copy-start.2 = (f32[6,12,128]{2,1,0:T(8,128)}, f32[6,12,128]{2,1,0:T(8,128)S(1)}, u32[]{:S(2)}) copy-start(f32[6,12,128]{2,1,0:T(8,128)S(1)} %collective-permute-done.6.after_1) | copy-start | bytes 110596
  49.2 4.2 %copy-start.3 = (f32[6,12,128]{2,1,0:T(8,128)}, f32[6,12,128]{2,1,0:T(8,128)S(1)}, u32[]{:S(2)}) copy-start(f32[6,12,128]{2,1,0:T(8,128)S(1)} %collective-permute-done.5.before_1) | copy-start | bytes 110596
  53.4 0.6 copy-start.4
  79.0 6.5 %copy-start = (f32[24,6,128]{2,1,0:T(8,128)S(1)}, f32[24,6,128]{2,1,0:T(8,128)}, u32[]{:S(2)}) copy-start(f32[24,6,128]{2,1,0:T(8,128)} %get-tuple-element.12) | copy-start | bytes 221188
  79.9 6.2 %collective-permute-start.9 = (f32[6,6,128]{2,1,0:T(8,128)S(1)}, f32[6,6,128]{2,1,0:T(8,128)S(1)}, u32[]{:S(2)}, u32[]{:S(2)}) collective-permute-start(f32[6,6,128]{2,1,0:T(8,128)S(1)} %get-tuple-element.14), channel_id=1, source_target_pairs={{1,0},{2,1},{3,2},{4,3},{5,4},{6,5},{7,6},{8,7},{9,8},{10,9},{11,1... | collective-permute-start | bytes 55304 | tf_op jit(solution)/shard_map/ppermute | solution.py:31
  82.5 3.9 %collective-permute-start.8 = (f32[6,6,128]{2,1,0:T(8,128)S(1)}, f32[6,6,128]{2,1,0:T(8,128)S(1)}, u32[]{:S(2)}, u32[]{:S(2)}) collective-permute-start(f32[6,6,128]{2,1,0:T(8,128)S(1)} %get-tuple-element.15), channel_id=1, source_target_pairs={{0,1},{1,2},{2,3},{3,4},{4,5},{5,6},{6,7},{7,8},{8,9},{9,10},{10,1... | collective-permute-start | bytes 55304 | tf_op jit(solution)/shard_map/ppermute | solution.py:31
  86.1 0.6 copy-start.9
  86.7 0.6 copy-start.10

commit v2 on v1

v2 whole, which is shorter than its diff:
```python
import functools

import jax
import jax.numpy as jnp
from jax import lax
from jax.experimental import pallas as pl
from jax.experimental.pallas import tpu as pltpu
from jax.sharding import PartitionSpec as P

AXES = ("gx", "gy")
STEPS = 2

soften = 0.05
time_step = 0.5
reach = 2
chunk = 4
feature_rows = 32
far_norm = 1e36
lanes = 128


def shifted(value, steps):
    count = lax.axis_size(AXES)
    pairs = [(source, (source + steps) % count) for source in range(count)]
    return lax.ppermute(value, AXES, pairs)


def shifted_open(value, steps):
    count = lax.axis_size(AXES)
    first, last = (max(0, -steps), min(count, count - steps))
    return lax.ppermute(value, AXES, [(source, source + steps) for source in range(first, last)])


def round_up(value, step):
    return -(-value // step) * step


def device_index():
    return lax.axis_index("gx") * lax.axis_size("gy") + lax.axis_index("gy")


def pieces(value, count):
    parts = []
    rest = value
    for _ in range(count - 1):
        part = rest.astype(jnp.bfloat16).astype(jnp.float32)
        parts.append(part)
        rest = rest - part
    parts.append(rest.astype(jnp.bfloat16).astype(jnp.float32))
    return parts


def pack_kernel(total_tiles, particles_ref, occupancy_ref, neighbours_ref, packed_ref, speed_ref):
    tiles, slots = packed_ref.shape[1:]
    listed = neighbours_ref.shape[1]
    for row in range(3):
        packed_ref[row] = particles_ref[:, row, :]
        speed_ref[row] = particles_ref[:, 3 + row, :]
    tile_ids = lax.broadcasted_iota(jnp.int32, (tiles, listed), 0)
    offsets = neighbours_ref[...] - (device_index() * tiles + tile_ids)
    offsets = jnp.where(offsets < 0, offsets + total_tiles, offsets)
    packed_ref[3] = jnp.zeros((tiles, slots), jnp.float32)
    packed_ref[3, :, :listed] = offsets.astype(jnp.float32)
    for tile in range(tiles):
        live = occupancy_ref[tile].astype(jnp.float32)
        packed_ref[3, tile : tile + 1, listed : listed + 1] = jnp.full((1, 1), live)


def build_lists(aux, window, tiles, listed, rows):
    center = reach * tiles
    place = lax.broadcasted_iota(jnp.int32, (rows, lanes), 0).astype(jnp.float32)
    lane = lax.broadcasted_iota(jnp.int32, (rows, lanes), 1).astype(jnp.float32)
    mask = place == lane + center
    for entry in range(listed):
        mask = mask | (place + aux[:, entry : entry + 1] == lane + center)
    own_rows = round_up(tiles, 8)
    own = aux[center : center + own_rows]
    own_place = lax.broadcasted_iota(jnp.int32, (own_rows, lanes), 0).astype(jnp.float32) + center
    own_lane = lax.broadcasted_iota(jnp.int32, (own_rows, lanes), 1).astype(jnp.float32)
    listing = own_place + own[:, 0:1] == own_lane
    for entry in range(1, listed):
        listing = listing | (own_place + own[:, entry : entry + 1] == own_lane)
    listing = jnp.where(listing, 1.0, 0.0)
    listing = jnp.concatenate([listing, jnp.zeros((lanes - own_rows, lanes), jnp.float32)], axis=0)
    listing = jnp.transpose(listing)[:rows]
    mask = jnp.where(lane < tiles, jnp.maximum(jnp.where(mask, 1.0, 0.0), listing), 0.0)
    earlier = lax.broadcasted_iota(jnp.int32, (rows, rows), 1) < lax.broadcasted_iota(jnp.int32, (rows, rows), 0)
    rank = jnp.dot(
        jnp.where(earlier, 1.0, 0.0).astype(jnp.bfloat16),
        mask.astype(jnp.bfloat16),
        preferred_element_type=jnp.float32,
    )
    key = jnp.where(mask > 0.5, rank, -1.0)
    counts = jnp.sum(mask, axis=0, keepdims=True)
    lists = []
    for tile in range(tiles):
        hit = key[:, tile : tile + 1] == lane
        lists.append(jnp.sum(jnp.where(hit, place - window, 0.0), axis=0, keepdims=True) + window)
    lists.append(jnp.full((1, lanes), float(window)))
    lists.append(counts)
    return [row.astype(jnp.int32) for row in lists]


def build_features(place_of, weight, tiles, refs):
    feature_ref, moment_ref, source_ref, target_ref = refs
    rows = feature_ref.shape[0]
    center = reach * tiles
    middle = [jnp.mean(axis[center : center + 8], keepdims=True) for axis in place_of]
    centred = [axis - mid for axis, mid in zip(place_of, middle)]
    ones = jnp.ones_like(weight)
    zeros = jnp.zeros_like(weight)
    source_rows = []
    target_rows = []
    norm = zeros
    for axis, value in enumerate(centred):
        norm = norm + value * value
        live = weight * value
        moment_ref[:, axis, :] = live
        near, mid, far = pieces(live, 3)
        source_rows += [near, near, mid, mid, near, far]
        near, mid, far = [-2.0 * part for part in pieces(value, 3)]
        target_rows += [near, mid, near, mid, far, near]
    source_rows += pieces(jnp.where(weight > 0.5, norm, far_norm), 3) + [ones] * 3
    target_rows += [ones] * 3 + pieces(norm + soften, 3)
    source_rows += [zeros] * (feature_rows - len(source_rows))
    target_rows += [zeros] * (feature_rows - len(target_rows))
    for row, value in enumerate(source_rows):
        feature_ref[:, row, :] = value
    for tile in range(rows):
        source_ref[tile] = feature_ref[tile].astype(jnp.bfloat16)
    own_rows = round_up(tiles, 8)
    for row, value in enumerate(target_rows):
        feature_ref[:own_rows, row, :] = value[center : center + own_rows]
    blank = jnp.zeros((lanes - feature_rows, lanes), jnp.float32)
    for tile in range(tiles + 1):
        block = jnp.concatenate([feature_ref[tile], blank], axis=0)
        target_ref[tile] = jnp.transpose(block)[:, :feature_rows].astype(jnp.bfloat16)
    return centred


def accumulate(tiles, lists_ref, source_ref, target_ref, moment_ref, distance_ref, total_ref, sums_ref):
    total_ref[...] = jnp.zeros(total_ref.shape, jnp.float32)
    chunk_counts = [(lists_ref[tiles + 1, tile] + chunk - 1) // chunk for tile in range(tiles)]
    chunk_total = functools.reduce(lambda left, right: left + right, chunk_counts)

    def step(_, carry):
        tile, part, tile_1, part_1 = carry
        places = []
        for entry in range(chunk):
            source = lists_ref[tile_1, part_1 * chunk + entry]
            places.append([jnp.broadcast_to(moment_ref[source, axis : axis + 1, :], (8, lanes)) for axis in range(3)])
        for first in range(0, lanes, 8):
            strip = slice(first, first + 8)
            sums = [total_ref[tile_1, row, strip, :] for row in range(4)]
            for entry in range(chunk):
                column = (entry % 2) * lanes
                inverse = lax.rsqrt(distance_ref[entry // 2, strip, column : column + lanes])
                kernel = inverse * inverse * inverse
                for axis in range(3):
                    sums[axis] = sums[axis] + kernel * places[entry][axis]
                sums[3] = sums[3] + kernel
            for row in range(4):
                total_ref[tile_1, row, strip, :] = sums[row]
        for pair in range(chunk // 2):
            sources = [lists_ref[tile, part * chunk + 2 * pair + entry] for entry in range(2)]
            distance_ref[pair] = jnp.dot(
                target_ref[tile],
                jnp.concatenate([source_ref[source] for source in sources], axis=1),
                preferred_element_type=jnp.float32,
            )
        more = (part + 1) * chunk < lists_ref[tiles + 1, tile]
        next_tile = jnp.where(more, tile, jnp.minimum(tile + 1, tiles))
        next_part = jnp.where(more, part + 1, 0)
        return (next_tile, next_part, tile, part)

    zero = jnp.int32(0)
    spare = jnp.int32(tiles)
    lax.fori_loop(0, chunk_total + 1, step, (zero, zero, spare, zero))
    for tile in range(tiles):
        for row in range(4):
            sums_ref[row, tile : tile + 1, :] = jnp.sum(jnp.transpose(total_ref[tile, row]), axis=0, keepdims=True)


def advance(centred, place_own, speed_own, weight_own, sums_ref, state_ref):
    tiles = weight_own.shape[0]
    center = reach * tiles
    zeroth = sums_ref[3, :tiles, :]
    for axis in range(3):
        force = sums_ref[axis, :tiles, :] - centred[axis][center : center + tiles] * zeroth
        speed = weight_own * (speed_own[axis] + time_step * force / lanes)
        state_ref[axis] = weight_own * (place_own[axis] + time_step * speed)
        state_ref[3 + axis] = speed


def first_kernel(
    listed, before_2, before_1, own_ref, after_1, after_2, speed_ref, state_ref, weight_ref, lists_ref, *scratch
):
    planes, scalars, copy_sem, feature_ref, moment_ref, source_ref, target_ref, *loop_refs = scratch
    tiles, slots = own_ref.shape[1:]
    rows = planes.shape[1]
    window = (2 * reach + 1) * tiles
    planes[:, window:, :] = jnp.zeros((4, rows - window, slots), jnp.float32)
    for block, ref in enumerate((before_2, before_1, own_ref, after_1, after_2)):
        planes[:, block * tiles : (block + 1) * tiles, :] = ref[...]
    aux = planes[3]
    for row, value in enumerate(build_lists(aux, window, tiles, listed, rows)):
        lists_ref[row : row + 1, :] = value
    copy = pltpu.make_async_copy(lists_ref, scalars, copy_sem)
    copy.start()
    slot = lax.broadcasted_iota(jnp.int32, (rows, slots), 1).astype(jnp.float32)
    weight = jnp.where(slot < aux[:, listed : listed + 1], 1.0, 0.0)
    weight_ref[...] = weight
    refs = (feature_ref, moment_ref, source_ref, target_ref)
    centred = build_features([planes[axis] for axis in range(3)], weight, tiles, refs)
    copy.wait()
    accumulate(tiles, scalars, source_ref, target_ref, moment_ref, *loop_refs)
    center = reach * tiles
    advance(
        centred,
        [own_ref[axis] for axis in range(3)],
        [speed_ref[axis] for axis in range(3)],
        weight[center : center + tiles],
        loop_refs[-1],
        state_ref,
    )


def place_rows(step, total_tiles, cuts_ref, lower, own, upper, pool_ref, out_ref):
    tiles, slots = own[0].shape
    half = tiles // 2
    capacity = out_ref.shape[1]
    device = device_index()
    last = cuts_ref.shape[1] - 1
    first_tile = cuts_ref[step, device]
    next_tile = jnp.where(device == last, total_tiles, cuts_ref[step, jnp.minimum(device + 1, last)])
    owned = next_tile - first_tile
    start = first_tile - (device * tiles - half)
    filled = lax.broadcasted_iota(jnp.int32, (capacity, slots), 0) < owned
    for row in range(6):
        pool_ref[row, :half, :] = lower[row]
        pool_ref[row, half : half + tiles, :] = own[row]
        pool_ref[row, half + tiles : 2 * tiles, :] = upper[row]
    for row in range(6):
        out_ref[row] = jnp.where(filled, pool_ref[row, pl.ds(start, capacity), :], 0.0)


def second_kernel(
    total_tiles,
    cuts_ref,
    lists_ref,
    before_2,
    before_1,
    own_ref,
    after_1,
    after_2,
    weight_ref,
    state_ref,
    down_ref,
    up_ref,
    out_ref,
    *scratch
):
    planes, scalars, copy_sem, pool_ref, feature_ref, moment_ref, source_ref, target_ref, *loop_refs = scratch
    tiles, slots = own_ref.shape[1:]
    half = tiles // 2
    rows = planes.shape[1]
    window = (2 * reach + 1) * tiles
    copy = pltpu.make_async_copy(lists_ref, scalars, copy_sem)
    copy.start()
    planes[:, window:, :] = jnp.zeros((3, rows - window, slots), jnp.float32)
    for block, ref in enumerate((before_2, before_1, own_ref, after_1, after_2)):
        planes[:, block * tiles : (block + 1) * tiles, :] = ref[:3]
    weight = weight_ref[...]
    refs = (feature_ref, moment_ref, source_ref, target_ref)
    centred = build_features([planes[axis] for axis in range(3)], weight, tiles, refs)
    copy.wait()
    accumulate(tiles, scalars, source_ref, target_ref, moment_ref, *loop_refs)
    center = reach * tiles
    advance(
        centred,
        [own_ref[axis] for axis in range(3)],
        [own_ref[3 + axis] for axis in range(3)],
        weight[center : center + tiles],
        loop_refs[-1],
        state_ref,
    )
    down_ref[...] = state_ref[:, :half, :]
    up_ref[...] = state_ref[:, tiles - half :, :]
    place_rows(
        0,
        total_tiles,
        cuts_ref,
        [before_1[row, tiles - half :, :] for row in range(6)],
        [own_ref[row] for row in range(6)],
        [after_1[row, :half, :] for row in range(6)],
        pool_ref,
        out_ref,
    )


def third_kernel(total_tiles, cuts_ref, lower_ref, own_ref, upper_ref, out_ref, pool_ref):
    place_rows(
        1,
        total_tiles,
        cuts_ref,
        [lower_ref[row] for row in range(6)],
        [own_ref[row] for row in range(6)],
        [upper_ref[row] for row in range(6)],
        pool_ref,
        out_ref,
    )


def near(value):
    return pltpu.with_memory_space_constraint(value, pltpu.VMEM)


def body(particles, occupancy, neighbours, curve_cuts):
    tiles, _, slots = particles.shape
    listed = neighbours.shape[1]
    total_tiles = tiles * lax.axis_size(AXES)
    half = tiles // 2
    capacity = 2 * tiles
    rows = round_up((2 * reach + 1) * tiles + 1, 8)
    list_rows = round_up(tiles + 2, 8)
    vmem = pl.BlockSpec(memory_space=pltpu.VMEM)
    smem = pl.BlockSpec(memory_space=pltpu.SMEM)

    def held(*sizes, dtype=jnp.float32):
        return pltpu.VMEM(sizes, dtype)

    packed, speed = pl.pallas_call(
        functools.partial(pack_kernel, total_tiles),
        out_shape=(held(4, tiles, slots), held(3, tiles, slots)),
        in_specs=[vmem, smem, vmem],
        out_specs=(vmem, vmem),
        name="pack",
    )(particles, occupancy, neighbours)
    list_scratch = [pltpu.SMEM((list_rows, lanes), jnp.int32), pltpu.SemaphoreType.DMA]
    feature_scratch = [
        pltpu.VMEM((rows, feature_rows, lanes), jnp.float32),
        pltpu.VMEM((rows, 8, lanes), jnp.float32),
        pltpu.VMEM((rows, feature_rows, lanes), jnp.bfloat16),
        pltpu.VMEM((tiles + 1, lanes, feature_rows), jnp.bfloat16),
        pltpu.VMEM((chunk // 2, lanes, 2 * lanes), jnp.float32),
        pltpu.VMEM((tiles + 1, 4, lanes, lanes), jnp.float32),
        pltpu.VMEM((4, round_up(tiles, 8), lanes), jnp.float32),
    ]
    pool_scratch = pltpu.VMEM((6, round_up(capacity + tiles, 8), slots), jnp.float32)
    blocks = [near(value) for value in (shifted(packed, 2), shifted(packed, 1), packed, shifted(packed, -1), shifted(packed, -2))]
    state, weight, lists = pl.pallas_call(
        functools.partial(first_kernel, listed),
        out_shape=(held(6, tiles, slots), held(rows, slots), held(list_rows, lanes, dtype=jnp.int32)),
        in_specs=[vmem] * 6,
        out_specs=(vmem, vmem, vmem),
        scratch_shapes=[pltpu.VMEM((4, rows, slots), jnp.float32)] + list_scratch + feature_scratch,
        name="first_step",
    )(*blocks, near(speed))
    blocks = [near(value) for value in (shifted(state, 2), shifted(state, 1), state, shifted(state, -1), shifted(state, -2))]
    state_2, down, up, after_first = pl.pallas_call(
        functools.partial(second_kernel, total_tiles),
        out_shape=(
            held(6, tiles, slots),
            held(6, half, slots),
            held(6, half, slots),
            jax.ShapeDtypeStruct((6, capacity, slots), jnp.float32),
        ),
        in_specs=[smem] + [vmem] * 7,
        out_specs=(vmem, vmem, vmem, vmem),
        scratch_shapes=[pltpu.VMEM((3, rows, slots), jnp.float32)] + list_scratch + [pool_scratch] + feature_scratch,
        name="second_step",
    )(curve_cuts, near(lists), *blocks, near(weight))
    lower = shifted_open(up, 1)
    upper = shifted_open(down, -1)
    after_second = pl.pallas_call(
        functools.partial(third_kernel, total_tiles),
        out_shape=jax.ShapeDtypeStruct((6, capacity, slots), jnp.float32),
        in_specs=[smem, vmem, vmem, vmem],
        out_specs=vmem,
        scratch_shapes=[pool_scratch],
        name="place",
    )(curve_cuts, near(lower), near(state_2), near(upper))
    return (jnp.transpose(after_first, (1, 0, 2)), jnp.transpose(after_second, (1, 0, 2)))


def solution(mesh):
    in_specs = (P(AXES, None, None), P(AXES), P(AXES, None), P())
    out_specs = (P(AXES, None, None), P(AXES, None, None))
    return jax.shard_map(body, mesh=mesh, in_specs=in_specs, out_specs=out_specs, check_vma=False)
```

time: 91.1 us -> 77.4 us (0.85)
  Pallas kernels: 54.2 us -> 46.1 us
  local copies, waits for them, and re-layouts: 5.25 us -> 0 us
  starting transfers between devices: 17.5 us -> 16.3 us
  waiting for transfers between devices: 12.8 us -> 13.9 us
    pallas_call x3, Pallas kernels: 29.2 us -> 24.1 us  [the longest x1 21.9 us: body(): pl.pallas_call(functools.partial(first_kernel, listed), out_shape=(held(6...]
    unnamed x24 -> x0, local copies, waits for them, and re-layouts: 4.37 us -> none
    pallas_call x1, Pallas kernels: 25 us -> 22 us  [body(): pl.pallas_call(functools.partial(second_kernel, total_tiles), out_shape=(...]
    ppermute x2, waiting for transfers between devices: 0.26 us -> 2.73 us  [shifted_open(): lax.ppermute(value, AXES, [(source, source + steps) for source in range(f...]
    ppermute x8, waiting for transfers between devices: 12.5 us -> 11.2 us  [shifted(): return lax.ppermute(value, AXES, pairs)]
    ppermute x2, starting transfers between devices: 5.55 us -> 4.32 us  [shifted_open(): lax.ppermute(value, AXES, [(source, source + steps) for source in range(f...]
  transfers between devices with their start and end apart: 10 -> 10, of which waited for: 5 -> 4; matrix products, arithmetic and copies ran while one was open for 1% -> 0% of each run, Pallas kernels for 0% -> 0%
where the time goes in v2:
time: 77.4 us; the launch traced here: 77 us
  Pallas kernels  46.1 us (60%)
  starting transfers between devices  16.3 us (21%)
  waiting for transfers between devices  13.9 us (18%)
    pallas_call x1, Pallas kernels, body(): pl.pallas_call(functools.partial(second_kernel, total_tiles), out_shape=(...  22 us
    pallas_call x1, Pallas kernels, body(): pl.pallas_call(functools.partial(first_kernel, listed), out_shape=(held(6...  21.9 us
    ppermute x8, starting transfers between devices, shifted(): return lax.ppermute(value, AXES, pairs)  12 us
    ppermute x8, waiting for transfers between devices, shifted(): return lax.ppermute(value, AXES, pairs)  11.2 us
    ppermute x2, starting transfers between devices, shifted_open(): lax.ppermute(value, AXES, [(source, source + steps) for source in range(f...  4.32 us
    ppermute x2, waiting for transfers between devices, shifted_open(): lax.ppermute(value, AXES, [(source, source + steps) for source in range(f...  2.73 us
  transfers between devices with their start and end apart: 10, of which 4 were waited for; matrix products, arithmetic and copies ran while one was open for 0% of the time, Pallas kernels for 0%

profile of v2, /device:TPU:1, one launch (start us, length us, event | category | flops | bytes accessed | tf_op | source)
XLA Modules:
  0.0 77.0 jit_solution(11813295660422699909)
XLA Ops:
  0.6 0.8 %pack.1 = (f32[4,12,128]{2,1,0:T(8,128)S(1)}, f32[3,12,128]{2,1,0:T(8,128)S(1)}) custom-call(f32[12,6,128]{2,1,0:T(8,128)} %particles_ref.1, s32[12]{0:T(128)} %occupancy_ref.1, s32[12,16]{1,0:T(8,128)} %neighbours_ref.1), custom_call_target="tpu_custom_call" | custom-call | tf_op jit(solution)/shard_map/pack/pallas_call | solution.py:332
  1.5 6.1 %collective-permute-start.3 = (f32[4,12,128]{2,1,0:T(8,128)S(1)}, f32[4,12,128]{2,1,0:T(8,128)S(1)}, u32[]{:S(2)}, u32[]{:S(2)}) collective-permute-start(f32[4,12,128]{2,1,0:T(8,128)S(1)} %get-tuple-element.11.own_ref), channel_id=1, source_target_pairs={{0,30},{1,31},{2,0},{3,1},{4,2},{5,3},{6,4},{7,5},{8,6},{9,7},{10,... | collective-permute-start | bytes 73736 | tf_op jit(solution)/shard_map/ppermute | solution.py:25
  7.6 1.0 %collective-permute-start.2 = (f32[4,12,128]{2,1,0:T(8,128)S(1)}, f32[4,12,128]{2,1,0:T(8,128)S(1)}, u32[]{:S(2)}, u32[]{:S(2)}) collective-permute-start(f32[4,12,128]{2,1,0:T(8,128)S(1)} %get-tuple-element.11.own_ref), channel_id=1, source_target_pairs={{0,31},{1,0},{2,1},{3,2},{4,3},{5,4},{6,5},{7,6},{8,7},{9,8},{10,9... | collective-permute-start | bytes 73736 | tf_op jit(solution)/shard_map/ppermute | solution.py:25
  8.5 0.8 %collective-permute-start.1 = (f32[4,12,128]{2,1,0:T(8,128)S(1)}, f32[4,12,128]{2,1,0:T(8,128)S(1)}, u32[]{:S(2)}, u32[]{:S(2)}) collective-permute-start(f32[4,12,128]{2,1,0:T(8,128)S(1)} %get-tuple-element.11.own_ref), channel_id=1, source_target_pairs={{0,1},{1,2},{2,3},{3,4},{4,5},{5,6},{6,7},{7,8},{8,9},{9,10},{10,1... | collective-permute-start | bytes 73736 | tf_op jit(solution)/shard_map/ppermute | solution.py:25
  9.3 0.0 collective-permute-start
  9.3 0.0 collective-permute-done.3.after_2
  9.3 1.6 %collective-permute-done.2.after_1 = f32[4,12,128]{2,1,0:T(8,128)S(1)} collective-permute-done((f32[4,12,128]{2,1,0:T(8,128)S(1)}, f32[4,12,128]{2,1,0:T(8,128)S(1)}, u32[]{:S(2)}, u32[]{:S(2)}) %collective-permute-start.2) | collective-permute-done | bytes 24608 | tf_op jit(solution)/shard_map/ppermute | solution.py:25
  10.9 0.0 collective-permute-done.1.before_1
  10.9 5.2 %collective-permute-done.before_2 = f32[4,12,128]{2,1,0:T(8,128)S(1)} collective-permute-done((f32[4,12,128]{2,1,0:T(8,128)S(1)}, f32[4,12,128]{2,1,0:T(8,128)S(1)}, u32[]{:S(2)}, u32[]{:S(2)}) %collective-permute-start) | collective-permute-done | bytes 24608 | tf_op jit(solution)/shard_map/ppermute | solution.py:25
  16.1 21.9 %first_step.1 = (f32[6,12,128]{2,1,0:T(8,128)S(1)}, f32[64,128]{1,0:T(8,128)S(1)}, s32[16,128]{1,0:T(8,128)S(1)}) custom-call(f32[4,12,128]{2,1,0:T(8,128)S(1)} %collective-permute-done.before_2, f32[4,12,128]{2,1,0:T(8,128)S(1)} %collective-permute-done.1.before_1, f32[4,12,128]{2,1,0:T(8,128)S(1)} %get-tuple-element.11.own_ref, ...), custom_call_target="tpu_custom_call" | custom-call | tf_op jit(solution)/shard_map/first_step/pallas_call | solution.py:351
  38.1 0.1 collective-permute-start.7
  38.1 0.3 collective-permute-start.6
  38.4 1.6 %collective-permute-start.5 = (f32[6,12,128]{2,1,0:T(8,128)S(1)}, f32[6,12,128]{2,1,0:T(8,128)S(1)}, u32[]{:S(2)}, u32[]{:S(2)}) collective-permute-start(f32[6,12,128]{2,1,0:T(8,128)S(1)} %get-tuple-element.14.own_ref), channel_id=1, source_target_pairs={{0,1},{1,2},{2,3},{3,4},{4,5},{5,6},{6,7},{7,8},{8,9},{9,10},{10,1... | collective-permute-start | bytes 110600 | tf_op jit(solution)/shard_map/ppermute | solution.py:25
  40.0 2.2 %collective-permute-start.4 = (f32[6,12,128]{2,1,0:T(8,128)S(1)}, f32[6,12,128]{2,1,0:T(8,128)S(1)}, u32[]{:S(2)}, u32[]{:S(2)}) collective-permute-start(f32[6,12,128]{2,1,0:T(8,128)S(1)} %get-tuple-element.14.own_ref), channel_id=1, source_target_pairs={{0,2},{1,3},{2,4},{3,5},{4,6},{5,7},{6,8},{7,9},{8,10},{9,11},{10,... | collective-permute-start | bytes 110600 | tf_op jit(solution)/shard_map/ppermute | solution.py:25
  42.2 0.0 collective-permute-done.7.after_2
  42.2 0.0 collective-permute-done.6.after_1
  42.3 0.0 collective-permute-done.5.before_1
  42.3 4.3 %collective-permute-done.4.before_2 = f32[6,12,128]{2,1,0:T(8,128)S(1)} collective-permute-done((f32[6,12,128]{2,1,0:T(8,128)S(1)}, f32[6,12,128]{2,1,0:T(8,128)S(1)}, u32[]{:S(2)}, u32[]{:S(2)}) %collective-permute-start.4) | collective-permute-done | bytes 36896 | tf_op jit(solution)/shard_map/ppermute | solution.py:25
  46.6 22.0 %second_step.1 = (f32[6,12,128]{2,1,0:T(8,128)S(1)}, f32[6,6,128]{2,1,0:T(8,128)S(1)}, f32[6,6,128]{2,1,0:T(8,128)S(1)}, f32[6,24,128]{2,1,0:T(8,128)}) custom-call(s32[2,32]{1,0:T(2,128)} %cuts_ref.3, s32[16,128]{1,0:T(8,128)S(1)} %get-tuple-element.13.lists_ref, f32[6,12,128]{2,1,0:T(8,128)S(1)} %collective-permute-done.4.before_2, ...), custom_call_target="tpu_custom_call" | custom-call | tf_op jit(solution)/shard_map/second_step/pallas_call | solution.py:360
  68.6 1.9 %collective-permute-start.8 = (f32[6,6,128]{2,1,0:T(8,128)S(1)}, f32[6,6,128]{2,1,0:T(8,128)S(1)}, u32[]{:S(2)}, u32[]{:S(2)}) collective-permute-start(f32[6,6,128]{2,1,0:T(8,128)S(1)} %get-tuple-element.17), channel_id=1, source_target_pairs={{0,1},{1,2},{2,3},{3,4},{4,5},{5,6},{6,7},{7,8},{8,9},{9,10},{10,1... | collective-permute-start | bytes 55304 | tf_op jit(solution)/shard_map/ppermute | solution.py:31
  70.5 2.4 %collective-permute-start.9 = (f32[6,6,128]{2,1,0:T(8,128)S(1)}, f32[6,6,128]{2,1,0:T(8,128)S(1)}, u32[]{:S(2)}, u32[]{:S(2)}) collective-permute-start(f32[6,6,128]{2,1,0:T(8,128)S(1)} %get-tuple-element.19), channel_id=1, source_target_pairs={{1,0},{2,1},{3,2},{4,3},{5,4},{6,5},{7,6},{8,7},{9,8},{10,9},{11,1... | collective-permute-start | bytes 55304 | tf_op jit(solution)/shard_map/ppermute | solution.py:31
  72.9 0.0 collective-permute-done.8.lower_ref
  73.0 2.7 %collective-permute-done.9.upper_ref = f32[6,6,128]{2,1,0:T(8,128)S(1)} collective-permute-done((f32[6,6,128]{2,1,0:T(8,128)S(1)}, f32[6,6,128]{2,1,0:T(8,128)S(1)}, u32[]{:S(2)}, u32[]{:S(2)}) %collective-permute-start.9) | collective-permute-done | bytes 18464 | tf_op jit(solution)/shard_map/ppermute | solution.py:31
  75.7 1.3 %place.1 = f32[6,24,128]{2,1,0:T(8,128)} custom-call(s32[2,32]{1,0:T(2,128)} %cuts_ref.3, f32[6,6,128]{2,1,0:T(8,128)S(1)} %collective-permute-done.8.lower_ref, f32[6,12,128]{2,1,0:T(8,128)S(1)} %get-tuple-element.18.own_ref, f32[6,6,128]{2,1,0:T(8,128)S(1)} %collective-permute-done.9.upper_ref), custom_call_target="tpu_custom_call" | custom-call | tf_op jit(solution)/shard_map/place/pallas_call | solution.py:375
Async XLA Ops:
  1.5 7.8 %collective-permute-start.3 = (f32[4,12,128]{2,1,0:T(8,128)S(1)}, f32[4,12,128]{2,1,0:T(8,128)S(1)}, u32[]{:S(2)}, u32[]{:S(2)}) collective-permute-start(f32[4,12,128]{2,1,0:T(8,128)S(1)} %get-tuple-element.11.own_ref), channel_id=1, source_target_pairs={{0,30},{1,31},{2,0},{3,1},{4,2},{5,3},{6,4},{7,5},{8,6},{9,7},{10,... | collective-permute-start | bytes 73736 | tf_op jit(solution)/shard_map/ppermute | solution.py:25
  7.6 3.3 %collective-permute-start.2 = (f32[4,12,128]{2,1,0:T(8,128)S(1)}, f32[4,12,128]{2,1,0:T(8,128)S(1)}, u32[]{:S(2)}, u32[]{:S(2)}) collective-permute-start(f32[4,12,128]{2,1,0:T(8,128)S(1)} %get-tuple-element.11.own_ref), channel_id=1, source_target_pairs={{0,31},{1,0},{2,1},{3,2},{4,3},{5,4},{6,5},{7,6},{8,7},{9,8},{10,9... | collective-permute-start | bytes 73736 | tf_op jit(solution)/shard_map/ppermute | solution.py:25
  8.5 2.4 %collective-permute-start.1 = (f32[4,12,128]{2,1,0:T(8,128)S(1)}, f32[4,12,128]{2,1,0:T(8,128)S(1)}, u32[]{:S(2)}, u32[]{:S(2)}) collective-permute-start(f32[4,12,128]{2,1,0:T(8,128)S(1)} %get-tuple-element.11.own_ref), channel_id=1, source_target_pairs={{0,1},{1,2},{2,3},{3,4},{4,5},{5,6},{6,7},{7,8},{8,9},{9,10},{10,1... | collective-permute-start | bytes 73736 | tf_op jit(solution)/shard_map/ppermute | solution.py:25
  9.3 6.8 %collective-permute-start = (f32[4,12,128]{2,1,0:T(8,128)S(1)}, f32[4,12,128]{2,1,0:T(8,128)S(1)}, u32[]{:S(2)}, u32[]{:S(2)}) collective-permute-start(f32[4,12,128]{2,1,0:T(8,128)S(1)} %get-tuple-element.11.own_ref), channel_id=1, source_target_pairs={{0,2},{1,3},{2,4},{3,5},{4,6},{5,7},{6,8},{7,9},{8,10},{9,11},{10,... | collective-permute-start | bytes 73736 | tf_op jit(solution)/shard_map/ppermute | solution.py:25
  38.1 4.2 %collective-permute-start.7 = (f32[6,12,128]{2,1,0:T(8,128)S(1)}, f32[6,12,128]{2,1,0:T(8,128)S(1)}, u32[]{:S(2)}, u32[]{:S(2)}) collective-permute-start(f32[6,12,128]{2,1,0:T(8,128)S(1)} %get-tuple-element.14.own_ref), channel_id=1, source_target_pairs={{0,30},{1,31},{2,0},{3,1},{4,2},{5,3},{6,4},{7,5},{8,6},{9,7},{10,... | collective-permute-start | bytes 110600 | tf_op jit(solution)/shard_map/ppermute | solution.py:25
  38.1 4.1 %collective-permute-start.6 = (f32[6,12,128]{2,1,0:T(8,128)S(1)}, f32[6,12,128]{2,1,0:T(8,128)S(1)}, u32[]{:S(2)}, u32[]{:S(2)}) collective-permute-start(f32[6,12,128]{2,1,0:T(8,128)S(1)} %get-tuple-element.14.own_ref), channel_id=1, source_target_pairs={{0,31},{1,0},{2,1},{3,2},{4,3},{5,4},{6,5},{7,6},{8,7},{9,8},{10,9... | collective-permute-start | bytes 110600 | tf_op jit(solution)/shard_map/ppermute | solution.py:25
  38.4 3.9 %collective-permute-start.5 = (f32[6,12,128]{2,1,0:T(8,128)S(1)}, f32[6,12,128]{2,1,0:T(8,128)S(1)}, u32[]{:S(2)}, u32[]{:S(2)}) collective-permute-start(f32[6,12,128]{2,1,0:T(8,128)S(1)} %get-tuple-element.14.own_ref), channel_id=1, source_target_pairs={{0,1},{1,2},{2,3},{3,4},{4,5},{5,6},{6,7},{7,8},{8,9},{9,10},{10,1... | collective-permute-start | bytes 110600 | tf_op jit(solution)/shard_map/ppermute | solution.py:25
  40.0 6.6 %collective-permute-start.4 = (f32[6,12,128]{2,1,0:T(8,128)S(1)}, f32[6,12,128]{2,1,0:T(8,128)S(1)}, u32[]{:S(2)}, u32[]{:S(2)}) collective-permute-start(f32[6,12,128]{2,1,0:T(8,128)S(1)} %get-tuple-element.14.own_ref), channel_id=1, source_target_pairs={{0,2},{1,3},{2,4},{3,5},{4,6},{5,7},{6,8},{7,9},{8,10},{9,11},{10,... | collective-permute-start | bytes 110600 | tf_op jit(solution)/shard_map/ppermute | solution.py:25
  68.6 4.3 %collective-permute-start.8 = (f32[6,6,128]{2,1,0:T(8,128)S(1)}, f32[6,6,128]{2,1,0:T(8,128)S(1)}, u32[]{:S(2)}, u32[]{:S(2)}) collective-permute-start(f32[6,6,128]{2,1,0:T(8,128)S(1)} %get-tuple-element.17), channel_id=1, source_target_pairs={{0,1},{1,2},{2,3},{3,4},{4,5},{5,6},{6,7},{7,8},{8,9},{9,10},{10,1... | collective-permute-start | bytes 55304 | tf_op jit(solution)/shard_map/ppermute | solution.py:31
  70.5 5.1 %collective-permute-start.9 = (f32[6,6,128]{2,1,0:T(8,128)S(1)}, f32[6,6,128]{2,1,0:T(8,128)S(1)}, u32[]{:S(2)}, u32[]{:S(2)}) collective-permute-start(f32[6,6,128]{2,1,0:T(8,128)S(1)} %get-tuple-element.19), channel_id=1, source_target_pairs={{1,0},{2,1},{3,2},{4,3},{5,4},{6,5},{7,6},{8,7},{9,8},{10,9},{11,1... | collective-permute-start | bytes 55304 | tf_op jit(solution)/shard_map/ppermute | solution.py:31

commit v3 on v2

--- a/solution.py
+++ b/solution.py
@@ -13,7 +13,7 @@
 soften = 0.05
 time_step = 0.5
 reach = 2
-chunk = 4
+chunk = 8
 feature_rows = 32
 far_norm = 1e36
 lanes = 128
@@ -51,19 +51,19 @@
 
 
 def pack_kernel(total_tiles, particles_ref, occupancy_ref, neighbours_ref, packed_ref, speed_ref):
-    tiles, slots = packed_ref.shape[1:]
+    tiles, slots = (particles_ref.shape[0], particles_ref.shape[2])
     listed = neighbours_ref.shape[1]
     for row in range(3):
-        packed_ref[row] = particles_ref[:, row, :]
-        speed_ref[row] = particles_ref[:, 3 + row, :]
+        packed_ref[row * tiles : (row + 1) * tiles, :] = particles_ref[:, row, :]
+        speed_ref[row * tiles : (row + 1) * tiles, :] = particles_ref[:, 3 + row, :]
     tile_ids = lax.broadcasted_iota(jnp.int32, (tiles, listed), 0)
     offsets = neighbours_ref[...] - (device_index() * tiles + tile_ids)
     offsets = jnp.where(offsets < 0, offsets + total_tiles, offsets)
-    packed_ref[3] = jnp.zeros((tiles, slots), jnp.float32)
-    packed_ref[3, :, :listed] = offsets.astype(jnp.float32)
+    packed_ref[3 * tiles :, :] = jnp.zeros((tiles, slots), jnp.float32)
+    packed_ref[3 * tiles :, :listed] = offsets.astype(jnp.float32)
     for tile in range(tiles):
         live = occupancy_ref[tile].astype(jnp.float32)
-        packed_ref[3, tile : tile + 1, listed : listed + 1] = jnp.full((1, 1), live)
+        packed_ref[3 * tiles + tile : 3 * tiles + tile + 1, listed : listed + 1] = jnp.full((1, 1), live)
 
 
 def build_lists(aux, window, tiles, listed, rows):
@@ -181,27 +181,53 @@
             sums_ref[row, tile : tile + 1, :] = jnp.sum(jnp.transpose(total_ref[tile, row]), axis=0, keepdims=True)
 
 
-def advance(centred, place_own, speed_own, weight_own, sums_ref, state_ref):
+def advance(centred, place_own, speed_own, weight_own, sums_ref):
     tiles = weight_own.shape[0]
     center = reach * tiles
     zeroth = sums_ref[3, :tiles, :]
+    places, speeds = ([], [])
     for axis in range(3):
         force = sums_ref[axis, :tiles, :] - centred[axis][center : center + tiles] * zeroth
-        speed = weight_own * (speed_own[axis] + time_step * force / lanes)
-        state_ref[axis] = weight_own * (place_own[axis] + time_step * speed)
-        state_ref[3 + axis] = speed
+        speeds.append(weight_own * (speed_own[axis] + time_step * force / lanes))
+        places.append(weight_own * (place_own[axis] + time_step * speeds[axis]))
+    return places, speeds
+
+
+def part_of(ref, tiles, row):
+    return ref[row * tiles : (row + 1) * tiles, :]
+
+
+def fill_planes(planes, tiles, blocks):
+    kinds, rows, slots = planes.shape
+    window = (2 * reach + 1) * tiles
+    planes[:, window:, :] = jnp.zeros((kinds, rows - window, slots), jnp.float32)
+    for block, ref in enumerate(blocks):
+        for kind in range(kinds):
+            planes[kind, block * tiles : (block + 1) * tiles, :] = part_of(ref, tiles, kind)
 
 
 def first_kernel(
-    listed, before_2, before_1, own_ref, after_1, after_2, speed_ref, state_ref, weight_ref, lists_ref, *scratch
+    listed,
+    before_2,
+    before_1,
+    own_ref,
+    after_1,
+    after_2,
+    speed_ref,
+    place_out,
+    speed_out,
+    down_out,
+    up_out,
+    weight_ref,
+    lists_ref,
+    *scratch
 ):
     planes, scalars, copy_sem, feature_ref, moment_ref, source_ref, target_ref, *loop_refs = scratch
-    tiles, slots = own_ref.shape[1:]
-    rows = planes.shape[1]
+    rows, slots = planes.shape[1:]
+    tiles = own_ref.shape[0] // 4
+    half = tiles // 2
     window = (2 * reach + 1) * tiles
-    planes[:, window:, :] = jnp.zeros((4, rows - window, slots), jnp.float32)
-    for block, ref in enumerate((before_2, before_1, own_ref, after_1, after_2)):
-        planes[:, block * tiles : (block + 1) * tiles, :] = ref[...]
+    fill_planes(planes, tiles, (before_2, before_1, own_ref, after_1, after_2))
     aux = planes[3]
     for row, value in enumerate(build_lists(aux, window, tiles, listed, rows)):
         lists_ref[row : row + 1, :] = value
@@ -215,14 +241,22 @@
     copy.wait()
     accumulate(tiles, scalars, source_ref, target_ref, moment_ref, *loop_refs)
     center = reach * tiles
-    advance(
+    places, speeds = advance(
         centred,
-        [own_ref[axis] for axis in range(3)],
-        [speed_ref[axis] for axis in range(3)],
+        [part_of(own_ref, tiles, axis) for axis in range(3)],
+        [part_of(speed_ref, tiles, axis) for axis in range(3)],
         weight[center : center + tiles],
         loop_refs[-1],
-        state_ref,
     )
+    for axis in range(3):
+        strip = slice(axis * tiles, (axis + 1) * tiles)
+        place_out[strip, :] = places[axis]
+        speed_out[strip, :] = speeds[axis]
+        down_out[strip, :] = places[axis]
+        up_out[strip, :] = places[axis]
+        strip = slice(3 * tiles + axis * half, 3 * tiles + (axis + 1) * half)
+        down_out[strip, :] = speeds[axis][:half]
+        up_out[strip, :] = speeds[axis][tiles - half :]
 
 
 def place_rows(step, total_tiles, cuts_ref, lower, own, upper, pool_ref, out_ref):
@@ -253,6 +287,7 @@
     own_ref,
     after_1,
     after_2,
+    speed_ref,
     weight_ref,
     state_ref,
     down_ref,
@@ -261,51 +296,46 @@
     *scratch
 ):
     planes, scalars, copy_sem, pool_ref, feature_ref, moment_ref, source_ref, target_ref, *loop_refs = scratch
-    tiles, slots = own_ref.shape[1:]
+    tiles = own_ref.shape[0] // 3
     half = tiles // 2
-    rows = planes.shape[1]
-    window = (2 * reach + 1) * tiles
     copy = pltpu.make_async_copy(lists_ref, scalars, copy_sem)
     copy.start()
-    planes[:, window:, :] = jnp.zeros((3, rows - window, slots), jnp.float32)
-    for block, ref in enumerate((before_2, before_1, own_ref, after_1, after_2)):
-        planes[:, block * tiles : (block + 1) * tiles, :] = ref[:3]
+    fill_planes(planes, tiles, (before_2, before_1, own_ref, after_1, after_2))
     weight = weight_ref[...]
     refs = (feature_ref, moment_ref, source_ref, target_ref)
     centred = build_features([planes[axis] for axis in range(3)], weight, tiles, refs)
     copy.wait()
     accumulate(tiles, scalars, source_ref, target_ref, moment_ref, *loop_refs)
     center = reach * tiles
-    advance(
-        centred,
-        [own_ref[axis] for axis in range(3)],
-        [own_ref[3 + axis] for axis in range(3)],
-        weight[center : center + tiles],
-        loop_refs[-1],
-        state_ref,
-    )
-    down_ref[...] = state_ref[:, :half, :]
-    up_ref[...] = state_ref[:, tiles - half :, :]
+    place_own = [part_of(own_ref, tiles, axis) for axis in range(3)]
+    speed_own = [part_of(speed_ref, tiles, axis) for axis in range(3)]
+    places, speeds = advance(centred, place_own, speed_own, weight[center : center + tiles], loop_refs[-1])
+    for row, value in enumerate(places + speeds):
+        state_ref[row] = value
+        down_ref[row * half : (row + 1) * half, :] = value[:half]
+        up_ref[row * half : (row + 1) * half, :] = value[tiles - half :]
+    speed_rows = [slice(3 * tiles + axis * half, 3 * tiles + (axis + 1) * half) for axis in range(3)]
     place_rows(
         0,
         total_tiles,
         cuts_ref,
-        [before_1[row, tiles - half :, :] for row in range(6)],
-        [own_ref[row] for row in range(6)],
-        [after_1[row, :half, :] for row in range(6)],
+        [part_of(before_1, tiles, axis)[tiles - half :] for axis in range(3)] + [before_1[strip, :] for strip in speed_rows],
+        place_own + speed_own,
+        [part_of(after_1, tiles, axis)[:half] for axis in range(3)] + [after_1[strip, :] for strip in speed_rows],
         pool_ref,
         out_ref,
     )
 
 
 def third_kernel(total_tiles, cuts_ref, lower_ref, own_ref, upper_ref, out_ref, pool_ref):
+    half = own_ref.shape[1] // 2
     place_rows(
         1,
         total_tiles,
         cuts_ref,
-        [lower_ref[row] for row in range(6)],
+        [part_of(lower_ref, half, row) for row in range(6)],
         [own_ref[row] for row in range(6)],
-        [upper_ref[row] for row in range(6)],
+        [part_of(upper_ref, half, row) for row in range(6)],
         pool_ref,
         out_ref,
     )
@@ -331,7 +361,7 @@
 
     packed, speed = pl.pallas_call(
         functools.partial(pack_kernel, total_tiles),
-        out_shape=(held(4, tiles, slots), held(3, tiles, slots)),
+        out_shape=(held(4 * tiles, slots), held(3 * tiles, slots)),
         in_specs=[vmem, smem, vmem],
         out_specs=(vmem, vmem),
         name="pack",
@@ -347,29 +377,37 @@
         pltpu.VMEM((4, round_up(tiles, 8), lanes), jnp.float32),
     ]
     pool_scratch = pltpu.VMEM((6, round_up(capacity + tiles, 8), slots), jnp.float32)
-    blocks = [near(value) for value in (shifted(packed, 2), shifted(packed, 1), packed, shifted(packed, -1), shifted(packed, -2))]
-    state, weight, lists = pl.pallas_call(
+    blocks = [shifted(packed, 2), shifted(packed, 1), packed, shifted(packed, -1), shifted(packed, -2)]
+    edge = 3 * tiles + 3 * half
+    place, speed, down, up, weight, lists = pl.pallas_call(
         functools.partial(first_kernel, listed),
-        out_shape=(held(6, tiles, slots), held(rows, slots), held(list_rows, lanes, dtype=jnp.int32)),
+        out_shape=(
+            held(3 * tiles, slots),
+            held(3 * tiles, slots),
+            held(edge, slots),
+            held(edge, slots),
+            held(rows, slots),
+            held(list_rows, lanes, dtype=jnp.int32),
+        ),
         in_specs=[vmem] * 6,
-        out_specs=(vmem, vmem, vmem),
+        out_specs=[vmem] * 6,
         scratch_shapes=[pltpu.VMEM((4, rows, slots), jnp.float32)] + list_scratch + feature_scratch,
         name="first_step",
-    )(*blocks, near(speed))
-    blocks = [near(value) for value in (shifted(state, 2), shifted(state, 1), state, shifted(state, -1), shifted(state, -2))]
+    )(*[near(value) for value in blocks], near(speed))
+    blocks = [shifted(place, 2), shifted(up, 1), place, shifted(down, -1), shifted(place, -2)]
     state_2, down, up, after_first = pl.pallas_call(
         functools.partial(second_kernel, total_tiles),
         out_shape=(
             held(6, tiles, slots),
-            held(6, half, slots),
-            held(6, half, slots),
+            held(6 * half, slots),
+            held(6 * half, slots),
             jax.ShapeDtypeStruct((6, capacity, slots), jnp.float32),
         ),
-        in_specs=[smem] + [vmem] * 7,
-        out_specs=(vmem, vmem, vmem, vmem),
+        in_specs=[smem] + [vmem] * 8,
+        out_specs=[vmem] * 4,
         scratch_shapes=[pltpu.VMEM((3, rows, slots), jnp.float32)] + list_scratch + [pool_scratch] + feature_scratch,
         name="second_step",
-    )(curve_cuts, near(lists), *blocks, near(weight))
+    )(curve_cuts, near(lists), *[near(value) for value in blocks], near(speed), near(weight))
     lower = shifted_open(up, 1)
     upper = shifted_open(down, -1)
     after_second = pl.pallas_call(

time: 77.4 us -> 76.3 us (0.986)
  Pallas kernels: 46.1 us -> 42.8 us
  waiting for transfers between devices: 13.9 us -> 15.6 us
    pallas_call x1, Pallas kernels: 21.9 us -> 20.2 us  [body(): pl.pallas_call(functools.partial(first_kernel, listed), out_shape=(held(3...]
    ppermute x8, waiting for transfers between devices: 11.2 us -> 12.9 us  [shifted(): return lax.ppermute(value, AXES, pairs)]
    pallas_call x1, Pallas kernels: 22 us -> 20.4 us  [body(): pl.pallas_call(functools.partial(second_kernel, total_tiles), out_shape=(...]
  transfers between devices with their start and end apart: 10 -> 10, of which waited for: 4 -> 5; matrix products, arithmetic and copies ran while one was open for 0% -> 0% of each run, Pallas kernels for 0% -> 0%
where the time goes in v3:
time: 76.3 us; the launch traced here: 75.9 us
  Pallas kernels  42.8 us (56%)
  starting transfers between devices  16.9 us (22%)
  waiting for transfers between devices  15.6 us (20%)
    pallas_call x1, Pallas kernels, body(): pl.pallas_call(functools.partial(second_kernel, total_tiles), out_shape=(...  20.4 us
    pallas_call x1, Pallas kernels, body(): pl.pallas_call(functools.partial(first_kernel, listed), out_shape=(held(3...  20.2 us
    ppermute x8, waiting for transfers between devices, shifted(): return lax.ppermute(value, AXES, pairs)  12.9 us
    ppermute x8, starting transfers between devices, shifted(): return lax.ppermute(value, AXES, pairs)  12.6 us
    ppermute x2, starting transfers between devices, shifted_open(): lax.ppermute(value, AXES, [(source, source + steps) for source in range(f...  4.32 us
    ppermute x2, waiting for transfers between devices, shifted_open(): lax.ppermute(value, AXES, [(source, source + steps) for source in range(f...  2.68 us
  transfers between devices with their start and end apart: 10, of which 5 were waited for; matrix products, arithmetic and copies ran while one was open for 0% of the time, Pallas kernels for 0%

profile of v3, /device:TPU:1, one launch (start us, length us, event | category | flops | bytes accessed | tf_op | source)
XLA Modules:
  0.0 75.9 jit_solution(182715404166358109)
XLA Ops:
  0.6 0.8 %pack.1 = (f32[48,128]{1,0:T(8,128)S(1)}, f32[36,128]{1,0:T(8,128)S(1)}) custom-call(f32[12,6,128]{2,1,0:T(8,128)} %particles_ref.1, s32[12]{0:T(128)} %occupancy_ref.1, s32[12,16]{1,0:T(8,128)} %neighbours_ref.1), custom_call_target="tpu_custom_call" | custom-call | tf_op jit(solution)/shard_map/pack/pallas_call | solution.py:362
  1.5 6.1 %collective-permute-start.3 = (f32[48,128]{1,0:T(8,128)S(1)}, f32[48,128]{1,0:T(8,128)S(1)}, u32[]{:S(2)}, u32[]{:S(2)}) collective-permute-start(f32[48,128]{1,0:T(8,128)S(1)} %get-tuple-element.14.own_ref), channel_id=1, source_target_pairs={{0,30},{1,31},{2,0},{3,1},{4,2},{5,3},{6,4},{7,5},{8,6},{9,7},{10,... | collective-permute-start | bytes 73736 | tf_op jit(solution)/shard_map/ppermute | solution.py:25
  7.6 1.0 %collective-permute-start.2 = (f32[48,128]{1,0:T(8,128)S(1)}, f32[48,128]{1,0:T(8,128)S(1)}, u32[]{:S(2)}, u32[]{:S(2)}) collective-permute-start(f32[48,128]{1,0:T(8,128)S(1)} %get-tuple-element.14.own_ref), channel_id=1, source_target_pairs={{0,31},{1,0},{2,1},{3,2},{4,3},{5,4},{6,5},{7,6},{8,7},{9,8},{10,9... | collective-permute-start | bytes 73736 | tf_op jit(solution)/shard_map/ppermute | solution.py:25
  8.5 0.8 %collective-permute-start.1 = (f32[48,128]{1,0:T(8,128)S(1)}, f32[48,128]{1,0:T(8,128)S(1)}, u32[]{:S(2)}, u32[]{:S(2)}) collective-permute-start(f32[48,128]{1,0:T(8,128)S(1)} %get-tuple-element.14.own_ref), channel_id=1, source_target_pairs={{0,1},{1,2},{2,3},{3,4},{4,5},{5,6},{6,7},{7,8},{8,9},{9,10},{10,1... | collective-permute-start | bytes 73736 | tf_op jit(solution)/shard_map/ppermute | solution.py:25
  9.3 0.0 collective-permute-start
  9.3 0.0 collective-permute-done.3.after_2
  9.3 1.5 %collective-permute-done.2.after_1 = f32[48,128]{1,0:T(8,128)S(1)} collective-permute-done((f32[48,128]{1,0:T(8,128)S(1)}, f32[48,128]{1,0:T(8,128)S(1)}, u32[]{:S(2)}, u32[]{:S(2)}) %collective-permute-start.2) | collective-permute-done | bytes 24608 | tf_op jit(solution)/shard_map/ppermute | solution.py:25
  10.8 0.0 collective-permute-done.1.before_1
  10.8 5.1 %collective-permute-done.before_2 = f32[48,128]{1,0:T(8,128)S(1)} collective-permute-done((f32[48,128]{1,0:T(8,128)S(1)}, f32[48,128]{1,0:T(8,128)S(1)}, u32[]{:S(2)}, u32[]{:S(2)}) %collective-permute-start) | collective-permute-done | bytes 24608 | tf_op jit(solution)/shard_map/ppermute | solution.py:25
  16.0 20.2 %first_step.1 = (f32[36,128]{1,0:T(8,128)S(1)}, f32[36,128]{1,0:T(8,128)S(1)}, f32[54,128]{1,0:T(8,128)S(1)}, f32[54,128]{1,0:T(8,128)S(1)}, f32[64,128]{1,0:T(8,128)S(1)}, /*index=5*/s32[16,128]{1,0:T(8,128)S(1)}) custom-call(f32[48,128]{1,0:T(8,128)S(1)} %collective-permute-done.before_2, f32[48,128]{1,0:T(8,128)S(1)} %collective-permute-done.1.before_1, ...), custom_call_target="tpu_custom_call" | custom-call | tf_op jit(solution)/shard_map/first_step/pallas_call | solution.py:382
  36.2 0.1 collective-permute-start.5
  36.2 0.5 collective-permute-start.6
  36.7 4.2 %collective-permute-start.7 = (f32[36,128]{1,0:T(8,128)S(1)}, f32[36,128]{1,0:T(8,128)S(1)}, u32[]{:S(2)}, u32[]{:S(2)}) collective-permute-start(f32[36,128]{1,0:T(8,128)S(1)} %get-tuple-element.17.own_ref), channel_id=1, source_target_pairs={{0,30},{1,31},{2,0},{3,1},{4,2},{5,3},{6,4},{7,5},{8,6},{9,7},{10,... | collective-permute-start | bytes 55304 | tf_op jit(solution)/shard_map/ppermute | solution.py:25
  40.9 0.0 collective-permute-start.4
  40.9 0.9 %collective-permute-done.7.after_2 = f32[36,128]{1,0:T(8,128)S(1)} collective-permute-done((f32[36,128]{1,0:T(8,128)S(1)}, f32[36,128]{1,0:T(8,128)S(1)}, u32[]{:S(2)}, u32[]{:S(2)}) %collective-permute-start.7) | collective-permute-done | bytes 18464 | tf_op jit(solution)/shard_map/ppermute | solution.py:25
  41.8 5.3 %collective-permute-done.4.before_2 = f32[36,128]{1,0:T(8,128)S(1)} collective-permute-done((f32[36,128]{1,0:T(8,128)S(1)}, f32[36,128]{1,0:T(8,128)S(1)}, u32[]{:S(2)}, u32[]{:S(2)}) %collective-permute-start.4) | collective-permute-done | bytes 18464 | tf_op jit(solution)/shard_map/ppermute | solution.py:25
  47.1 0.0 collective-permute-done.5.before_1
  47.1 0.0 collective-permute-done.6.after_1
  47.1 20.4 %second_step.1 = (f32[6,12,128]{2,1,0:T(8,128)S(1)}, f32[36,128]{1,0:T(8,128)S(1)}, f32[36,128]{1,0:T(8,128)S(1)}, f32[6,24,128]{2,1,0:T(8,128)}) custom-call(s32[2,32]{1,0:T(2,128)} %cuts_ref.3, s32[16,128]{1,0:T(8,128)S(1)} %get-tuple-element.16.lists_ref, f32[36,128]{1,0:T(8,128)S(1)} %collective-permute-done.4.before_2, ...), custom_call_target="tpu_custom_call" | custom-call | tf_op jit(solution)/shard_map/second_step/pallas_call | solution.py:398
  67.6 1.9 %collective-permute-start.8 = (f32[36,128]{1,0:T(8,128)S(1)}, f32[36,128]{1,0:T(8,128)S(1)}, u32[]{:S(2)}, u32[]{:S(2)}) collective-permute-start(f32[36,128]{1,0:T(8,128)S(1)} %get-tuple-element.23), channel_id=1, source_target_pairs={{0,1},{1,2},{2,3},{3,4},{4,5},{5,6},{6,7},{7,8},{8,9},{9,10},{10,1... | collective-permute-start | bytes 55304 | tf_op jit(solution)/shard_map/ppermute | solution.py:31
  69.5 2.4 %collective-permute-start.9 = (f32[36,128]{1,0:T(8,128)S(1)}, f32[36,128]{1,0:T(8,128)S(1)}, u32[]{:S(2)}, u32[]{:S(2)}) collective-permute-start(f32[36,128]{1,0:T(8,128)S(1)} %get-tuple-element.25), channel_id=1, source_target_pairs={{1,0},{2,1},{3,2},{4,3},{5,4},{6,5},{7,6},{8,7},{9,8},{10,9},{11,1... | collective-permute-start | bytes 55304 | tf_op jit(solution)/shard_map/ppermute | solution.py:31
  71.9 0.0 collective-permute-done.8.lower_ref
  71.9 2.7 %collective-permute-done.9.upper_ref = f32[36,128]{1,0:T(8,128)S(1)} collective-permute-done((f32[36,128]{1,0:T(8,128)S(1)}, f32[36,128]{1,0:T(8,128)S(1)}, u32[]{:S(2)}, u32[]{:S(2)}) %collective-permute-start.9) | collective-permute-done | bytes 18464 | tf_op jit(solution)/shard_map/ppermute | solution.py:31
  74.6 1.3 %place.1 = f32[6,24,128]{2,1,0:T(8,128)} custom-call(s32[2,32]{1,0:T(2,128)} %cuts_ref.3, f32[36,128]{1,0:T(8,128)S(1)} %collective-permute-done.8.lower_ref, f32[6,12,128]{2,1,0:T(8,128)S(1)} %get-tuple-element.24.own_ref, f32[36,128]{1,0:T(8,128)S(1)} %collective-permute-done.9.upper_ref), custom_call_target="tpu_custom_call" | custom-call | tf_op jit(solution)/shard_map/place/pallas_call | solution.py:413
Async XLA Ops:
  1.5 7.8 %collective-permute-start.3 = (f32[48,128]{1,0:T(8,128)S(1)}, f32[48,128]{1,0:T(8,128)S(1)}, u32[]{:S(2)}, u32[]{:S(2)}) collective-permute-start(f32[48,128]{1,0:T(8,128)S(1)} %get-tuple-element.14.own_ref), channel_id=1, source_target_pairs={{0,30},{1,31},{2,0},{3,1},{4,2},{5,3},{6,4},{7,5},{8,6},{9,7},{10,... | collective-permute-start | bytes 73736 | tf_op jit(solution)/shard_map/ppermute | solution.py:25
  7.6 3.3 %collective-permute-start.2 = (f32[48,128]{1,0:T(8,128)S(1)}, f32[48,128]{1,0:T(8,128)S(1)}, u32[]{:S(2)}, u32[]{:S(2)}) collective-permute-start(f32[48,128]{1,0:T(8,128)S(1)} %get-tuple-element.14.own_ref), channel_id=1, source_target_pairs={{0,31},{1,0},{2,1},{3,2},{4,3},{5,4},{6,5},{7,6},{8,7},{9,8},{10,9... | collective-permute-start | bytes 73736 | tf_op jit(solution)/shard_map/ppermute | solution.py:25
  8.5 2.3 %collective-permute-start.1 = (f32[48,128]{1,0:T(8,128)S(1)}, f32[48,128]{1,0:T(8,128)S(1)}, u32[]{:S(2)}, u32[]{:S(2)}) collective-permute-start(f32[48,128]{1,0:T(8,128)S(1)} %get-tuple-element.14.own_ref), channel_id=1, source_target_pairs={{0,1},{1,2},{2,3},{3,4},{4,5},{5,6},{6,7},{7,8},{8,9},{9,10},{10,1... | collective-permute-start | bytes 73736 | tf_op jit(solution)/shard_map/ppermute | solution.py:25
  9.3 6.7 %collective-permute-start = (f32[48,128]{1,0:T(8,128)S(1)}, f32[48,128]{1,0:T(8,128)S(1)}, u32[]{:S(2)}, u32[]{:S(2)}) collective-permute-start(f32[48,128]{1,0:T(8,128)S(1)} %get-tuple-element.14.own_ref), channel_id=1, source_target_pairs={{0,2},{1,3},{2,4},{3,5},{4,6},{5,7},{6,8},{7,9},{8,10},{9,11},{10,... | collective-permute-start | bytes 73736 | tf_op jit(solution)/shard_map/ppermute | solution.py:25
  36.2 11.0 %collective-permute-start.5 = (f32[54,128]{1,0:T(8,128)S(1)}, f32[54,128]{1,0:T(8,128)S(1)}, u32[]{:S(2)}, u32[]{:S(2)}) collective-permute-start(f32[54,128]{1,0:T(8,128)S(1)} %get-tuple-element.18), channel_id=1, source_target_pairs={{0,1},{1,2},{2,3},{3,4},{4,5},{5,6},{6,7},{7,8},{8,9},{9,10},{10,1... | collective-permute-start | bytes 82952 | tf_op jit(solution)/shard_map/ppermute | solution.py:25
  36.2 10.9 %collective-permute-start.6 = (f32[54,128]{1,0:T(8,128)S(1)}, f32[54,128]{1,0:T(8,128)S(1)}, u32[]{:S(2)}, u32[]{:S(2)}) collective-permute-start(f32[54,128]{1,0:T(8,128)S(1)} %get-tuple-element.19), channel_id=1, source_target_pairs={{0,31},{1,0},{2,1},{3,2},{4,3},{5,4},{6,5},{7,6},{8,7},{9,8},{10,9... | collective-permute-start | bytes 82952 | tf_op jit(solution)/shard_map/ppermute | solution.py:25
  36.7 5.1 %collective-permute-start.7 = (f32[36,128]{1,0:T(8,128)S(1)}, f32[36,128]{1,0:T(8,128)S(1)}, u32[]{:S(2)}, u32[]{:S(2)}) collective-permute-start(f32[36,128]{1,0:T(8,128)S(1)} %get-tuple-element.17.own_ref), channel_id=1, source_target_pairs={{0,30},{1,31},{2,0},{3,1},{4,2},{5,3},{6,4},{7,5},{8,6},{9,7},{10,... | collective-permute-start | bytes 55304 | tf_op jit(solution)/shard_map/ppermute | solution.py:25
  40.9 6.2 %collective-permute-start.4 = (f32[36,128]{1,0:T(8,128)S(1)}, f32[36,128]{1,0:T(8,128)S(1)}, u32[]{:S(2)}, u32[]{:S(2)}) collective-permute-start(f32[36,128]{1,0:T(8,128)S(1)} %get-tuple-element.17.own_ref), channel_id=1, source_target_pairs={{0,2},{1,3},{2,4},{3,5},{4,6},{5,7},{6,8},{7,9},{8,10},{9,11},{10,... | collective-permute-start | bytes 55304 | tf_op jit(solution)/shard_map/ppermute | solution.py:25
  67.6 4.3 %collective-permute-start.8 = (f32[36,128]{1,0:T(8,128)S(1)}, f32[36,128]{1,0:T(8,128)S(1)}, u32[]{:S(2)}, u32[]{:S(2)}) collective-permute-start(f32[36,128]{1,0:T(8,128)S(1)} %get-tuple-element.23), channel_id=1, source_target_pairs={{0,1},{1,2},{2,3},{3,4},{4,5},{5,6},{6,7},{7,8},{8,9},{9,10},{10,1... | collective-permute-start | bytes 55304 | tf_op jit(solution)/shard_map/ppermute | solution.py:31
  69.5 5.1 %collective-permute-start.9 = (f32[36,128]{1,0:T(8,128)S(1)}, f32[36,128]{1,0:T(8,128)S(1)}, u32[]{:S(2)}, u32[]{:S(2)}) collective-permute-start(f32[36,128]{1,0:T(8,128)S(1)} %get-tuple-element.25), channel_id=1, source_target_pairs={{1,0},{2,1},{3,2},{4,3},{5,4},{6,5},{7,6},{8,7},{9,8},{10,9},{11,1... | collective-permute-start | bytes 55304 | tf_op jit(solution)/shard_map/ppermute | solution.py:31

commit v4 on v3

--- a/solution.py
+++ b/solution.py
@@ -154,8 +154,7 @@
             sums = [total_ref[tile_1, row, strip, :] for row in range(4)]
             for entry in range(chunk):
                 column = (entry % 2) * lanes
-                inverse = lax.rsqrt(distance_ref[entry // 2, strip, column : column + lanes])
-                kernel = inverse * inverse * inverse
+                kernel = jnp.exp(-1.5 * jnp.log(distance_ref[entry // 2, strip, column : column + lanes]))
                 for axis in range(3):
                     sums[axis] = sums[axis] + kernel * places[entry][axis]
                 sums[3] = sums[3] + kernel

time: 76.3 us -> 83.5 us (1.094)
  Pallas kernels: 42.8 us -> 47.1 us
  starting transfers between devices: 16.9 us -> 19.5 us
    pallas_call x1, Pallas kernels: 20.2 us -> 22.4 us  [body(): pl.pallas_call(functools.partial(first_kernel, listed), out_shape=(held(3...]
    pallas_call x1, Pallas kernels: 20.4 us -> 22.5 us  [body(): pl.pallas_call(functools.partial(second_kernel, total_tiles), out_shape=(...]
    ppermute x8, starting transfers between devices: 12.6 us -> 14.1 us  [shifted(): return lax.ppermute(value, AXES, pairs)]
    ppermute x2, starting transfers between devices: 4.32 us -> 5.41 us  [shifted_open(): lax.ppermute(value, AXES, [(source, source + steps) for source in range(f...]
where the time goes in v4:
time: 83.5 us; the launch traced here: 83.1 us
  Pallas kernels  47.1 us (56%)
  starting transfers between devices  19.5 us (23%)
  waiting for transfers between devices  15.7 us (19%)
    pallas_call x1, Pallas kernels, body(): pl.pallas_call(functools.partial(second_kernel, total_tiles), out_shape=(...  22.5 us
    pallas_call x1, Pallas kernels, body(): pl.pallas_call(functools.partial(first_kernel, listed), out_shape=(held(3...  22.4 us
    ppermute x8, starting transfers between devices, shifted(): return lax.ppermute(value, AXES, pairs)  14.1 us
    ppermute x8, waiting for transfers between devices, shifted(): return lax.ppermute(value, AXES, pairs)  12.9 us
    ppermute x2, starting transfers between devices, shifted_open(): lax.ppermute(value, AXES, [(source, source + steps) for source in range(f...  5.41 us
    ppermute x2, waiting for transfers between devices, shifted_open(): lax.ppermute(value, AXES, [(source, source + steps) for source in range(f...  2.87 us
  transfers between devices with their start and end apart: 10, of which 5 were waited for; matrix products, arithmetic and copies ran while one was open for 0% of the time, Pallas kernels for 0%

profile of v4, /device:TPU:1, one launch (start us, length us, event | category | flops | bytes accessed | tf_op | source)
XLA Modules:
  0.0 83.1 jit_solution(9839361812109391791)
XLA Ops:
  0.6 0.8 %pack.1 = (f32[48,128]{1,0:T(8,128)S(1)}, f32[36,128]{1,0:T(8,128)S(1)}) custom-call(f32[12,6,128]{2,1,0:T(8,128)} %particles_ref.1, s32[12]{0:T(128)} %occupancy_ref.1, s32[12,16]{1,0:T(8,128)} %neighbours_ref.1), custom_call_target="tpu_custom_call" | custom-call | tf_op jit(solution)/shard_map/pack/pallas_call | solution.py:361
  1.5 6.1 %collective-permute-start.3 = (f32[48,128]{1,0:T(8,128)S(1)}, f32[48,128]{1,0:T(8,128)S(1)}, u32[]{:S(2)}, u32[]{:S(2)}) collective-permute-start(f32[48,128]{1,0:T(8,128)S(1)} %get-tuple-element.14.own_ref), channel_id=1, source_target_pairs={{0,30},{1,31},{2,0},{3,1},{4,2},{5,3},{6,4},{7,5},{8,6},{9,7},{10,... | collective-permute-start | bytes 73736 | tf_op jit(solution)/shard_map/ppermute | solution.py:25
  7.6 1.0 %collective-permute-start.2 = (f32[48,128]{1,0:T(8,128)S(1)}, f32[48,128]{1,0:T(8,128)S(1)}, u32[]{:S(2)}, u32[]{:S(2)}) collective-permute-start(f32[48,128]{1,0:T(8,128)S(1)} %get-tuple-element.14.own_ref), channel_id=1, source_target_pairs={{0,31},{1,0},{2,1},{3,2},{4,3},{5,4},{6,5},{7,6},{8,7},{9,8},{10,9... | collective-permute-start | bytes 73736 | tf_op jit(solution)/shard_map/ppermute | solution.py:25
  8.5 0.8 collective-permute-start.1
  9.3 0.0 collective-permute-start
  9.3 0.0 collective-permute-done.3.after_2
  9.3 1.5 %collective-permute-done.2.after_1 = f32[48,128]{1,0:T(8,128)S(1)} collective-permute-done((f32[48,128]{1,0:T(8,128)S(1)}, f32[48,128]{1,0:T(8,128)S(1)}, u32[]{:S(2)}, u32[]{:S(2)}) %collective-permute-start.2) | collective-permute-done | bytes 24608 | tf_op jit(solution)/shard_map/ppermute | solution.py:25
  10.8 0.0 collective-permute-done.1.before_1
  10.8 5.1 %collective-permute-done.before_2 = f32[48,128]{1,0:T(8,128)S(1)} collective-permute-done((f32[48,128]{1,0:T(8,128)S(1)}, f32[48,128]{1,0:T(8,128)S(1)}, u32[]{:S(2)}, u32[]{:S(2)}) %collective-permute-start) | collective-permute-done | bytes 24608 | tf_op jit(solution)/shard_map/ppermute | solution.py:25
  16.0 22.4 %first_step.1 = (f32[36,128]{1,0:T(8,128)S(1)}, f32[36,128]{1,0:T(8,128)S(1)}, f32[54,128]{1,0:T(8,128)S(1)}, f32[54,128]{1,0:T(8,128)S(1)}, f32[64,128]{1,0:T(8,128)S(1)}, /*index=5*/s32[16,128]{1,0:T(8,128)S(1)}) custom-call(f32[48,128]{1,0:T(8,128)S(1)} %collective-permute-done.before_2, f32[48,128]{1,0:T(8,128)S(1)} %collective-permute-done.1.before_1, ...), custom_call_target="tpu_custom_call" | custom-call | tf_op jit(solution)/shard_map/first_step/pallas_call | solution.py:381
  38.3 0.1 collective-permute-start.5
  38.4 1.3 %collective-permute-start.6 = (f32[54,128]{1,0:T(8,128)S(1)}, f32[54,128]{1,0:T(8,128)S(1)}, u32[]{:S(2)}, u32[]{:S(2)}) collective-permute-start(f32[54,128]{1,0:T(8,128)S(1)} %get-tuple-element.19), channel_id=1, source_target_pairs={{0,31},{1,0},{2,1},{3,2},{4,3},{5,4},{6,5},{7,6},{8,7},{9,8},{10,9... | collective-permute-start | bytes 82952 | tf_op jit(solution)/shard_map/ppermute | solution.py:25
  39.7 4.9 %collective-permute-start.7 = (f32[36,128]{1,0:T(8,128)S(1)}, f32[36,128]{1,0:T(8,128)S(1)}, u32[]{:S(2)}, u32[]{:S(2)}) collective-permute-start(f32[36,128]{1,0:T(8,128)S(1)} %get-tuple-element.17.own_ref), channel_id=1, source_target_pairs={{0,30},{1,31},{2,0},{3,1},{4,2},{5,3},{6,4},{7,5},{8,6},{9,7},{10,... | collective-permute-start | bytes 55304 | tf_op jit(solution)/shard_map/ppermute | solution.py:25
  44.6 0.0 collective-permute-start.4
  44.6 0.9 %collective-permute-done.7.after_2 = f32[36,128]{1,0:T(8,128)S(1)} collective-permute-done((f32[36,128]{1,0:T(8,128)S(1)}, f32[36,128]{1,0:T(8,128)S(1)}, u32[]{:S(2)}, u32[]{:S(2)}) %collective-permute-start.7) | collective-permute-done | bytes 18464 | tf_op jit(solution)/shard_map/ppermute | solution.py:25
  45.5 5.3 %collective-permute-done.4.before_2 = f32[36,128]{1,0:T(8,128)S(1)} collective-permute-done((f32[36,128]{1,0:T(8,128)S(1)}, f32[36,128]{1,0:T(8,128)S(1)}, u32[]{:S(2)}, u32[]{:S(2)}) %collective-permute-start.4) | collective-permute-done | bytes 18464 | tf_op jit(solution)/shard_map/ppermute | solution.py:25
  50.9 0.0 collective-permute-done.5.before_1
  50.9 0.0 collective-permute-done.6.after_1
  50.9 22.5 %second_step.1 = (f32[6,12,128]{2,1,0:T(8,128)S(1)}, f32[36,128]{1,0:T(8,128)S(1)}, f32[36,128]{1,0:T(8,128)S(1)}, f32[6,24,128]{2,1,0:T(8,128)}) custom-call(s32[2,32]{1,0:T(2,128)} %cuts_ref.3, s32[16,128]{1,0:T(8,128)S(1)} %get-tuple-element.16.lists_ref, f32[36,128]{1,0:T(8,128)S(1)} %collective-permute-done.4.before_2, ...), custom_call_target="tpu_custom_call" | custom-call | tf_op jit(solution)/shard_map/second_step/pallas_call | solution.py:397
  73.4 3.2 %collective-permute-start.8 = (f32[36,128]{1,0:T(8,128)S(1)}, f32[36,128]{1,0:T(8,128)S(1)}, u32[]{:S(2)}, u32[]{:S(2)}) collective-permute-start(f32[36,128]{1,0:T(8,128)S(1)} %get-tuple-element.23), channel_id=1, source_target_pairs={{0,1},{1,2},{2,3},{3,4},{4,5},{5,6},{6,7},{7,8},{8,9},{9,10},{10,1... | collective-permute-start | bytes 55304 | tf_op jit(solution)/shard_map/ppermute | solution.py:31
  76.6 2.2 %collective-permute-start.9 = (f32[36,128]{1,0:T(8,128)S(1)}, f32[36,128]{1,0:T(8,128)S(1)}, u32[]{:S(2)}, u32[]{:S(2)}) collective-permute-start(f32[36,128]{1,0:T(8,128)S(1)} %get-tuple-element.25), channel_id=1, source_target_pairs={{1,0},{2,1},{3,2},{4,3},{5,4},{6,5},{7,6},{8,7},{9,8},{10,9},{11,1... | collective-permute-start | bytes 55304 | tf_op jit(solution)/shard_map/ppermute | solution.py:31
  78.8 0.0 collective-permute-done.8.lower_ref
  78.8 2.9 %collective-permute-done.9.upper_ref = f32[36,128]{1,0:T(8,128)S(1)} collective-permute-done((f32[36,128]{1,0:T(8,128)S(1)}, f32[36,128]{1,0:T(8,128)S(1)}, u32[]{:S(2)}, u32[]{:S(2)}) %collective-permute-start.9) | collective-permute-done | bytes 18464 | tf_op jit(solution)/shard_map/ppermute | solution.py:31
  81.7 1.3 %place.1 = f32[6,24,128]{2,1,0:T(8,128)} custom-call(s32[2,32]{1,0:T(2,128)} %cuts_ref.3, f32[36,128]{1,0:T(8,128)S(1)} %collective-permute-done.8.lower_ref, f32[6,12,128]{2,1,0:T(8,128)S(1)} %get-tuple-element.24.own_ref, f32[36,128]{1,0:T(8,128)S(1)} %collective-permute-done.9.upper_ref), custom_call_target="tpu_custom_call" | custom-call | tf_op jit(solution)/shard_map/place/pallas_call | solution.py:412
Async XLA Ops:
  1.5 7.8 %collective-permute-start.3 = (f32[48,128]{1,0:T(8,128)S(1)}, f32[48,128]{1,0:T(8,128)S(1)}, u32[]{:S(2)}, u32[]{:S(2)}) collective-permute-start(f32[48,128]{1,0:T(8,128)S(1)} %get-tuple-element.14.own_ref), channel_id=1, source_target_pairs={{0,30},{1,31},{2,0},{3,1},{4,2},{5,3},{6,4},{7,5},{8,6},{9,7},{10,... | collective-permute-start | bytes 73736 | tf_op jit(solution)/shard_map/ppermute | solution.py:25
  7.6 3.3 %collective-permute-start.2 = (f32[48,128]{1,0:T(8,128)S(1)}, f32[48,128]{1,0:T(8,128)S(1)}, u32[]{:S(2)}, u32[]{:S(2)}) collective-permute-start(f32[48,128]{1,0:T(8,128)S(1)} %get-tuple-element.14.own_ref), channel_id=1, source_target_pairs={{0,31},{1,0},{2,1},{3,2},{4,3},{5,4},{6,5},{7,6},{8,7},{9,8},{10,9... | collective-permute-start | bytes 73736 | tf_op jit(solution)/shard_map/ppermute | solution.py:25
  8.5 2.3 %collective-permute-start.1 = (f32[48,128]{1,0:T(8,128)S(1)}, f32[48,128]{1,0:T(8,128)S(1)}, u32[]{:S(2)}, u32[]{:S(2)}) collective-permute-start(f32[48,128]{1,0:T(8,128)S(1)} %get-tuple-element.14.own_ref), channel_id=1, source_target_pairs={{0,1},{1,2},{2,3},{3,4},{4,5},{5,6},{6,7},{7,8},{8,9},{9,10},{10,1... | collective-permute-start | bytes 73736 | tf_op jit(solution)/shard_map/ppermute | solution.py:25
  9.3 6.7 %collective-permute-start = (f32[48,128]{1,0:T(8,128)S(1)}, f32[48,128]{1,0:T(8,128)S(1)}, u32[]{:S(2)}, u32[]{:S(2)}) collective-permute-start(f32[48,128]{1,0:T(8,128)S(1)} %get-tuple-element.14.own_ref), channel_id=1, source_target_pairs={{0,2},{1,3},{2,4},{3,5},{4,6},{5,7},{6,8},{7,9},{8,10},{9,11},{10,... | collective-permute-start | bytes 73736 | tf_op jit(solution)/shard_map/ppermute | solution.py:25
  38.3 12.5 %collective-permute-start.5 = (f32[54,128]{1,0:T(8,128)S(1)}, f32[54,128]{1,0:T(8,128)S(1)}, u32[]{:S(2)}, u32[]{:S(2)}) collective-permute-start(f32[54,128]{1,0:T(8,128)S(1)} %get-tuple-element.18), channel_id=1, source_target_pairs={{0,1},{1,2},{2,3},{3,4},{4,5},{5,6},{6,7},{7,8},{8,9},{9,10},{10,1... | collective-permute-start | bytes 82952 | tf_op jit(solution)/shard_map/ppermute | solution.py:25
  38.4 12.5 %collective-permute-start.6 = (f32[54,128]{1,0:T(8,128)S(1)}, f32[54,128]{1,0:T(8,128)S(1)}, u32[]{:S(2)}, u32[]{:S(2)}) collective-permute-start(f32[54,128]{1,0:T(8,128)S(1)} %get-tuple-element.19), channel_id=1, source_target_pairs={{0,31},{1,0},{2,1},{3,2},{4,3},{5,4},{6,5},{7,6},{8,7},{9,8},{10,9... | collective-permute-start | bytes 82952 | tf_op jit(solution)/shard_map/ppermute | solution.py:25
  39.7 5.8 %collective-permute-start.7 = (f32[36,128]{1,0:T(8,128)S(1)}, f32[36,128]{1,0:T(8,128)S(1)}, u32[]{:S(2)}, u32[]{:S(2)}) collective-permute-start(f32[36,128]{1,0:T(8,128)S(1)} %get-tuple-element.17.own_ref), channel_id=1, source_target_pairs={{0,30},{1,31},{2,0},{3,1},{4,2},{5,3},{6,4},{7,5},{8,6},{9,7},{10,... | collective-permute-start | bytes 55304 | tf_op jit(solution)/shard_map/ppermute | solution.py:25
  44.6 6.2 %collective-permute-start.4 = (f32[36,128]{1,0:T(8,128)S(1)}, f32[36,128]{1,0:T(8,128)S(1)}, u32[]{:S(2)}, u32[]{:S(2)}) collective-permute-start(f32[36,128]{1,0:T(8,128)S(1)} %get-tuple-element.17.own_ref), channel_id=1, source_target_pairs={{0,2},{1,3},{2,4},{3,5},{4,6},{5,7},{6,8},{7,9},{8,10},{9,11},{10,... | collective-permute-start | bytes 55304 | tf_op jit(solution)/shard_map/ppermute | solution.py:25
  73.4 5.4 %collective-permute-start.8 = (f32[36,128]{1,0:T(8,128)S(1)}, f32[36,128]{1,0:T(8,128)S(1)}, u32[]{:S(2)}, u32[]{:S(2)}) collective-permute-start(f32[36,128]{1,0:T(8,128)S(1)} %get-tuple-element.23), channel_id=1, source_target_pairs={{0,1},{1,2},{2,3},{3,4},{4,5},{5,6},{6,7},{7,8},{8,9},{9,10},{10,1... | collective-permute-start | bytes 55304 | tf_op jit(solution)/shard_map/ppermute | solution.py:31
  76.6 5.1 %collective-permute-start.9 = (f32[36,128]{1,0:T(8,128)S(1)}, f32[36,128]{1,0:T(8,128)S(1)}, u32[]{:S(2)}, u32[]{:S(2)}) collective-permute-start(f32[36,128]{1,0:T(8,128)S(1)} %get-tuple-element.25), channel_id=1, source_target_pairs={{1,0},{2,1},{3,2},{4,3},{5,4},{6,5},{7,6},{8,7},{9,8},{10,9},{11,1... | collective-permute-start | bytes 55304 | tf_op jit(solution)/shard_map/ppermute | solution.py:31

commit v5 on v3

v5 whole, which is shorter than its diff:
```python
import functools

import jax
import jax.numpy as jnp
from jax import lax
from jax.experimental import pallas as pl
from jax.experimental.pallas import tpu as pltpu
from jax.sharding import PartitionSpec as P

AXES = ("gx", "gy")
STEPS = 2

soften = 0.05
time_step = 0.5
reach = 2
chunk = 4
feature_rows = 32
far_norm = 1e36
lanes = 128
vmem_limit = 16 << 20


def shifted(value, steps):
    count = lax.axis_size(AXES)
    pairs = [(source, (source + steps) % count) for source in range(count)]
    return lax.ppermute(value, AXES, pairs)


def swapped(value, first, wrap=True):
    count = lax.axis_size(AXES)
    pairs = []
    for lower in range(first, count, 2):
        if wrap or lower + 1 < count:
            upper = (lower + 1) % count
            pairs += [(lower, upper), (upper, lower)]
    return lax.ppermute(value, AXES, pairs)


def round_up(value, step):
    return -(-value // step) * step


def device_index():
    return lax.axis_index("gx") * lax.axis_size("gy") + lax.axis_index("gy")


def pieces(value, count):
    parts = []
    rest = value
    for _ in range(count - 1):
        part = rest.astype(jnp.bfloat16).astype(jnp.float32)
        parts.append(part)
        rest = rest - part
    parts.append(rest.astype(jnp.bfloat16).astype(jnp.float32))
    return parts


def pack_kernel(total_tiles, particles_ref, occupancy_ref, neighbours_ref, packed_ref, speed_ref):
    tiles, slots = (particles_ref.shape[0], particles_ref.shape[2])
    listed = neighbours_ref.shape[1]
    for row in range(3):
        packed_ref[row * tiles : (row + 1) * tiles, :] = particles_ref[:, row, :]
        speed_ref[row * tiles : (row + 1) * tiles, :] = particles_ref[:, 3 + row, :]
    tile_ids = lax.broadcasted_iota(jnp.int32, (tiles, listed), 0)
    offsets = neighbours_ref[...] - (device_index() * tiles + tile_ids)
    offsets = jnp.where(offsets < 0, offsets + total_tiles, offsets)
    packed_ref[3 * tiles :, :] = jnp.zeros((tiles, slots), jnp.float32)
    packed_ref[3 * tiles :, :listed] = offsets.astype(jnp.float32)
    for tile in range(tiles):
        live = occupancy_ref[tile].astype(jnp.float32)
        packed_ref[3 * tiles + tile : 3 * tiles + tile + 1, listed : listed + 1] = jnp.full((1, 1), live)


def places_of(index, tiles, offsets):
    place = index + offsets[0]
    for block in range(1, len(offsets)):
        place = jnp.where(index >= block * tiles, index - block * tiles + offsets[block], place)
    return jnp.where(index >= len(offsets) * tiles, -1000.0, place)


def build_lists(aux, own, tiles, listed, offsets):
    rows = aux.shape[0]
    dummy = len(offsets) * tiles
    index = lax.broadcasted_iota(jnp.int32, (rows, lanes), 0).astype(jnp.float32)
    lane = lax.broadcasted_iota(jnp.int32, (rows, lanes), 1).astype(jnp.float32)
    place = places_of(index, tiles, offsets)
    mask = place == lane
    for entry in range(listed):
        mask = mask | (place + aux[:, entry : entry + 1] == lane)
    own_rows = own.shape[0]
    own_index = lax.broadcasted_iota(jnp.int32, (own_rows, lanes), 0).astype(jnp.float32)
    own_lane = lax.broadcasted_iota(jnp.int32, (own_rows, lanes), 1).astype(jnp.float32)
    own_place = places_of(own_lane, tiles, offsets)
    listing = own_index + own[:, 0:1] == own_place
    for entry in range(1, listed):
        listing = listing | (own_index + own[:, entry : entry + 1] == own_place)
    listing = jnp.where(listing, 1.0, 0.0)
    listing = jnp.concatenate([listing, jnp.zeros((lanes - own_rows, lanes), jnp.float32)], axis=0)
    listing = jnp.transpose(listing)[:rows]
    mask = jnp.maximum(jnp.where(mask, 1.0, 0.0), listing)
    mask = jnp.where((lane < tiles) & (index < dummy), mask, 0.0)
    earlier = lax.broadcasted_iota(jnp.int32, (rows, rows), 1) < lax.broadcasted_iota(jnp.int32, (rows, rows), 0)
    rank = jnp.dot(
        jnp.where(earlier, 1.0, 0.0).astype(jnp.bfloat16),
        mask.astype(jnp.bfloat16),
        preferred_element_type=jnp.float32,
    )
    key = jnp.where(mask > 0.5, rank, -1.0)
    counts = jnp.sum(mask, axis=0, keepdims=True)
    lists = []
    for tile in range(tiles):
        hit = key[:, tile : tile + 1] == lane
        lists.append(jnp.sum(jnp.where(hit, index - dummy, 0.0), axis=0, keepdims=True) + dummy)
    lists.append(jnp.full((1, lanes), float(dummy)))
    lists.append(counts)
    return [row.astype(jnp.int32) for row in lists]


def middles(own_place):
    return [jnp.mean(axis[:8], keepdims=True) for axis in own_place]


def build_sources(places, middle, weight, feature_ref, moment_ref, source_ref):
    rows = weight.shape[0]
    ones = jnp.ones_like(weight)
    zeros = jnp.zeros_like(weight)
    features = []
    norm = zeros
    for axis in range(3):
        value = weight * (places[axis] - middle[axis])
        norm = norm + value * value
        moment_ref[:rows, axis, :] = value
        high, mid, low = pieces(value, 3)
        features += [high, high, mid, mid, high, low]
    features += pieces(jnp.where(weight > 0.5, norm, far_norm), 3) + [ones] * 3
    features += [zeros] * (feature_rows - len(features))
    for row, value in enumerate(features):
        feature_ref[:rows, row, :] = value
    for tile in range(rows):
        source_ref[tile] = feature_ref[tile].astype(jnp.bfloat16)


def build_targets(own_place, middle, feature_ref, target_ref):
    tiles = own_place[0].shape[0]
    ones = jnp.ones_like(own_place[0])
    zeros = jnp.zeros_like(own_place[0])
    features = []
    norm = zeros
    for axis in range(3):
        value = own_place[axis] - middle[axis]
        norm = norm + value * value
        high, mid, low = [-2.0 * part for part in pieces(value, 3)]
        features += [high, mid, high, mid, low, high]
    features += [ones] * 3 + pieces(norm + soften, 3)
    features += [zeros] * (feature_rows - len(features))
    for row, value in enumerate(features):
        feature_ref[:tiles, row, :] = value
    blank = jnp.zeros((lanes - feature_rows, lanes), jnp.float32)
    for tile in range(tiles):
        block = jnp.concatenate([feature_ref[tile], blank], axis=0)
        target_ref[tile] = jnp.transpose(block)[:, :feature_rows].astype(jnp.bfloat16)
    target_ref[tiles] = target_ref[0]


def accumulate(tiles, lists_ref, source_ref, target_ref, moment_ref, buffers, total_ref):
    chunk_counts = [(lists_ref[tiles + 1, tile] + chunk - 1) // chunk for tile in range(tiles)]
    chunk_total = functools.reduce(lambda left, right: left + right, [jnp.maximum(count, 1) for count in chunk_counts])

    def following(tile, part):
        more = (part + 1) * chunk < lists_ref[tiles + 1, tile]
        return (jnp.where(more, tile, jnp.minimum(tile + 1, tiles)), jnp.where(more, part + 1, 0))

    def distances(tile, part, distance_ref):
        for pair in range(chunk // 2):
            sources = [lists_ref[tile, part * chunk + 2 * pair + entry] for entry in range(2)]
            distance_ref[pair] = jnp.dot(
                target_ref[tile],
                jnp.concatenate([source_ref[source] for source in sources], axis=1),
                preferred_element_type=jnp.float32,
            )

    def kernels(tile, part, distance_ref):
        places = []
        for entry in range(chunk):
            source = lists_ref[tile, part * chunk + entry]
            places.append([jnp.broadcast_to(moment_ref[source, axis : axis + 1, :], (8, lanes)) for axis in range(3)])
        for first in range(0, lanes, 8):
            strip = slice(first, first + 8)
            sums = [total_ref[tile, row, strip, :] for row in range(4)]
            for entry in range(chunk):
                column = (entry % 2) * lanes
                inverse = lax.rsqrt(distance_ref[entry // 2, strip, column : column + lanes])
                kernel = inverse * inverse * inverse
                for axis in range(3):
                    sums[axis] = sums[axis] + kernel * places[entry][axis]
                sums[3] = sums[3] + kernel
            for row in range(4):
                total_ref[tile, row, strip, :] = sums[row]

    def step(_, carry):
        tile, part = carry
        tile_1, part_1 = following(tile, part)
        tile_2, part_2 = following(tile_1, part_1)
        kernels(tile, part, buffers[0])
        distances(tile_1, part_1, buffers[1])
        kernels(tile_1, part_1, buffers[1])
        distances(tile_2, part_2, buffers[0])
        return (tile_2, part_2)

    zero = jnp.int32(0)
    distances(zero, zero, buffers[0])
    lax.fori_loop(0, (chunk_total + 1) // 2, step, (zero, zero))


def advance(middle, place_own, speed_own, weight_own, total_ref, sums_ref):
    tiles = weight_own.shape[0]
    for tile in range(tiles):
        for row in range(4):
            sums_ref[row, tile : tile + 1, :] = jnp.sum(jnp.transpose(total_ref[tile, row]), axis=0, keepdims=True)
    zeroth = sums_ref[3, :tiles, :]
    places, speeds = ([], [])
    for axis in range(3):
        force = sums_ref[axis, :tiles, :] - (place_own[axis] - middle[axis]) * zeroth
        speeds.append(weight_own * (speed_own[axis] + time_step * force / lanes))
        places.append(weight_own * (place_own[axis] + time_step * speeds[axis]))
    return places, speeds


def part_of(ref, tiles, row):
    return ref[row * tiles : (row + 1) * tiles, :]


def fill_planes(planes, tiles, blocks):
    kinds, rows, slots = planes.shape
    filled = len(blocks) * tiles
    planes[:, filled:, :] = jnp.zeros((kinds, rows - filled, slots), jnp.float32)
    for block, ref in enumerate(blocks):
        for kind in range(kinds):
            planes[kind, block * tiles : (block + 1) * tiles, :] = part_of(ref, tiles, kind)


def weights_of(aux, listed):
    slot = lax.broadcasted_iota(jnp.int32, aux.shape, 1).astype(jnp.float32)
    return jnp.where(slot < aux[:, listed : listed + 1], 1.0, 0.0)


def offsets_of(tiles, near_pair):
    toward = jnp.where(device_index() % 2 == 0, 1.0, -1.0) * float(tiles)
    if near_pair:
        return [0.0, toward]
    return [-float(reach * tiles), -toward, float(reach * tiles)]


def prepare(first, near_pair, listed, own_ref, blocks, lists_ref, weight_ref, tools):
    planes, scalars, copy_sem, feature_ref, moment_ref, source_ref = tools
    tiles = own_ref.shape[0] // planes.shape[0]
    if not first:
        copy = pltpu.make_async_copy(lists_ref, scalars, copy_sem)
        copy.start()
    fill_planes(planes, tiles, blocks)
    if first:
        aux = planes[3]
        own_aux = jnp.concatenate(
            [part_of(own_ref, tiles, 3), jnp.zeros((round_up(tiles, 8) - tiles, lanes), jnp.float32)], axis=0
        )
        for row, value in enumerate(build_lists(aux, own_aux, tiles, listed, offsets_of(tiles, near_pair))):
            lists_ref[row : row + 1, :] = value
        copy = pltpu.make_async_copy(lists_ref, scalars, copy_sem)
        copy.start()
        weight_ref[...] = weights_of(aux, listed)
    middle = middles([part_of(own_ref, tiles, axis) for axis in range(3)])
    build_sources([planes[axis] for axis in range(3)], middle, weight_ref[...], feature_ref, moment_ref, source_ref)
    return middle, copy


def begin(listed, first, *refs):
    if first:
        own_ref, sibling_ref, total_ref, target_ref, lists_ref, weight_ref, *scratch = refs
    else:
        own_ref, sibling_ref, lists_ref, weight_ref, total_ref, target_ref, *scratch = refs
    *tools, buffer_0, buffer_1 = scratch
    tiles = own_ref.shape[0] // tools[0].shape[0]
    middle, copy = prepare(first, True, listed, own_ref, (own_ref, sibling_ref), lists_ref, weight_ref, tools)
    build_targets([part_of(own_ref, tiles, axis) for axis in range(3)], middle, tools[3], target_ref)
    total_ref[...] = jnp.zeros(total_ref.shape, jnp.float32)
    copy.wait()
    accumulate(tiles, tools[1], tools[5], target_ref, tools[4], (buffer_0, buffer_1), total_ref)


def halves(speed, even, half):
    first, last = (speed[:half], speed[half:])
    return jnp.where(even, last, first), jnp.where(even, first, last)


def first_finish(
    listed, own_ref, below, beside, above, total_in, target_ref, weight_own_ref, speed_ref, *refs
):
    total_ref, lists_ref, weight_ref, place_out, speed_out, sibling_out, beside_out, *scratch = refs
    *tools, buffer_0, buffer_1, sums_ref = scratch
    tiles = own_ref.shape[0] // tools[0].shape[0]
    half = tiles // 2
    middle, copy = prepare(True, False, listed, own_ref, (below, beside, above), lists_ref, weight_ref, tools)
    copy.wait()
    accumulate(tiles, tools[1], tools[5], target_ref, tools[4], (buffer_0, buffer_1), total_ref)
    places, speeds = advance(
        middle,
        [part_of(own_ref, tiles, axis) for axis in range(3)],
        [part_of(speed_ref, tiles, axis) for axis in range(3)],
        weight_own_ref[:tiles, :],
        total_ref,
        sums_ref,
    )
    even = device_index() % 2 == 0
    for axis in range(3):
        strip = slice(axis * tiles, (axis + 1) * tiles)
        place_out[strip, :] = places[axis]
        speed_out[strip, :] = speeds[axis]
        sibling_out[strip, :] = places[axis]
        beside_out[strip, :] = places[axis]
        strip = slice(3 * tiles + axis * half, 3 * tiles + (axis + 1) * half)
        sibling_out[strip, :], beside_out[strip, :] = halves(speeds[axis], even, half)


def second_finish(
    total_tiles,
    cuts_ref,
    own_ref,
    below,
    beside,
    above,
    total_in,
    target_ref,
    weight_own_ref,
    speed_ref,
    sibling_ref,
    lists_ref,
    weight_ref,
    total_ref,
    state_ref,
    sibling_out,
    beside_out,
    out_ref,
    *scratch
):
    *tools, buffer_0, buffer_1, sums_ref, pool_ref = scratch
    tiles = own_ref.shape[0] // 3
    half = tiles // 2
    middle, copy = prepare(False, False, None, own_ref, (below, beside, above), lists_ref, weight_ref, tools)
    copy.wait()
    accumulate(tiles, tools[1], tools[5], target_ref, tools[4], (buffer_0, buffer_1), total_ref)
    place_own = [part_of(own_ref, tiles, axis) for axis in range(3)]
    speed_own = [part_of(speed_ref, tiles, axis) for axis in range(3)]
    places, speeds = advance(middle, place_own, speed_own, weight_own_ref[:tiles, :], total_ref, sums_ref)
    even = device_index() % 2 == 0
    for row, value in enumerate(places + speeds):
        state_ref[row] = value
        strip = slice(row * half, (row + 1) * half)
        sibling_out[strip, :], beside_out[strip, :] = halves(value, even, half)
    lower, upper = ([], [])
    for row in range(6):
        if row < 3:
            sides = [part_of(ref, tiles, row) for ref in (sibling_ref, beside)]
            low_sides, high_sides = ([side[tiles - half :] for side in sides], [side[:half] for side in sides])
        else:
            strip = slice(3 * tiles + (row - 3) * half, 3 * tiles + (row - 2) * half)
            low_sides = high_sides = [ref[strip, :] for ref in (sibling_ref, beside)]
        lower.append(jnp.where(even, low_sides[1], low_sides[0]))
        upper.append(jnp.where(even, high_sides[0], high_sides[1]))
    place_rows(0, total_tiles, cuts_ref, lower, place_own + speed_own, upper, pool_ref, out_ref)


def place_rows(step, total_tiles, cuts_ref, lower, own, upper, pool_ref, out_ref):
    tiles, slots = own[0].shape
    half = tiles // 2
    capacity = out_ref.shape[1]
    device = device_index()
    last = cuts_ref.shape[1] - 1
    first_tile = cuts_ref[step, device]
    next_tile = jnp.where(device == last, total_tiles, cuts_ref[step, jnp.minimum(device + 1, last)])
    owned = next_tile - first_tile
    start = first_tile - (device * tiles - half)
    filled = lax.broadcasted_iota(jnp.int32, (capacity, slots), 0) < owned
    for row in range(6):
        pool_ref[row, :half, :] = lower[row]
        pool_ref[row, half : half + tiles, :] = own[row]
        pool_ref[row, half + tiles : 2 * tiles, :] = upper[row]
    for row in range(6):
        out_ref[row] = jnp.where(filled, pool_ref[row, pl.ds(start, capacity), :], 0.0)


def third_kernel(total_tiles, cuts_ref, sibling_ref, own_ref, beside_ref, out_ref, pool_ref):
    half = own_ref.shape[1] // 2
    even = device_index() % 2 == 0
    lower, upper = ([], [])
    for row in range(6):
        sibling, beside = (part_of(sibling_ref, half, row), part_of(beside_ref, half, row))
        lower.append(jnp.where(even, beside, sibling))
        upper.append(jnp.where(even, sibling, beside))
    place_rows(1, total_tiles, cuts_ref, lower, [own_ref[row] for row in range(6)], upper, pool_ref, out_ref)


def near(value):
    return pltpu.with_memory_space_constraint(value, pltpu.VMEM)


def body(particles, occupancy, neighbours, curve_cuts):
    tiles, _, slots = particles.shape
    listed = neighbours.shape[1]
    total_tiles = tiles * lax.axis_size(AXES)
    half = tiles // 2
    capacity = 2 * tiles
    near_rows = round_up(2 * tiles + 1, 8)
    far_rows = round_up((reach + 1) * tiles + 1, 8)
    list_rows = round_up(tiles + 2, 8)
    vmem = pl.BlockSpec(memory_space=pltpu.VMEM)
    smem = pl.BlockSpec(memory_space=pltpu.SMEM)

    def held(*sizes, dtype=jnp.float32):
        return pltpu.VMEM(sizes, dtype)

    def call(kernel, name, outs, ins, scratch, flops=0, aliases=None):
        held_ins = [value if kind is smem else near(value) for kind, value in ins]
        return pl.pallas_call(
            kernel,
            out_shape=outs,
            in_specs=[kind for kind, _ in ins],
            out_specs=[vmem] * len(outs),
            scratch_shapes=scratch,
            input_output_aliases=aliases or {},
            compiler_params=pltpu.CompilerParams(vmem_limit_bytes=vmem_limit),
            cost_estimate=pl.CostEstimate(flops=flops, bytes_accessed=1 << 20, transcendentals=0),
            name=name,
        )(*held_ins)

    def tools(rows, kinds):
        return [
            pltpu.VMEM((kinds, rows, slots), jnp.float32),
            pltpu.SMEM((list_rows, lanes), jnp.int32),
            pltpu.SemaphoreType.DMA,
            pltpu.VMEM((rows, feature_rows, lanes), jnp.float32),
            pltpu.VMEM((rows, 8, lanes), jnp.float32),
            pltpu.VMEM((rows, feature_rows, lanes), jnp.bfloat16),
            pltpu.VMEM((chunk // 2, lanes, 2 * lanes), jnp.float32),
            pltpu.VMEM((chunk // 2, lanes, 2 * lanes), jnp.float32),
        ]

    packed, speed = pl.pallas_call(
        functools.partial(pack_kernel, total_tiles),
        out_shape=(held(4 * tiles, slots), held(3 * tiles, slots)),
        in_specs=[vmem, smem, vmem],
        out_specs=(vmem, vmem),
        compiler_params=pltpu.CompilerParams(vmem_limit_bytes=vmem_limit),
        name="pack",
    )(particles, occupancy, neighbours)
    pool_scratch = pltpu.VMEM((6, round_up(capacity + tiles, 8), slots), jnp.float32)
    sums_scratch = pltpu.VMEM((4, round_up(tiles, 8), lanes), jnp.float32)
    totals = held(tiles + 1, 4, lanes, lanes)
    targets = held(tiles + 1, lanes, feature_rows, dtype=jnp.bfloat16)
    lists = held(list_rows, lanes, dtype=jnp.int32)
    edge = 3 * tiles + 3 * half
    work = 1 << 32

    sibling = swapped(packed, 0)
    beside, below, above = (swapped(packed, 1), shifted(packed, reach), shifted(packed, -reach))
    total, target, near_lists, near_weight = call(
        functools.partial(begin, listed, True),
        "first_near",
        [totals, targets, lists, held(near_rows, slots)],
        [(vmem, packed), (vmem, sibling)],
        tools(near_rows, 4),
        work,
    )
    total, far_lists, far_weight, place, speed, sibling, beside = call(
        functools.partial(first_finish, listed),
        "first_far",
        [totals, lists, held(far_rows, slots), held(3 * tiles, slots), held(3 * tiles, slots), held(edge, slots), held(edge, slots)],
        [(vmem, value) for value in (packed, below, beside, above, total, target, near_weight, speed)],
        tools(far_rows, 4) + [sums_scratch],
        work,
        {4: 0},
    )
    sibling = swapped(sibling, 0)
    beside, below, above = (swapped(beside, 1), shifted(place, reach), shifted(place, -reach))
    total, target = call(
        functools.partial(begin, listed, False),
        "second_near",
        [totals, targets],
        [(vmem, value) for value in (place, sibling, near_lists, near_weight)],
        tools(near_rows, 3),
        work,
    )
    _, state, sibling, beside, after_first = call(
        functools.partial(second_finish, total_tiles),
        "second_far",
        [
            totals,
            held(6, tiles, slots),
            held(6 * half, slots),
            held(6 * half, slots),
            jax.ShapeDtypeStruct((6, capacity, slots), jnp.float32),
        ],
        [(smem, curve_cuts)]
        + [
            (vmem, value)
            for value in (place, below, beside, above, total, target, near_weight, speed, sibling, far_lists, far_weight)
        ],
        tools(far_rows, 3) + [sums_scratch, pool_scratch],
        work,
        {5: 0},
    )
    (after_second,) = call(
        functools.partial(third_kernel, total_tiles),
        "place",
        [jax.ShapeDtypeStruct((6, capacity, slots), jnp.float32)],
        [(smem, curve_cuts), (vmem, swapped(sibling, 0)), (vmem, state), (vmem, swapped(beside, 1, wrap=False))],
        [pool_scratch],
    )
    return (jnp.transpose(after_first, (1, 0, 2)), jnp.transpose(after_second, (1, 0, 2)))


def solution(mesh):
    in_specs = (P(AXES, None, None), P(AXES), P(AXES, None), P())
    out_specs = (P(AXES, None, None), P(AXES, None, None))
    return jax.shard_map(body, mesh=mesh, in_specs=in_specs, out_specs=out_specs, check_vma=False)
```

time: 76.3 us -> 74.3 us (0.974)
  waiting for transfers between devices: 15.6 us -> 3.19 us
  Pallas kernels: 42.8 us -> 47.9 us
  starting transfers between devices: 16.9 us -> 20.2 us
  local copies, waits for them, and re-layouts: 0 us -> 2.15 us
    ppermute x8 -> x4, waiting for transfers between devices: 12.9 us -> 0.01 us  [shifted(): return lax.ppermute(value, AXES, pairs)]
    pallas_call x3 -> x5, Pallas kernels: 41.9 us -> 47.4 us  [call(): pl.pallas_call(kernel, out_shape=outs, in_specs=[kind for kind, _ in ins]...]
    ppermute x2 -> x6, starting transfers between devices: 4.32 us -> 9.73 us  [swapped(): return lax.ppermute(value, AXES, pairs)]
    unnamed x0 -> x8, local copies, waits for them, and re-layouts: none -> 2.15 us
    ppermute x8 -> x4, starting transfers between devices: 12.6 us -> 10.5 us  [shifted(): return lax.ppermute(value, AXES, pairs)]
    ppermute x2 -> x6, waiting for transfers between devices: 2.68 us -> 3.18 us  [swapped(): return lax.ppermute(value, AXES, pairs)]
  transfers between devices with their start and end apart: 10 -> 10, of which waited for: 5 -> 1; matrix products, arithmetic and copies ran while one was open for 0% -> 0% of each run, Pallas kernels for 0% -> 28%
where the time goes in v5:
time: 74.3 us
  Pallas kernels  47.9 us (64%)
  starting transfers between devices  20.2 us (27%)
  waiting for transfers between devices  3.19 us (4%)
  local copies, waits for them, and re-layouts  2.15 us (3%)
  between operations  0.77 us (1%)
    pallas_call x5, Pallas kernels, call(): pl.pallas_call(kernel, out_shape=outs, in_specs=[kind for kind, _ in ins]...  47.4 us
    ppermute x4, starting transfers between devices, shifted(): return lax.ppermute(value, AXES, pairs)  10.5 us
    ppermute x6, starting transfers between devices, swapped(): return lax.ppermute(value, AXES, pairs)  9.73 us
    ppermute x6, waiting for transfers between devices, swapped(): return lax.ppermute(value, AXES, pairs)  3.18 us
    unnamed x8, local copies, waits for them, and re-layouts  2.15 us
  transfers between devices with their start and end apart: 10, of which 1 were waited for; matrix products, arithmetic and copies ran while one was open for 0% of the time, Pallas kernels for 28%

profile of v5, /device:TPU:1, one launch (start us, length us, event | category | flops | bytes accessed | tf_op | source)
XLA Modules:
  0.0 74.3 jit_solution(9695851063952612631)
XLA Ops:
  0.6 0.0 copy-start
  0.6 0.8 %copy-done = f32[12,6,128]{2,1,0:T(8,128)S(1)} copy-done((f32[12,6,128]{2,1,0:T(8,128)S(1)}, f32[12,6,128]{2,1,0:T(8,128)}, u32[]{:S(2)}) %copy-start) | copy-done | bytes 36888
  1.4 0.0 copy-start.1
  1.4 0.7 copy-done.1
  2.1 0.0 copy-start.3
  2.1 0.7 copy-done.3
  2.8 0.6 pack.1
  3.4 0.1 collective-permute-start.3
  3.5 6.7 %collective-permute-start.2 = (f32[48,128]{1,0:T(8,128)S(1)}, f32[48,128]{1,0:T(8,128)S(1)}, u32[]{:S(2)}, u32[]{:S(2)}) collective-permute-start(f32[48,128]{1,0:T(8,128)S(1)} %get-tuple-element.20.refs_0_.own_ref), channel_id=1, source_target_pairs={{0,30},{1,31},{2,0},{3,1},{4,2},{5,3},{6,4},{7,5},{8,6},{9,7},{10,... | collective-permute-start | bytes 73736 | tf_op jit(solution)/shard_map/ppermute | solution.py:26
  10.1 0.0 collective-permute-start.1
  10.1 0.0 collective-permute-start
  10.1 0.0 collective-permute-done.3.refs_1_
  10.1 10.7 %first_near.1 = (f32[13,4,128,128]{3,2,1,0:T(8,128)S(1)}, bf16[13,128,32]{2,1,0:T(8,128)(2,1)S(1)}, s32[16,128]{1,0:T(8,128)S(1)}, f32[32,128]{1,0:T(8,128)S(1)}) custom-call(f32[48,128]{1,0:T(8,128)S(1)} %get-tuple-element.20.refs_0_.own_ref, f32[48,128]{1,0:T(8,128)S(1)} %collective-permute-done.3.refs_1_), custom_call_target="tpu_custom_call" | custom-call | flops 4294967296 | bytes 1048576 | tf_op jit(solution)/shard_map/first_near/pallas_call | solution.py:423
  20.9 0.0 collective-permute-done.2.above
  20.9 0.0 collective-permute-done.1.beside
  20.9 0.0 collective-permute-done.below
  20.9 12.9 %first_far.1 = (f32[13,4,128,128]{3,2,1,0:T(8,128)S(1)}, s32[16,128]{1,0:T(8,128)S(1)}, f32[40,128]{1,0:T(8,128)S(1)}, f32[36,128]{1,0:T(8,128)S(1)}, f32[36,128...) custom-call(f32[48,128]{1,0:T(8,128)S(1)} %get-tuple-element.20.refs_0_.own_ref,, ...), custom_call_target="tpu_custom_call", output_to_operand_aliasing={{0}: (4, {})} | custom-call | flops 4294967296 | bytes 1048576 | tf_op jit(solution)/shard_map/first_far/pallas_call | solution.py:423
  33.8 2.2 %collective-permute-start.7 = (f32[54,128]{1,0:T(8,128)S(1)}, f32[54,128]{1,0:T(8,128)S(1)}, u32[]{:S(2)}, u32[]{:S(2)}) collective-permute-start(f32[54,128]{1,0:T(8,128)S(1)} %get-tuple-element.27), channel_id=1, source_target_pairs={{0,1},{1,0},{2,3},{3,2},{4,5},{5,4},{6,7},{7,6},{8,9},{9,8},{10,11... | collective-permute-start | bytes 82952 | tf_op jit(solution)/shard_map/ppermute | solution.py:36
  36.0 3.8 %collective-permute-start.6 = (f32[36,128]{1,0:T(8,128)S(1)}, f32[36,128]{1,0:T(8,128)S(1)}, u32[]{:S(2)}, u32[]{:S(2)}) collective-permute-start(f32[36,128]{1,0:T(8,128)S(1)} %get-tuple-element.25.refs_0_.own_ref), channel_id=1, source_target_pairs={{0,30},{1,31},{2,0},{3,1},{4,2},{5,3},{6,4},{7,5},{8,6},{9,7},{10,... | collective-permute-start | bytes 55304 | tf_op jit(solution)/shard_map/ppermute | solution.py:26
  39.8 0.0 collective-permute-start.4
  39.8 0.0 collective-permute-start.5
  39.8 0.0 collective-permute-done.7.refs_1_.sibling_ref
  39.8 0.0 copy-start.2
  39.8 9.7 %second_near.1 = (f32[13,4,128,128]{3,2,1,0:T(8,128)S(1)}, bf16[13,128,32]{2,1,0:T(8,128)(2,1)S(1)}) custom-call(f32[36,128]{1,0:T(8,128)S(1)} %get-tuple-element.25.refs_0_.own_ref, f32[54,128]{1,0:T(8,128)S(1)} %collective-permute-done.7.refs_1_.sibling_ref, s32[16,128]{1,0:T(8,128)S(1)} %get-tuple-element.28.refs_2_, ...), custom_call_target="tpu_custom_call" | custom-call | flops 4294967296 | bytes 1048576 | tf_op jit(solution)/shard_map/second_near/pallas_call | solution.py:423
  49.6 0.0 collective-permute-done.6.above
  49.6 0.0 collective-permute-done.4.below
  49.6 0.0 collective-permute-done.5.beside
  49.6 0.0 copy-done.2
  49.6 12.8 %second_far.1 = (f32[13,4,128,128]{3,2,1,0:T(8,128)S(1)}, f32[6,12,128]{2,1,0:T(8,128)S(1)}, f32[36,128]{1,0:T(8,128)S(1)}, f32[36,128]{1,0:T(8,128)S(1)}, f32[6,24,128]{2,1,0:T(8,128)}) custom-call(s32[2,32]{1,0:T(2,128)S(1)} %copy-done.2, f32[36,128]{1,0:T(8,128)S(1)} %get-tuple-element.25.refs_0_.own_ref, ...), custom_call_target="tpu_custom_call", output_to_operand_aliasing={{0}: (5, {})} | custom-call | flops 4294967296 | bytes 1048576 | tf_op jit(solution)/shard_map/second_far/pallas_call | solution.py:423
  62.5 5.5 %collective-permute-start.8 = (f32[36,128]{1,0:T(8,128)S(1)}, f32[36,128]{1,0:T(8,128)S(1)}, u32[]{:S(2)}, u32[]{:S(2)}) collective-permute-start(f32[36,128]{1,0:T(8,128)S(1)} %get-tuple-element.35), channel_id=1, source_target_pairs={{0,1},{1,0},{2,3},{3,2},{4,5},{5,4},{6,7},{7,6},{8,9},{9,8},{10,11... | collective-permute-start | bytes 55304 | tf_op jit(solution)/shard_map/ppermute | solution.py:36
  68.0 1.9 %collective-permute-start.9 = (f32[36,128]{1,0:T(8,128)S(1)}, f32[36,128]{1,0:T(8,128)S(1)}, u32[]{:S(2)}, u32[]{:S(2)}) collective-permute-start(f32[36,128]{1,0:T(8,128)S(1)} %get-tuple-element.37), channel_id=1, source_target_pairs={{1,2},{2,1},{3,4},{4,3},{5,6},{6,5},{7,8},{8,7},{9,10},{10,9},{11,... | collective-permute-start | bytes 55304 | tf_op jit(solution)/shard_map/ppermute | solution.py:36
  69.9 0.0 collective-permute-done.8.sibling_ref
  69.9 3.2 %collective-permute-done.9.beside_ref = f32[36,128]{1,0:T(8,128)S(1)} collective-permute-done((f32[36,128]{1,0:T(8,128)S(1)}, f32[36,128]{1,0:T(8,128)S(1)}, u32[]{:S(2)}, u32[]{:S(2)}) %collective-permute-start.9) | collective-permute-done | bytes 18464 | tf_op jit(solution)/shard_map/ppermute | solution.py:36
  73.1 1.2 %place.1 = f32[6,24,128]{2,1,0:T(8,128)} custom-call(s32[2,32]{1,0:T(2,128)S(1)} %copy-done.2, f32[36,128]{1,0:T(8,128)S(1)} %collective-permute-done.8.sibling_ref, f32[6,12,128]{2,1,0:T(8,128)S(1)} %get-tuple-element.36.own_ref, f32[36,128]{1,0:T(8,128)S(1)} %collective-permute-done.9.beside_ref), custom_call_target="tpu_custom_call" | custom-call | bytes 1048576 | tf_op jit(solution)/shard_map/place/pallas_call | solution.py:423
Async XLA Ops:
  0.6 0.8 %copy-start = (f32[12,6,128]{2,1,0:T(8,128)S(1)}, f32[12,6,128]{2,1,0:T(8,128)}, u32[]{:S(2)}) copy-start(f32[12,6,128]{2,1,0:T(8,128)} %particles_ref.1) | copy-start | bytes 110596
  1.4 0.7 copy-start.1
  2.1 0.7 copy-start.3
  3.4 6.8 %collective-permute-start.3 = (f32[48,128]{1,0:T(8,128)S(1)}, f32[48,128]{1,0:T(8,128)S(1)}, u32[]{:S(2)}, u32[]{:S(2)}) collective-permute-start(f32[48,128]{1,0:T(8,128)S(1)} %get-tuple-element.20.refs_0_.own_ref), channel_id=1, source_target_pairs={{0,1},{1,0},{2,3},{3,2},{4,5},{5,4},{6,7},{7,6},{8,9},{9,8},{10,11... | collective-permute-start | bytes 73736 | tf_op jit(solution)/shard_map/ppermute | solution.py:36
  3.5 17.4 %collective-permute-start.2 = (f32[48,128]{1,0:T(8,128)S(1)}, f32[48,128]{1,0:T(8,128)S(1)}, u32[]{:S(2)}, u32[]{:S(2)}) collective-permute-start(f32[48,128]{1,0:T(8,128)S(1)} %get-tuple-element.20.refs_0_.own_ref), channel_id=1, source_target_pairs={{0,30},{1,31},{2,0},{3,1},{4,2},{5,3},{6,4},{7,5},{8,6},{9,7},{10,... | collective-permute-start | bytes 73736 | tf_op jit(solution)/shard_map/ppermute | solution.py:26
  10.1 10.7 %collective-permute-start.1 = (f32[48,128]{1,0:T(8,128)S(1)}, f32[48,128]{1,0:T(8,128)S(1)}, u32[]{:S(2)}, u32[]{:S(2)}) collective-permute-start(f32[48,128]{1,0:T(8,128)S(1)} %get-tuple-element.20.refs_0_.own_ref), channel_id=1, source_target_pairs={{1,2},{2,1},{3,4},{4,3},{5,6},{6,5},{7,8},{8,7},{9,10},{10,9},{11,... | collective-permute-start | bytes 73736 | tf_op jit(solution)/shard_map/ppermute | solution.py:36
  10.1 10.7 %collective-permute-start = (f32[48,128]{1,0:T(8,128)S(1)}, f32[48,128]{1,0:T(8,128)S(1)}, u32[]{:S(2)}, u32[]{:S(2)}) collective-permute-start(f32[48,128]{1,0:T(8,128)S(1)} %get-tuple-element.20.refs_0_.own_ref), channel_id=1, source_target_pairs={{0,2},{1,3},{2,4},{3,5},{4,6},{5,7},{6,8},{7,9},{8,10},{9,11},{10,... | collective-permute-start | bytes 73736 | tf_op jit(solution)/shard_map/ppermute | solution.py:26
  33.8 6.0 %collective-permute-start.7 = (f32[54,128]{1,0:T(8,128)S(1)}, f32[54,128]{1,0:T(8,128)S(1)}, u32[]{:S(2)}, u32[]{:S(2)}) collective-permute-start(f32[54,128]{1,0:T(8,128)S(1)} %get-tuple-element.27), channel_id=1, source_target_pairs={{0,1},{1,0},{2,3},{3,2},{4,5},{5,4},{6,7},{7,6},{8,9},{9,8},{10,11... | collective-permute-start | bytes 82952 | tf_op jit(solution)/shard_map/ppermute | solution.py:36
  36.0 13.6 %collective-permute-start.6 = (f32[36,128]{1,0:T(8,128)S(1)}, f32[36,128]{1,0:T(8,128)S(1)}, u32[]{:S(2)}, u32[]{:S(2)}) collective-permute-start(f32[36,128]{1,0:T(8,128)S(1)} %get-tuple-element.25.refs_0_.own_ref), channel_id=1, source_target_pairs={{0,30},{1,31},{2,0},{3,1},{4,2},{5,3},{6,4},{7,5},{8,6},{9,7},{10,... | collective-permute-start | bytes 55304 | tf_op jit(solution)/shard_map/ppermute | solution.py:26
  39.8 9.8 %collective-permute-start.4 = (f32[36,128]{1,0:T(8,128)S(1)}, f32[36,128]{1,0:T(8,128)S(1)}, u32[]{:S(2)}, u32[]{:S(2)}) collective-permute-start(f32[36,128]{1,0:T(8,128)S(1)} %get-tuple-element.25.refs_0_.own_ref), channel_id=1, source_target_pairs={{0,2},{1,3},{2,4},{3,5},{4,6},{5,7},{6,8},{7,9},{8,10},{9,11},{10,... | collective-permute-start | bytes 55304 | tf_op jit(solution)/shard_map/ppermute | solution.py:26
  39.8 9.8 %collective-permute-start.5 = (f32[54,128]{1,0:T(8,128)S(1)}, f32[54,128]{1,0:T(8,128)S(1)}, u32[]{:S(2)}, u32[]{:S(2)}) collective-permute-start(f32[54,128]{1,0:T(8,128)S(1)} %get-tuple-element.26), channel_id=1, source_target_pairs={{1,2},{2,1},{3,4},{4,3},{5,6},{6,5},{7,8},{8,7},{9,10},{10,9},{11,... | collective-permute-start | bytes 82952 | tf_op jit(solution)/shard_map/ppermute | solution.py:36
  39.8 9.8 %copy-start.2 = (s32[2,32]{1,0:T(2,128)S(1)}, s32[2,32]{1,0:T(2,128)}, u32[]{:S(2)}) copy-start(s32[2,32]{1,0:T(2,128)} %cuts_ref.3) | copy-start | bytes 772
  62.5 7.4 %collective-permute-start.8 = (f32[36,128]{1,0:T(8,128)S(1)}, f32[36,128]{1,0:T(8,128)S(1)}, u32[]{:S(2)}, u32[]{:S(2)}) collective-permute-start(f32[36,128]{1,0:T(8,128)S(1)} %get-tuple-element.35), channel_id=1, source_target_pairs={{0,1},{1,0},{2,3},{3,2},{4,5},{5,4},{6,7},{7,6},{8,9},{9,8},{10,11... | collective-permute-start | bytes 55304 | tf_op jit(solution)/shard_map/ppermute | solution.py:36
  68.0 5.1 %collective-permute-start.9 = (f32[36,128]{1,0:T(8,128)S(1)}, f32[36,128]{1,0:T(8,128)S(1)}, u32[]{:S(2)}, u32[]{:S(2)}) collective-permute-start(f32[36,128]{1,0:T(8,128)S(1)} %get-tuple-element.37), channel_id=1, source_target_pairs={{1,2},{2,1},{3,4},{4,3},{5,6},{6,5},{7,8},{8,7},{9,10},{10,9},{11,... | collective-permute-start | bytes 55304 | tf_op jit(solution)/shard_map/ppermute | solution.py:36

commit v6 on v5

--- a/solution.py
+++ b/solution.py
@@ -15,6 +15,7 @@
 reach = 2
 chunk = 4
 feature_rows = 32
+moment_rows = 16
 far_norm = 1e36
 lanes = 128
 vmem_limit = 16 << 20
@@ -120,24 +121,35 @@
     return [jnp.mean(axis[:8], keepdims=True) for axis in own_place]
 
 
-def build_sources(places, middle, weight, feature_ref, moment_ref, source_ref):
+def build_sources(places, middle, weight, feature_ref, moment_ref, source_ref, moments_ref):
     rows = weight.shape[0]
     ones = jnp.ones_like(weight)
     zeros = jnp.zeros_like(weight)
     features = []
+    moments = []
     norm = zeros
     for axis in range(3):
         value = weight * (places[axis] - middle[axis])
         norm = norm + value * value
-        moment_ref[:rows, axis, :] = value
         high, mid, low = pieces(value, 3)
         features += [high, high, mid, mid, high, low]
+        moments += [high, mid, low]
     features += pieces(jnp.where(weight > 0.5, norm, far_norm), 3) + [ones] * 3
     features += [zeros] * (feature_rows - len(features))
+    moments.append(weight)
+    moments += [zeros] * (moment_rows - len(moments))
     for row, value in enumerate(features):
         feature_ref[:rows, row, :] = value
+    for row, value in enumerate(moments):
+        moment_ref[:, row, :] = value
     for tile in range(rows):
         source_ref[tile] = feature_ref[tile].astype(jnp.bfloat16)
+    group = lanes // moment_rows
+    lane_group = lax.broadcasted_iota(jnp.int32, (lanes, lanes), 1) // moment_rows
+    for first in range(0, rows, group):
+        block = jnp.transpose(moment_ref[first : first + group].reshape(lanes, lanes))
+        for entry in range(group):
+            moments_ref[first + entry] = jnp.where(lane_group == entry, block, 0.0).astype(jnp.bfloat16)
 
 
 def build_targets(own_place, middle, feature_ref, target_ref):
@@ -155,68 +167,78 @@
     features += [zeros] * (feature_rows - len(features))
     for row, value in enumerate(features):
         feature_ref[:tiles, row, :] = value
-    blank = jnp.zeros((lanes - feature_rows, lanes), jnp.float32)
+    lane_group = lax.broadcasted_iota(jnp.int32, (lanes, lanes), 1) // feature_rows
+    pairs = chunk // 2
     for tile in range(tiles):
-        block = jnp.concatenate([feature_ref[tile], blank], axis=0)
-        target_ref[tile] = jnp.transpose(block)[:, :feature_rows].astype(jnp.bfloat16)
+        feature = feature_ref[tile]
+        block = jnp.transpose(jnp.concatenate([feature] * (lanes // feature_rows), axis=0))
+        for pair in range(pairs):
+            part = jnp.where(lane_group == pair, block, 0.0)[:, : pairs * feature_rows]
+            target_ref[tile, pair * lanes : (pair + 1) * lanes, :] = part.astype(jnp.bfloat16)
     target_ref[tiles] = target_ref[0]
 
 
-def accumulate(tiles, lists_ref, source_ref, target_ref, moment_ref, buffers, total_ref):
+def accumulate(tiles, lists_ref, source_ref, target_ref, moments_ref, buffers, total_ref):
     chunk_counts = [(lists_ref[tiles + 1, tile] + chunk - 1) // chunk for tile in range(tiles)]
     chunk_total = functools.reduce(lambda left, right: left + right, [jnp.maximum(count, 1) for count in chunk_counts])
+    distance_refs, kernel_refs = (buffers[:2], buffers[2:])
 
     def following(tile, part):
         more = (part + 1) * chunk < lists_ref[tiles + 1, tile]
         return (jnp.where(more, tile, jnp.minimum(tile + 1, tiles)), jnp.where(more, part + 1, 0))
 
+    def sources_of(tile, part):
+        return [lists_ref[tile, part * chunk + entry] for entry in range(chunk)]
+
     def distances(tile, part, distance_ref):
+        features = [source_ref[source] for source in sources_of(tile, part)]
+        pairs = [jnp.concatenate(features[first : first + 2], axis=1) for first in range(0, chunk, 2)]
+        distance_ref[...] = jnp.dot(target_ref[tile], jnp.concatenate(pairs, axis=0), preferred_element_type=jnp.float32)
+
+    def kernels(distance_ref, kernel_ref):
         for pair in range(chunk // 2):
-            sources = [lists_ref[tile, part * chunk + 2 * pair + entry] for entry in range(2)]
-            distance_ref[pair] = jnp.dot(
-                target_ref[tile],
-                jnp.concatenate([source_ref[source] for source in sources], axis=1),
-                preferred_element_type=jnp.float32,
-            )
-
-    def kernels(tile, part, distance_ref):
-        places = []
-        for entry in range(chunk):
-            source = lists_ref[tile, part * chunk + entry]
-            places.append([jnp.broadcast_to(moment_ref[source, axis : axis + 1, :], (8, lanes)) for axis in range(3)])
-        for first in range(0, lanes, 8):
-            strip = slice(first, first + 8)
-            sums = [total_ref[tile, row, strip, :] for row in range(4)]
-            for entry in range(chunk):
-                column = (entry % 2) * lanes
-                inverse = lax.rsqrt(distance_ref[entry // 2, strip, column : column + lanes])
+            columns = slice(pair * 2 * lanes, (pair + 1) * 2 * lanes)
+            for first in range(0, lanes, 16):
+                inverse = lax.rsqrt(distance_ref[pair * lanes + first : pair * lanes + first + 16, :])
                 kernel = inverse * inverse * inverse
-                for axis in range(3):
-                    sums[axis] = sums[axis] + kernel * places[entry][axis]
-                sums[3] = sums[3] + kernel
-            for row in range(4):
-                total_ref[tile, row, strip, :] = sums[row]
+                high = kernel.astype(jnp.bfloat16)
+                kernel_ref[first : first + 16, columns] = high
+                kernel_ref[lanes + first : lanes + first + 16, columns] = (kernel - high.astype(jnp.float32)).astype(
+                    jnp.bfloat16
+                )
+
+    def sums(tile, part, kernel_ref):
+        moments = jnp.concatenate([moments_ref[source] for source in sources_of(tile, part)], axis=0)
+        both = jnp.dot(kernel_ref[...], moments, preferred_element_type=jnp.float32)
+        total_ref[tile] += both[:lanes] + both[lanes:]
 
     def step(_, carry):
-        tile, part = carry
-        tile_1, part_1 = following(tile, part)
+        (tile_0, part_0), (tile_1, part_1) = carry
         tile_2, part_2 = following(tile_1, part_1)
-        kernels(tile, part, buffers[0])
-        distances(tile_1, part_1, buffers[1])
-        kernels(tile_1, part_1, buffers[1])
-        distances(tile_2, part_2, buffers[0])
-        return (tile_2, part_2)
+        tile_3, part_3 = following(tile_2, part_2)
+        sums(tile_0, part_0, kernel_refs[1])
+        kernels(distance_refs[0], kernel_refs[0])
+        distances(tile_2, part_2, distance_refs[1])
+        sums(tile_1, part_1, kernel_refs[0])
+        kernels(distance_refs[1], kernel_refs[1])
+        distances(tile_3, part_3, distance_refs[0])
+        return ((tile_2, part_2), (tile_3, part_3))
 
     zero = jnp.int32(0)
-    distances(zero, zero, buffers[0])
-    lax.fori_loop(0, (chunk_total + 1) // 2, step, (zero, zero))
+    spare = jnp.int32(tiles)
+    distances(zero, zero, distance_refs[0])
+    lax.fori_loop(0, (chunk_total + 2) // 2, step, ((spare, zero), (zero, zero)))
 
 
 def advance(middle, place_own, speed_own, weight_own, total_ref, sums_ref):
     tiles = weight_own.shape[0]
     for tile in range(tiles):
-        for row in range(4):
-            sums_ref[row, tile : tile + 1, :] = jnp.sum(jnp.transpose(total_ref[tile, row]), axis=0, keepdims=True)
+        folded = jnp.sum(jnp.transpose(total_ref[tile]).reshape(lanes // moment_rows, moment_rows, lanes), axis=0)
+        for axis in range(3):
+            sums_ref[axis, tile : tile + 1, :] = (
+                folded[3 * axis : 3 * axis + 1] + folded[3 * axis + 1 : 3 * axis + 2] + folded[3 * axis + 2 : 3 * axis + 3]
+            )
+        sums_ref[3, tile : tile + 1, :] = folded[9:10]
     zeroth = sums_ref[3, :tiles, :]
     places, speeds = ([], [])
     for axis in range(3):
@@ -252,7 +274,7 @@
 
 
 def prepare(first, near_pair, listed, own_ref, blocks, lists_ref, weight_ref, tools):
-    planes, scalars, copy_sem, feature_ref, moment_ref, source_ref = tools
+    planes, scalars, copy_sem, feature_ref, moment_ref, source_ref, moments_ref = tools
     tiles = own_ref.shape[0] // planes.shape[0]
     if not first:
         copy = pltpu.make_async_copy(lists_ref, scalars, copy_sem)
@@ -269,7 +291,7 @@
         copy.start()
         weight_ref[...] = weights_of(aux, listed)
     middle = middles([part_of(own_ref, tiles, axis) for axis in range(3)])
-    build_sources([planes[axis] for axis in range(3)], middle, weight_ref[...], feature_ref, moment_ref, source_ref)
+    build_sources([planes[axis] for axis in range(3)], middle, weight_ref[...], feature_ref, moment_ref, source_ref, moments_ref)
     return middle, copy
 
 
@@ -278,13 +300,13 @@
         own_ref, sibling_ref, total_ref, target_ref, lists_ref, weight_ref, *scratch = refs
     else:
         own_ref, sibling_ref, lists_ref, weight_ref, total_ref, target_ref, *scratch = refs
-    *tools, buffer_0, buffer_1 = scratch
+    tools, buffers = (scratch[:7], scratch[7:])
     tiles = own_ref.shape[0] // tools[0].shape[0]
     middle, copy = prepare(first, True, listed, own_ref, (own_ref, sibling_ref), lists_ref, weight_ref, tools)
     build_targets([part_of(own_ref, tiles, axis) for axis in range(3)], middle, tools[3], target_ref)
     total_ref[...] = jnp.zeros(total_ref.shape, jnp.float32)
     copy.wait()
-    accumulate(tiles, tools[1], tools[5], target_ref, tools[4], (buffer_0, buffer_1), total_ref)
+    accumulate(tiles, tools[1], tools[5], target_ref, tools[6], buffers, total_ref)
 
 
 def halves(speed, even, half):
@@ -296,12 +318,13 @@
     listed, own_ref, below, beside, above, total_in, target_ref, weight_own_ref, speed_ref, *refs
 ):
     total_ref, lists_ref, weight_ref, place_out, speed_out, sibling_out, beside_out, *scratch = refs
-    *tools, buffer_0, buffer_1, sums_ref = scratch
+    *rest, sums_ref = scratch
+    tools, buffers = (rest[:7], rest[7:])
     tiles = own_ref.shape[0] // tools[0].shape[0]
     half = tiles // 2
     middle, copy = prepare(True, False, listed, own_ref, (below, beside, above), lists_ref, weight_ref, tools)
     copy.wait()
-    accumulate(tiles, tools[1], tools[5], target_ref, tools[4], (buffer_0, buffer_1), total_ref)
+    accumulate(tiles, tools[1], tools[5], target_ref, tools[6], buffers, total_ref)
     places, speeds = advance(
         middle,
         [part_of(own_ref, tiles, axis) for axis in range(3)],
@@ -342,12 +365,13 @@
     out_ref,
     *scratch
 ):
-    *tools, buffer_0, buffer_1, sums_ref, pool_ref = scratch
+    *rest, sums_ref, pool_ref = scratch
+    tools, buffers = (rest[:7], rest[7:])
     tiles = own_ref.shape[0] // 3
     half = tiles // 2
     middle, copy = prepare(False, False, None, own_ref, (below, beside, above), lists_ref, weight_ref, tools)
     copy.wait()
-    accumulate(tiles, tools[1], tools[5], target_ref, tools[4], (buffer_0, buffer_1), total_ref)
+    accumulate(tiles, tools[1], tools[5], target_ref, tools[6], buffers, total_ref)
     place_own = [part_of(own_ref, tiles, axis) for axis in range(3)]
     speed_own = [part_of(speed_ref, tiles, axis) for axis in range(3)]
     places, speeds = advance(middle, place_own, speed_own, weight_own_ref[:tiles, :], total_ref, sums_ref)
@@ -438,10 +462,13 @@
             pltpu.SMEM((list_rows, lanes), jnp.int32),
             pltpu.SemaphoreType.DMA,
             pltpu.VMEM((rows, feature_rows, lanes), jnp.float32),
-            pltpu.VMEM((rows, 8, lanes), jnp.float32),
+            pltpu.VMEM((rows, moment_rows, lanes), jnp.float32),
             pltpu.VMEM((rows, feature_rows, lanes), jnp.bfloat16),
-            pltpu.VMEM((chunk // 2, lanes, 2 * lanes), jnp.float32),
-            pltpu.VMEM((chunk // 2, lanes, 2 * lanes), jnp.float32),
+            pltpu.VMEM((rows, lanes, lanes), jnp.bfloat16),
+            pltpu.VMEM((chunk // 2 * lanes, 2 * lanes), jnp.float32),
+            pltpu.VMEM((chunk // 2 * lanes, 2 * lanes), jnp.float32),
+            pltpu.VMEM((2 * lanes, chunk * lanes), jnp.bfloat16),
+            pltpu.VMEM((2 * lanes, chunk * lanes), jnp.bfloat16),
         ]
 
     packed, speed = pl.pallas_call(
@@ -454,8 +481,8 @@
     )(particles, occupancy, neighbours)
     pool_scratch = pltpu.VMEM((6, round_up(capacity + tiles, 8), slots), jnp.float32)
     sums_scratch = pltpu.VMEM((4, round_up(tiles, 8), lanes), jnp.float32)
-    totals = held(tiles + 1, 4, lanes, lanes)
-    targets = held(tiles + 1, lanes, feature_rows, dtype=jnp.bfloat16)
+    totals = held(tiles + 1, lanes, lanes)
+    targets = held(tiles + 1, chunk // 2 * lanes, chunk // 2 * feature_rows, dtype=jnp.bfloat16)
     lists = held(list_rows, lanes, dtype=jnp.int32)
     edge = 3 * tiles + 3 * half
     work = 1 << 32

time: 74.3 us -> 78.8 us (1.061)
  Pallas kernels: 47.9 us -> 50.3 us
  starting transfers between devices: 20.2 us -> 21.8 us
    pallas_call x5, Pallas kernels: 47.4 us -> 49.7 us  [call(): pl.pallas_call(kernel, out_shape=outs, in_specs=[kind for kind, _ in ins]...]
    ppermute x6, starting transfers between devices: 9.73 us -> 11.2 us  [swapped(): return lax.ppermute(value, AXES, pairs)]
  transfers between devices with their start and end apart: 10 -> 10, of which waited for: 1 -> 1; matrix products, arithmetic and copies ran while one was open for 0% -> 0% of each run, Pallas kernels for 28% -> 29%
where the time goes in v6:
time: 78.8 us
  Pallas kernels  50.3 us (64%)
  starting transfers between devices  21.8 us (28%)
  waiting for transfers between devices  3.19 us (4%)
  local copies, waits for them, and re-layouts  2.82 us (4%)
    pallas_call x5, Pallas kernels, call(): pl.pallas_call(kernel, out_shape=outs, in_specs=[kind for kind, _ in ins]...  49.7 us
    ppermute x6, starting transfers between devices, swapped(): return lax.ppermute(value, AXES, pairs)  11.2 us
    ppermute x4, starting transfers between devices, shifted(): return lax.ppermute(value, AXES, pairs)  10.6 us
    ppermute x6, waiting for transfers between devices, swapped(): return lax.ppermute(value, AXES, pairs)  3.18 us
    unnamed x8, local copies, waits for them, and re-layouts  2.82 us
  transfers between devices with their start and end apart: 10, of which 1 were waited for; matrix products, arithmetic and copies ran while one was open for 0% of the time, Pallas kernels for 29%

profile of v6, /device:TPU:1, one launch (start us, length us, event | category | flops | bytes accessed | tf_op | source)
XLA Modules:
  0.0 78.8 jit_solution(14561007146668258205)
XLA Ops:
  0.6 0.0 copy-start
  0.6 0.8 %copy-done = f32[12,6,128]{2,1,0:T(8,128)S(1)} copy-done((f32[12,6,128]{2,1,0:T(8,128)S(1)}, f32[12,6,128]{2,1,0:T(8,128)}, u32[]{:S(2)}) %copy-start) | copy-done | bytes 36888
  1.4 0.0 copy-start.1
  1.4 0.7 copy-done.1
  2.1 0.0 copy-start.3
  2.1 0.7 copy-done.3
  2.8 0.6 pack.1
  3.4 0.1 collective-permute-start.3
  3.5 6.7 %collective-permute-start.2 = (f32[48,128]{1,0:T(8,128)S(1)}, f32[48,128]{1,0:T(8,128)S(1)}, u32[]{:S(2)}, u32[]{:S(2)}) collective-permute-start(f32[48,128]{1,0:T(8,128)S(1)} %get-tuple-element.20.refs_0_.own_ref), channel_id=1, source_target_pairs={{0,30},{1,31},{2,0},{3,1},{4,2},{5,3},{6,4},{7,5},{8,6},{9,7},{10,... | collective-permute-start | bytes 73736 | tf_op jit(solution)/shard_map/ppermute | solution.py:27
  10.1 0.0 collective-permute-start.1
  10.1 0.0 collective-permute-start
  10.1 0.0 collective-permute-done.3.refs_1_
  10.1 11.8 %first_near.1 = (f32[13,128,128]{2,1,0:T(8,128)S(1)}, bf16[13,256,64]{2,1,0:T(8,128)(2,1)S(1)}, s32[16,128]{1,0:T(8,128)S(1)}, f32[32,128]{1,0:T(8,128)S(1)}) custom-call(f32[48,128]{1,0:T(8,128)S(1)} %get-tuple-element.20.refs_0_.own_ref, f32[48,128]{1,0:T(8,128)S(1)} %collective-permute-done.3.refs_1_), custom_call_target="tpu_custom_call" | custom-call | flops 4294967296 | bytes 1048576 | tf_op jit(solution)/shard_map/first_near/pallas_call | solution.py:447
  21.9 0.0 collective-permute-done.2.above
  22.0 0.0 collective-permute-done.1.beside
  22.0 0.0 collective-permute-done.below
  22.0 12.9 %first_far.1 = (f32[13,128,128]{2,1,0:T(8,128)S(1)}, s32[16,128]{1,0:T(8,128)S(1)}, f32[40,128]{1,0:T(8,128)S(1)}, f32[36,128]{1,0:T(8,128)S(1)}, f32[36,128]{1,...) custom-call(f32[48,128]{1,0:T(8,128)S(1)} %get-tuple-element.20.refs_0_.own_ref, ...), custom_call_target="tpu_custom_call", output_to_operand_aliasing={{0}: (4, {})} | custom-call | flops 4294967296 | bytes 1048576 | tf_op jit(solution)/shard_map/first_far/pallas_call | solution.py:447
  34.9 2.9 %collective-permute-start.7 = (f32[54,128]{1,0:T(8,128)S(1)}, f32[54,128]{1,0:T(8,128)S(1)}, u32[]{:S(2)}, u32[]{:S(2)}) collective-permute-start(f32[54,128]{1,0:T(8,128)S(1)} %get-tuple-element.27), channel_id=1, source_target_pairs={{0,1},{1,0},{2,3},{3,2},{4,5},{5,4},{6,7},{7,6},{8,9},{9,8},{10,11... | collective-permute-start | bytes 82952 | tf_op jit(solution)/shard_map/ppermute | solution.py:37
  37.8 4.0 %collective-permute-start.6 = (f32[36,128]{1,0:T(8,128)S(1)}, f32[36,128]{1,0:T(8,128)S(1)}, u32[]{:S(2)}, u32[]{:S(2)}) collective-permute-start(f32[36,128]{1,0:T(8,128)S(1)} %get-tuple-element.25.refs_0_.own_ref), channel_id=1, source_target_pairs={{0,30},{1,31},{2,0},{3,1},{4,2},{5,3},{6,4},{7,5},{8,6},{9,7},{10,... | collective-permute-start | bytes 55304 | tf_op jit(solution)/shard_map/ppermute | solution.py:27
  41.8 0.0 collective-permute-start.4
  41.8 0.0 collective-permute-start.5
  41.8 0.0 collective-permute-done.7.refs_1_.sibling_ref
  41.8 10.9 %second_near.1 = (f32[13,128,128]{2,1,0:T(8,128)S(1)}, bf16[13,256,64]{2,1,0:T(8,128)(2,1)S(1)}) custom-call(f32[36,128]{1,0:T(8,128)S(1)} %get-tuple-element.25.refs_0_.own_ref, f32[54,128]{1,0:T(8,128)S(1)} %collective-permute-done.7.refs_1_.sibling_ref, s32[16,128]{1,0:T(8,128)S(1)} %get-tuple-element.28.refs_2_, ...), custom_call_target="tpu_custom_call" | custom-call | flops 4294967296 | bytes 1048576 | tf_op jit(solution)/shard_map/second_near/pallas_call | solution.py:447
  52.7 0.0 collective-permute-done.6.above
  52.7 0.0 collective-permute-done.4.below
  52.7 0.0 collective-permute-done.5.beside
  52.7 0.0 copy-start.2
  52.7 0.7 copy-done.2
  53.4 12.9 %second_far.1 = (f32[13,128,128]{2,1,0:T(8,128)S(1)}, f32[6,12,128]{2,1,0:T(8,128)S(1)}, f32[36,128]{1,0:T(8,128)S(1)}, f32[36,128]{1,0:T(8,128)S(1)}, f32[6,24,128]{2,1,0:T(8,128)}) custom-call(s32[2,32]{1,0:T(2,128)S(1)} %copy-done.2, f32[36,128]{1,0:T(8,128)S(1)} %get-tuple-element.25.refs_0_.own_ref, ...), custom_call_target="tpu_custom_call", output_to_operand_aliasing={{0}: (5, {})} | custom-call | flops 4294967296 | bytes 1048576 | tf_op jit(solution)/shard_map/second_far/pallas_call | solution.py:447
  66.3 6.2 %collective-permute-start.8 = (f32[36,128]{1,0:T(8,128)S(1)}, f32[36,128]{1,0:T(8,128)S(1)}, u32[]{:S(2)}, u32[]{:S(2)}) collective-permute-start(f32[36,128]{1,0:T(8,128)S(1)} %get-tuple-element.35), channel_id=1, source_target_pairs={{0,1},{1,0},{2,3},{3,2},{4,5},{5,4},{6,7},{7,6},{8,9},{9,8},{10,11... | collective-permute-start | bytes 55304 | tf_op jit(solution)/shard_map/ppermute | solution.py:37
  72.5 1.9 %collective-permute-start.9 = (f32[36,128]{1,0:T(8,128)S(1)}, f32[36,128]{1,0:T(8,128)S(1)}, u32[]{:S(2)}, u32[]{:S(2)}) collective-permute-start(f32[36,128]{1,0:T(8,128)S(1)} %get-tuple-element.37), channel_id=1, source_target_pairs={{1,2},{2,1},{3,4},{4,3},{5,6},{6,5},{7,8},{8,7},{9,10},{10,9},{11,... | collective-permute-start | bytes 55304 | tf_op jit(solution)/shard_map/ppermute | solution.py:37
  74.4 0.0 collective-permute-done.8.sibling_ref
  74.4 3.2 %collective-permute-done.9.beside_ref = f32[36,128]{1,0:T(8,128)S(1)} collective-permute-done((f32[36,128]{1,0:T(8,128)S(1)}, f32[36,128]{1,0:T(8,128)S(1)}, u32[]{:S(2)}, u32[]{:S(2)}) %collective-permute-start.9) | collective-permute-done | bytes 18464 | tf_op jit(solution)/shard_map/ppermute | solution.py:37
  77.6 1.2 %place.1 = f32[6,24,128]{2,1,0:T(8,128)} custom-call(s32[2,32]{1,0:T(2,128)S(1)} %copy-done.2, f32[36,128]{1,0:T(8,128)S(1)} %collective-permute-done.8.sibling_ref, f32[6,12,128]{2,1,0:T(8,128)S(1)} %get-tuple-element.36.own_ref, f32[36,128]{1,0:T(8,128)S(1)} %collective-permute-done.9.beside_ref), custom_call_target="tpu_custom_call" | custom-call | bytes 1048576 | tf_op jit(solution)/shard_map/place/pallas_call | solution.py:447
Async XLA Ops:
  0.6 0.8 %copy-start = (f32[12,6,128]{2,1,0:T(8,128)S(1)}, f32[12,6,128]{2,1,0:T(8,128)}, u32[]{:S(2)}) copy-start(f32[12,6,128]{2,1,0:T(8,128)} %particles_ref.1) | copy-start | bytes 110596
  1.4 0.7 copy-start.1
  2.1 0.7 copy-start.3
  3.4 6.8 %collective-permute-start.3 = (f32[48,128]{1,0:T(8,128)S(1)}, f32[48,128]{1,0:T(8,128)S(1)}, u32[]{:S(2)}, u32[]{:S(2)}) collective-permute-start(f32[48,128]{1,0:T(8,128)S(1)} %get-tuple-element.20.refs_0_.own_ref), channel_id=1, source_target_pairs={{0,1},{1,0},{2,3},{3,2},{4,5},{5,4},{6,7},{7,6},{8,9},{9,8},{10,11... | collective-permute-start | bytes 73736 | tf_op jit(solution)/shard_map/ppermute | solution.py:37
  3.5 18.5 %collective-permute-start.2 = (f32[48,128]{1,0:T(8,128)S(1)}, f32[48,128]{1,0:T(8,128)S(1)}, u32[]{:S(2)}, u32[]{:S(2)}) collective-permute-start(f32[48,128]{1,0:T(8,128)S(1)} %get-tuple-element.20.refs_0_.own_ref), channel_id=1, source_target_pairs={{0,30},{1,31},{2,0},{3,1},{4,2},{5,3},{6,4},{7,5},{8,6},{9,7},{10,... | collective-permute-start | bytes 73736 | tf_op jit(solution)/shard_map/ppermute | solution.py:27
  10.1 11.8 %collective-permute-start.1 = (f32[48,128]{1,0:T(8,128)S(1)}, f32[48,128]{1,0:T(8,128)S(1)}, u32[]{:S(2)}, u32[]{:S(2)}) collective-permute-start(f32[48,128]{1,0:T(8,128)S(1)} %get-tuple-element.20.refs_0_.own_ref), channel_id=1, source_target_pairs={{1,2},{2,1},{3,4},{4,3},{5,6},{6,5},{7,8},{8,7},{9,10},{10,9},{11,... | collective-permute-start | bytes 73736 | tf_op jit(solution)/shard_map/ppermute | solution.py:37
  10.1 11.8 %collective-permute-start = (f32[48,128]{1,0:T(8,128)S(1)}, f32[48,128]{1,0:T(8,128)S(1)}, u32[]{:S(2)}, u32[]{:S(2)}) collective-permute-start(f32[48,128]{1,0:T(8,128)S(1)} %get-tuple-element.20.refs_0_.own_ref), channel_id=1, source_target_pairs={{0,2},{1,3},{2,4},{3,5},{4,6},{5,7},{6,8},{7,9},{8,10},{9,11},{10,... | collective-permute-start | bytes 73736 | tf_op jit(solution)/shard_map/ppermute | solution.py:27
  34.9 6.9 %collective-permute-start.7 = (f32[54,128]{1,0:T(8,128)S(1)}, f32[54,128]{1,0:T(8,128)S(1)}, u32[]{:S(2)}, u32[]{:S(2)}) collective-permute-start(f32[54,128]{1,0:T(8,128)S(1)} %get-tuple-element.27), channel_id=1, source_target_pairs={{0,1},{1,0},{2,3},{3,2},{4,5},{5,4},{6,7},{7,6},{8,9},{9,8},{10,11... | collective-permute-start | bytes 82952 | tf_op jit(solution)/shard_map/ppermute | solution.py:37
  37.8 14.9 %collective-permute-start.6 = (f32[36,128]{1,0:T(8,128)S(1)}, f32[36,128]{1,0:T(8,128)S(1)}, u32[]{:S(2)}, u32[]{:S(2)}) collective-permute-start(f32[36,128]{1,0:T(8,128)S(1)} %get-tuple-element.25.refs_0_.own_ref), channel_id=1, source_target_pairs={{0,30},{1,31},{2,0},{3,1},{4,2},{5,3},{6,4},{7,5},{8,6},{9,7},{10,... | collective-permute-start | bytes 55304 | tf_op jit(solution)/shard_map/ppermute | solution.py:27
  41.8 10.9 %collective-permute-start.4 = (f32[36,128]{1,0:T(8,128)S(1)}, f32[36,128]{1,0:T(8,128)S(1)}, u32[]{:S(2)}, u32[]{:S(2)}) collective-permute-start(f32[36,128]{1,0:T(8,128)S(1)} %get-tuple-element.25.refs_0_.own_ref), channel_id=1, source_target_pairs={{0,2},{1,3},{2,4},{3,5},{4,6},{5,7},{6,8},{7,9},{8,10},{9,11},{10,... | collective-permute-start | bytes 55304 | tf_op jit(solution)/shard_map/ppermute | solution.py:27
  41.8 10.9 %collective-permute-start.5 = (f32[54,128]{1,0:T(8,128)S(1)}, f32[54,128]{1,0:T(8,128)S(1)}, u32[]{:S(2)}, u32[]{:S(2)}) collective-permute-start(f32[54,128]{1,0:T(8,128)S(1)} %get-tuple-element.26), channel_id=1, source_target_pairs={{1,2},{2,1},{3,4},{4,3},{5,6},{6,5},{7,8},{8,7},{9,10},{10,9},{11,... | collective-permute-start | bytes 82952 | tf_op jit(solution)/shard_map/ppermute | solution.py:37
  52.7 0.7 copy-start.2
  66.3 8.2 %collective-permute-start.8 = (f32[36,128]{1,0:T(8,128)S(1)}, f32[36,128]{1,0:T(8,128)S(1)}, u32[]{:S(2)}, u32[]{:S(2)}) collective-permute-start(f32[36,128]{1,0:T(8,128)S(1)} %get-tuple-element.35), channel_id=1, source_target_pairs={{0,1},{1,0},{2,3},{3,2},{4,5},{5,4},{6,7},{7,6},{8,9},{9,8},{10,11... | collective-permute-start | bytes 55304 | tf_op jit(solution)/shard_map/ppermute | solution.py:37
  72.5 5.1 %collective-permute-start.9 = (f32[36,128]{1,0:T(8,128)S(1)}, f32[36,128]{1,0:T(8,128)S(1)}, u32[]{:S(2)}, u32[]{:S(2)}) collective-permute-start(f32[36,128]{1,0:T(8,128)S(1)} %get-tuple-element.37), channel_id=1, source_target_pairs={{1,2},{2,1},{3,4},{4,3},{5,6},{6,5},{7,8},{8,7},{9,10},{10,9},{11,... | collective-permute-start | bytes 55304 | tf_op jit(solution)/shard_map/ppermute | solution.py:37

commit v7 on v6

--- a/solution.py
+++ b/solution.py
@@ -167,14 +167,10 @@
     features += [zeros] * (feature_rows - len(features))
     for row, value in enumerate(features):
         feature_ref[:tiles, row, :] = value
-    lane_group = lax.broadcasted_iota(jnp.int32, (lanes, lanes), 1) // feature_rows
-    pairs = chunk // 2
+    blank = jnp.zeros((lanes - feature_rows, lanes), jnp.float32)
     for tile in range(tiles):
-        feature = feature_ref[tile]
-        block = jnp.transpose(jnp.concatenate([feature] * (lanes // feature_rows), axis=0))
-        for pair in range(pairs):
-            part = jnp.where(lane_group == pair, block, 0.0)[:, : pairs * feature_rows]
-            target_ref[tile, pair * lanes : (pair + 1) * lanes, :] = part.astype(jnp.bfloat16)
+        block = jnp.concatenate([feature_ref[tile], blank], axis=0)
+        target_ref[tile] = jnp.transpose(block)[:, :feature_rows].astype(jnp.bfloat16)
     target_ref[tiles] = target_ref[0]
 
 
@@ -192,8 +188,12 @@
 
     def distances(tile, part, distance_ref):
         features = [source_ref[source] for source in sources_of(tile, part)]
-        pairs = [jnp.concatenate(features[first : first + 2], axis=1) for first in range(0, chunk, 2)]
-        distance_ref[...] = jnp.dot(target_ref[tile], jnp.concatenate(pairs, axis=0), preferred_element_type=jnp.float32)
+        for pair in range(chunk // 2):
+            distance_ref[pair * lanes : (pair + 1) * lanes, :] = jnp.dot(
+                target_ref[tile],
+                jnp.concatenate(features[2 * pair : 2 * pair + 2], axis=1),
+                preferred_element_type=jnp.float32,
+            )
 
     def kernels(distance_ref, kernel_ref):
         for pair in range(chunk // 2):
@@ -208,9 +208,16 @@
                 )
 
     def sums(tile, part, kernel_ref):
-        moments = jnp.concatenate([moments_ref[source] for source in sources_of(tile, part)], axis=0)
-        both = jnp.dot(kernel_ref[...], moments, preferred_element_type=jnp.float32)
-        total_ref[tile] += both[:lanes] + both[lanes:]
+        moments = [moments_ref[source] for source in sources_of(tile, part)]
+        total = total_ref[tile]
+        for pair in range(chunk // 2):
+            both = jnp.dot(
+                kernel_ref[:, pair * 2 * lanes : (pair + 1) * 2 * lanes],
+                jnp.concatenate(moments[2 * pair : 2 * pair + 2], axis=0),
+                preferred_element_type=jnp.float32,
+            )
+            total = total + (both[:lanes] + both[lanes:])
+        total_ref[tile] = total
 
     def step(_, carry):
         (tile_0, part_0), (tile_1, part_1) = carry
@@ -482,7 +489,7 @@
     pool_scratch = pltpu.VMEM((6, round_up(capacity + tiles, 8), slots), jnp.float32)
     sums_scratch = pltpu.VMEM((4, round_up(tiles, 8), lanes), jnp.float32)
     totals = held(tiles + 1, lanes, lanes)
-    targets = held(tiles + 1, chunk // 2 * lanes, chunk // 2 * feature_rows, dtype=jnp.bfloat16)
+    targets = held(tiles + 1, lanes, feature_rows, dtype=jnp.bfloat16)
     lists = held(list_rows, lanes, dtype=jnp.int32)
     edge = 3 * tiles + 3 * half
     work = 1 << 32

time: 78.8 us -> 78.2 us (level)
  starting transfers between devices: 21.8 us -> 20.3 us
    ppermute x6, starting transfers between devices: 11.2 us -> 9.76 us  [swapped(): return lax.ppermute(value, AXES, pairs)]
  transfers between devices with their start and end apart: 10 -> 10, of which waited for: 1 -> 1; matrix products, arithmetic and copies ran while one was open for 0% -> 0% of each run, Pallas kernels for 29% -> 31%
where the time goes in v7:
time: 78.2 us; the launch traced here: 77.6 us
  Pallas kernels  50.5 us (65%)
  starting transfers between devices  20.3 us (26%)
  waiting for transfers between devices  3.19 us (4%)
  local copies, waits for them, and re-layouts  2.82 us (4%)
    pallas_call x5, Pallas kernels, call(): pl.pallas_call(kernel, out_shape=outs, in_specs=[kind for kind, _ in ins]...  50 us
    ppermute x4, starting transfers between devices, shifted(): return lax.ppermute(value, AXES, pairs)  10.5 us
    ppermute x6, starting transfers between devices, swapped(): return lax.ppermute(value, AXES, pairs)  9.76 us
    ppermute x6, waiting for transfers between devices, swapped(): return lax.ppermute(value, AXES, pairs)  3.18 us
    unnamed x8, local copies, waits for them, and re-layouts  2.82 us
  transfers between devices with their start and end apart: 10, of which 1 were waited for; matrix products, arithmetic and copies ran while one was open for 0% of the time, Pallas kernels for 31%

profile of v7, /device:TPU:1, one launch (start us, length us, event | category | flops | bytes accessed | tf_op | source)
XLA Modules:
  0.0 77.6 jit_solution(10846409640698974279)
XLA Ops:
  0.6 0.0 copy-start
  0.6 0.8 %copy-done = f32[12,6,128]{2,1,0:T(8,128)S(1)} copy-done((f32[12,6,128]{2,1,0:T(8,128)S(1)}, f32[12,6,128]{2,1,0:T(8,128)}, u32[]{:S(2)}) %copy-start) | copy-done | bytes 36888
  1.4 0.0 copy-start.1
  1.4 0.7 copy-done.1
  2.1 0.0 copy-start.3
  2.1 0.7 copy-done.3
  2.8 0.6 pack.1
  3.4 0.1 collective-permute-start.3
  3.5 6.7 %collective-permute-start.2 = (f32[48,128]{1,0:T(8,128)S(1)}, f32[48,128]{1,0:T(8,128)S(1)}, u32[]{:S(2)}, u32[]{:S(2)}) collective-permute-start(f32[48,128]{1,0:T(8,128)S(1)} %get-tuple-element.20.refs_0_.own_ref), channel_id=1, source_target_pairs={{0,30},{1,31},{2,0},{3,1},{4,2},{5,3},{6,4},{7,5},{8,6},{9,7},{10,... | collective-permute-start | bytes 73736 | tf_op jit(solution)/shard_map/ppermute | solution.py:27
  10.1 0.0 collective-permute-start.1
  10.1 0.0 collective-permute-start
  10.1 0.0 collective-permute-done.3.refs_1_
  10.1 12.4 %first_near.1 = (f32[13,128,128]{2,1,0:T(8,128)S(1)}, bf16[13,128,32]{2,1,0:T(8,128)(2,1)S(1)}, s32[16,128]{1,0:T(8,128)S(1)}, f32[32,128]{1,0:T(8,128)S(1)}) custom-call(f32[48,128]{1,0:T(8,128)S(1)} %get-tuple-element.20.refs_0_.own_ref, f32[48,128]{1,0:T(8,128)S(1)} %collective-permute-done.3.refs_1_), custom_call_target="tpu_custom_call" | custom-call | flops 4294967296 | bytes 1048576 | tf_op jit(solution)/shard_map/first_near/pallas_call | solution.py:454
  22.5 0.0 collective-permute-done.2.above
  22.5 0.0 collective-permute-done.1.beside
  22.6 0.0 collective-permute-done.below
  22.6 12.5 %first_far.1 = (f32[13,128,128]{2,1,0:T(8,128)S(1)}, s32[16,128]{1,0:T(8,128)S(1)}, f32[40,128]{1,0:T(8,128)S(1)}, f32[36,128]{1,0:T(8,128)S(1)}, f32[36,128]{1,...) custom-call(f32[48,128]{1,0:T(8,128)S(1)} %get-tuple-element.20.refs_0_.own_ref, ...), custom_call_target="tpu_custom_call", output_to_operand_aliasing={{0}: (4, {})} | custom-call | flops 4294967296 | bytes 1048576 | tf_op jit(solution)/shard_map/first_far/pallas_call | solution.py:454
  35.0 2.2 %collective-permute-start.7 = (f32[54,128]{1,0:T(8,128)S(1)}, f32[54,128]{1,0:T(8,128)S(1)}, u32[]{:S(2)}, u32[]{:S(2)}) collective-permute-start(f32[54,128]{1,0:T(8,128)S(1)} %get-tuple-element.27), channel_id=1, source_target_pairs={{0,1},{1,0},{2,3},{3,2},{4,5},{5,4},{6,7},{7,6},{8,9},{9,8},{10,11... | collective-permute-start | bytes 82952 | tf_op jit(solution)/shard_map/ppermute | solution.py:37
  37.2 3.9 %collective-permute-start.6 = (f32[36,128]{1,0:T(8,128)S(1)}, f32[36,128]{1,0:T(8,128)S(1)}, u32[]{:S(2)}, u32[]{:S(2)}) collective-permute-start(f32[36,128]{1,0:T(8,128)S(1)} %get-tuple-element.25.refs_0_.own_ref), channel_id=1, source_target_pairs={{0,30},{1,31},{2,0},{3,1},{4,2},{5,3},{6,4},{7,5},{8,6},{9,7},{10,... | collective-permute-start | bytes 55304 | tf_op jit(solution)/shard_map/ppermute | solution.py:27
  41.1 0.0 collective-permute-start.4
  41.1 0.0 collective-permute-start.5
  41.1 0.0 collective-permute-done.7.refs_1_.sibling_ref
  41.1 11.4 %second_near.1 = (f32[13,128,128]{2,1,0:T(8,128)S(1)}, bf16[13,128,32]{2,1,0:T(8,128)(2,1)S(1)}) custom-call(f32[36,128]{1,0:T(8,128)S(1)} %get-tuple-element.25.refs_0_.own_ref, f32[54,128]{1,0:T(8,128)S(1)} %collective-permute-done.7.refs_1_.sibling_ref, s32[16,128]{1,0:T(8,128)S(1)} %get-tuple-element.28.refs_2_, ...), custom_call_target="tpu_custom_call" | custom-call | flops 4294967296 | bytes 1048576 | tf_op jit(solution)/shard_map/second_near/pallas_call | solution.py:454
  52.5 0.0 collective-permute-done.6.above
  52.5 0.0 collective-permute-done.4.below
  52.5 0.0 collective-permute-done.5.beside
  52.5 0.0 copy-start.2
  52.5 0.7 copy-done.2
  53.2 12.5 %second_far.1 = (f32[13,128,128]{2,1,0:T(8,128)S(1)}, f32[6,12,128]{2,1,0:T(8,128)S(1)}, f32[36,128]{1,0:T(8,128)S(1)}, f32[36,128]{1,0:T(8,128)S(1)}, f32[6,24,128]{2,1,0:T(8,128)}) custom-call(s32[2,32]{1,0:T(2,128)S(1)} %copy-done.2, f32[36,128]{1,0:T(8,128)S(1)} %get-tuple-element.25.refs_0_.own_ref, ...), custom_call_target="tpu_custom_call", output_to_operand_aliasing={{0}: (5, {})} | custom-call | flops 4294967296 | bytes 1048576 | tf_op jit(solution)/shard_map/second_far/pallas_call | solution.py:454
  65.7 5.5 %collective-permute-start.8 = (f32[36,128]{1,0:T(8,128)S(1)}, f32[36,128]{1,0:T(8,128)S(1)}, u32[]{:S(2)}, u32[]{:S(2)}) collective-permute-start(f32[36,128]{1,0:T(8,128)S(1)} %get-tuple-element.35), channel_id=1, source_target_pairs={{0,1},{1,0},{2,3},{3,2},{4,5},{5,4},{6,7},{7,6},{8,9},{9,8},{10,11... | collective-permute-start | bytes 55304 | tf_op jit(solution)/shard_map/ppermute | solution.py:37
  71.3 1.9 %collective-permute-start.9 = (f32[36,128]{1,0:T(8,128)S(1)}, f32[36,128]{1,0:T(8,128)S(1)}, u32[]{:S(2)}, u32[]{:S(2)}) collective-permute-start(f32[36,128]{1,0:T(8,128)S(1)} %get-tuple-element.37), channel_id=1, source_target_pairs={{1,2},{2,1},{3,4},{4,3},{5,6},{6,5},{7,8},{8,7},{9,10},{10,9},{11,... | collective-permute-start | bytes 55304 | tf_op jit(solution)/shard_map/ppermute | solution.py:37
  73.2 0.0 collective-permute-done.8.sibling_ref
  73.2 3.2 %collective-permute-done.9.beside_ref = f32[36,128]{1,0:T(8,128)S(1)} collective-permute-done((f32[36,128]{1,0:T(8,128)S(1)}, f32[36,128]{1,0:T(8,128)S(1)}, u32[]{:S(2)}, u32[]{:S(2)}) %collective-permute-start.9) | collective-permute-done | bytes 18464 | tf_op jit(solution)/shard_map/ppermute | solution.py:37
  76.4 1.2 %place.1 = f32[6,24,128]{2,1,0:T(8,128)} custom-call(s32[2,32]{1,0:T(2,128)S(1)} %copy-done.2, f32[36,128]{1,0:T(8,128)S(1)} %collective-permute-done.8.sibling_ref, f32[6,12,128]{2,1,0:T(8,128)S(1)} %get-tuple-element.36.own_ref, f32[36,128]{1,0:T(8,128)S(1)} %collective-permute-done.9.beside_ref), custom_call_target="tpu_custom_call" | custom-call | bytes 1048576 | tf_op jit(solution)/shard_map/place/pallas_call | solution.py:454
Async XLA Ops:
  0.6 0.8 %copy-start = (f32[12,6,128]{2,1,0:T(8,128)S(1)}, f32[12,6,128]{2,1,0:T(8,128)}, u32[]{:S(2)}) copy-start(f32[12,6,128]{2,1,0:T(8,128)} %particles_ref.1) | copy-start | bytes 110596
  1.4 0.7 copy-start.1
  2.1 0.7 copy-start.3
  3.4 6.8 %collective-permute-start.3 = (f32[48,128]{1,0:T(8,128)S(1)}, f32[48,128]{1,0:T(8,128)S(1)}, u32[]{:S(2)}, u32[]{:S(2)}) collective-permute-start(f32[48,128]{1,0:T(8,128)S(1)} %get-tuple-element.20.refs_0_.own_ref), channel_id=1, source_target_pairs={{0,1},{1,0},{2,3},{3,2},{4,5},{5,4},{6,7},{7,6},{8,9},{9,8},{10,11... | collective-permute-start | bytes 73736 | tf_op jit(solution)/shard_map/ppermute | solution.py:37
  3.5 19.1 %collective-permute-start.2 = (f32[48,128]{1,0:T(8,128)S(1)}, f32[48,128]{1,0:T(8,128)S(1)}, u32[]{:S(2)}, u32[]{:S(2)}) collective-permute-start(f32[48,128]{1,0:T(8,128)S(1)} %get-tuple-element.20.refs_0_.own_ref), channel_id=1, source_target_pairs={{0,30},{1,31},{2,0},{3,1},{4,2},{5,3},{6,4},{7,5},{8,6},{9,7},{10,... | collective-permute-start | bytes 73736 | tf_op jit(solution)/shard_map/ppermute | solution.py:27
  10.1 12.4 %collective-permute-start.1 = (f32[48,128]{1,0:T(8,128)S(1)}, f32[48,128]{1,0:T(8,128)S(1)}, u32[]{:S(2)}, u32[]{:S(2)}) collective-permute-start(f32[48,128]{1,0:T(8,128)S(1)} %get-tuple-element.20.refs_0_.own_ref), channel_id=1, source_target_pairs={{1,2},{2,1},{3,4},{4,3},{5,6},{6,5},{7,8},{8,7},{9,10},{10,9},{11,... | collective-permute-start | bytes 73736 | tf_op jit(solution)/shard_map/ppermute | solution.py:37
  10.1 12.4 %collective-permute-start = (f32[48,128]{1,0:T(8,128)S(1)}, f32[48,128]{1,0:T(8,128)S(1)}, u32[]{:S(2)}, u32[]{:S(2)}) collective-permute-start(f32[48,128]{1,0:T(8,128)S(1)} %get-tuple-element.20.refs_0_.own_ref), channel_id=1, source_target_pairs={{0,2},{1,3},{2,4},{3,5},{4,6},{5,7},{6,8},{7,9},{8,10},{9,11},{10,... | collective-permute-start | bytes 73736 | tf_op jit(solution)/shard_map/ppermute | solution.py:27
  35.0 6.1 %collective-permute-start.7 = (f32[54,128]{1,0:T(8,128)S(1)}, f32[54,128]{1,0:T(8,128)S(1)}, u32[]{:S(2)}, u32[]{:S(2)}) collective-permute-start(f32[54,128]{1,0:T(8,128)S(1)} %get-tuple-element.27), channel_id=1, source_target_pairs={{0,1},{1,0},{2,3},{3,2},{4,5},{5,4},{6,7},{7,6},{8,9},{9,8},{10,11... | collective-permute-start | bytes 82952 | tf_op jit(solution)/shard_map/ppermute | solution.py:37
  37.2 15.2 %collective-permute-start.6 = (f32[36,128]{1,0:T(8,128)S(1)}, f32[36,128]{1,0:T(8,128)S(1)}, u32[]{:S(2)}, u32[]{:S(2)}) collective-permute-start(f32[36,128]{1,0:T(8,128)S(1)} %get-tuple-element.25.refs_0_.own_ref), channel_id=1, source_target_pairs={{0,30},{1,31},{2,0},{3,1},{4,2},{5,3},{6,4},{7,5},{8,6},{9,7},{10,... | collective-permute-start | bytes 55304 | tf_op jit(solution)/shard_map/ppermute | solution.py:27
  41.1 11.4 %collective-permute-start.4 = (f32[36,128]{1,0:T(8,128)S(1)}, f32[36,128]{1,0:T(8,128)S(1)}, u32[]{:S(2)}, u32[]{:S(2)}) collective-permute-start(f32[36,128]{1,0:T(8,128)S(1)} %get-tuple-element.25.refs_0_.own_ref), channel_id=1, source_target_pairs={{0,2},{1,3},{2,4},{3,5},{4,6},{5,7},{6,8},{7,9},{8,10},{9,11},{10,... | collective-permute-start | bytes 55304 | tf_op jit(solution)/shard_map/ppermute | solution.py:27
  41.1 11.4 %collective-permute-start.5 = (f32[54,128]{1,0:T(8,128)S(1)}, f32[54,128]{1,0:T(8,128)S(1)}, u32[]{:S(2)}, u32[]{:S(2)}) collective-permute-start(f32[54,128]{1,0:T(8,128)S(1)} %get-tuple-element.26), channel_id=1, source_target_pairs={{1,2},{2,1},{3,4},{4,3},{5,6},{6,5},{7,8},{8,7},{9,10},{10,9},{11,... | collective-permute-start | bytes 82952 | tf_op jit(solution)/shard_map/ppermute | solution.py:37
  52.5 0.7 copy-start.2
  65.7 7.5 %collective-permute-start.8 = (f32[36,128]{1,0:T(8,128)S(1)}, f32[36,128]{1,0:T(8,128)S(1)}, u32[]{:S(2)}, u32[]{:S(2)}) collective-permute-start(f32[36,128]{1,0:T(8,128)S(1)} %get-tuple-element.35), channel_id=1, source_target_pairs={{0,1},{1,0},{2,3},{3,2},{4,5},{5,4},{6,7},{7,6},{8,9},{9,8},{10,11... | collective-permute-start | bytes 55304 | tf_op jit(solution)/shard_map/ppermute | solution.py:37
  71.3 5.1 %collective-permute-start.9 = (f32[36,128]{1,0:T(8,128)S(1)}, f32[36,128]{1,0:T(8,128)S(1)}, u32[]{:S(2)}, u32[]{:S(2)}) collective-permute-start(f32[36,128]{1,0:T(8,128)S(1)} %get-tuple-element.37), channel_id=1, source_target_pairs={{1,2},{2,1},{3,4},{4,3},{5,6},{6,5},{7,8},{8,7},{9,10},{10,9},{11,... | collective-permute-start | bytes 55304 | tf_op jit(solution)/shard_map/ppermute | solution.py:37

commit v8 on v5

--- a/solution.py
+++ b/solution.py
@@ -14,6 +14,7 @@
 time_step = 0.5
 reach = 2
 chunk = 4
+units = 4
 feature_rows = 32
 far_norm = 1e36
 lanes = 128
@@ -162,7 +163,7 @@
     target_ref[tiles] = target_ref[0]
 
 
-def accumulate(tiles, lists_ref, source_ref, target_ref, moment_ref, buffers, total_ref):
+def accumulate(tiles, lists_ref, source_ref, target_ref, moment_ref, total_ref):
     chunk_counts = [(lists_ref[tiles + 1, tile] + chunk - 1) // chunk for tile in range(tiles)]
     chunk_total = functools.reduce(lambda left, right: left + right, [jnp.maximum(count, 1) for count in chunk_counts])
 
@@ -170,26 +171,24 @@
         more = (part + 1) * chunk < lists_ref[tiles + 1, tile]
         return (jnp.where(more, tile, jnp.minimum(tile + 1, tiles)), jnp.where(more, part + 1, 0))
 
-    def distances(tile, part, distance_ref):
-        for pair in range(chunk // 2):
-            sources = [lists_ref[tile, part * chunk + 2 * pair + entry] for entry in range(2)]
-            distance_ref[pair] = jnp.dot(
-                target_ref[tile],
-                jnp.concatenate([source_ref[source] for source in sources], axis=1),
-                preferred_element_type=jnp.float32,
-            )
-
-    def kernels(tile, part, distance_ref):
-        places = []
-        for entry in range(chunk):
-            source = lists_ref[tile, part * chunk + entry]
-            places.append([jnp.broadcast_to(moment_ref[source, axis : axis + 1, :], (8, lanes)) for axis in range(3)])
+    def sources_of(tile, part):
+        return [lists_ref[tile, part * chunk + entry] for entry in range(chunk)]
+
+    def distances(tile, sources):
+        target = target_ref[tile]
+        features = [source_ref[source] for source in sources]
+        return [
+            jnp.dot(target, jnp.concatenate(features[first : first + 2], axis=1), preferred_element_type=jnp.float32)
+            for first in range(0, chunk, 2)
+        ]
+
+    def kernels(tile, places, squares):
         for first in range(0, lanes, 8):
             strip = slice(first, first + 8)
             sums = [total_ref[tile, row, strip, :] for row in range(4)]
             for entry in range(chunk):
                 column = (entry % 2) * lanes
-                inverse = lax.rsqrt(distance_ref[entry // 2, strip, column : column + lanes])
+                inverse = lax.rsqrt(squares[entry // 2][strip, column : column + lanes])
                 kernel = inverse * inverse * inverse
                 for axis in range(3):
                     sums[axis] = sums[axis] + kernel * places[entry][axis]
@@ -199,17 +198,21 @@
 
     def step(_, carry):
         tile, part = carry
-        tile_1, part_1 = following(tile, part)
-        tile_2, part_2 = following(tile_1, part_1)
-        kernels(tile, part, buffers[0])
-        distances(tile_1, part_1, buffers[1])
-        kernels(tile_1, part_1, buffers[1])
-        distances(tile_2, part_2, buffers[0])
-        return (tile_2, part_2)
+        work = []
+        for _ in range(units):
+            sources = sources_of(tile, part)
+            places = [
+                [jnp.broadcast_to(moment_ref[source, axis : axis + 1, :], (8, lanes)) for axis in range(3)]
+                for source in sources
+            ]
+            work.append((tile, places, distances(tile, sources)))
+            tile, part = following(tile, part)
+        for item in work:
+            kernels(*item)
+        return (tile, part)
 
     zero = jnp.int32(0)
-    distances(zero, zero, buffers[0])
-    lax.fori_loop(0, (chunk_total + 1) // 2, step, (zero, zero))
+    lax.fori_loop(0, (chunk_total + units - 1) // units, step, (zero, zero))
 
 
 def advance(middle, place_own, speed_own, weight_own, total_ref, sums_ref):
@@ -278,13 +281,13 @@
         own_ref, sibling_ref, total_ref, target_ref, lists_ref, weight_ref, *scratch = refs
     else:
         own_ref, sibling_ref, lists_ref, weight_ref, total_ref, target_ref, *scratch = refs
-    *tools, buffer_0, buffer_1 = scratch
+    tools = scratch
     tiles = own_ref.shape[0] // tools[0].shape[0]
     middle, copy = prepare(first, True, listed, own_ref, (own_ref, sibling_ref), lists_ref, weight_ref, tools)
     build_targets([part_of(own_ref, tiles, axis) for axis in range(3)], middle, tools[3], target_ref)
     total_ref[...] = jnp.zeros(total_ref.shape, jnp.float32)
     copy.wait()
-    accumulate(tiles, tools[1], tools[5], target_ref, tools[4], (buffer_0, buffer_1), total_ref)
+    accumulate(tiles, tools[1], tools[5], target_ref, tools[4], total_ref)
 
 
 def halves(speed, even, half):
@@ -296,12 +299,12 @@
     listed, own_ref, below, beside, above, total_in, target_ref, weight_own_ref, speed_ref, *refs
 ):
     total_ref, lists_ref, weight_ref, place_out, speed_out, sibling_out, beside_out, *scratch = refs
-    *tools, buffer_0, buffer_1, sums_ref = scratch
+    *tools, sums_ref = scratch
     tiles = own_ref.shape[0] // tools[0].shape[0]
     half = tiles // 2
     middle, copy = prepare(True, False, listed, own_ref, (below, beside, above), lists_ref, weight_ref, tools)
     copy.wait()
-    accumulate(tiles, tools[1], tools[5], target_ref, tools[4], (buffer_0, buffer_1), total_ref)
+    accumulate(tiles, tools[1], tools[5], target_ref, tools[4], total_ref)
     places, speeds = advance(
         middle,
         [part_of(own_ref, tiles, axis) for axis in range(3)],
@@ -342,12 +345,12 @@
     out_ref,
     *scratch
 ):
-    *tools, buffer_0, buffer_1, sums_ref, pool_ref = scratch
+    *tools, sums_ref, pool_ref = scratch
     tiles = own_ref.shape[0] // 3
     half = tiles // 2
     middle, copy = prepare(False, False, None, own_ref, (below, beside, above), lists_ref, weight_ref, tools)
     copy.wait()
-    accumulate(tiles, tools[1], tools[5], target_ref, tools[4], (buffer_0, buffer_1), total_ref)
+    accumulate(tiles, tools[1], tools[5], target_ref, tools[4], total_ref)
     place_own = [part_of(own_ref, tiles, axis) for axis in range(3)]
     speed_own = [part_of(speed_ref, tiles, axis) for axis in range(3)]
     places, speeds = advance(middle, place_own, speed_own, weight_own_ref[:tiles, :], total_ref, sums_ref)
@@ -440,8 +443,6 @@
             pltpu.VMEM((rows, feature_rows, lanes), jnp.float32),
             pltpu.VMEM((rows, 8, lanes), jnp.float32),
             pltpu.VMEM((rows, feature_rows, lanes), jnp.bfloat16),
-            pltpu.VMEM((chunk // 2, lanes, 2 * lanes), jnp.float32),
-            pltpu.VMEM((chunk // 2, lanes, 2 * lanes), jnp.float32),
         ]
 
     packed, speed = pl.pallas_call(

time: 74.3 us -> 67 us (0.902)
  Pallas kernels: 47.9 us -> 40.5 us
    pallas_call x5, Pallas kernels: 47.4 us -> 39.9 us  [call(): pl.pallas_call(kernel, out_shape=outs, in_specs=[kind for kind, _ in ins]...]
  transfers between devices with their start and end apart: 10 -> 10, of which waited for: 1 -> 1; matrix products, arithmetic and copies ran while one was open for 0% -> 0% of each run, Pallas kernels for 28% -> 27%
where the time goes in v8:
time: 67 us; the launch traced here: 66.8 us
  Pallas kernels  40.5 us (60%)
  starting transfers between devices  20.2 us (30%)
  waiting for transfers between devices  3.19 us (5%)
  local copies, waits for them, and re-layouts  2.15 us (3%)
  between operations  0.77 us (1%)
    pallas_call x5, Pallas kernels, call(): pl.pallas_call(kernel, out_shape=outs, in_specs=[kind for kind, _ in ins]...  39.9 us
    ppermute x4, starting transfers between devices, shifted(): return lax.ppermute(value, AXES, pairs)  10.5 us
    ppermute x6, starting transfers between devices, swapped(): return lax.ppermute(value, AXES, pairs)  9.71 us
    ppermute x6, waiting for transfers between devices, swapped(): return lax.ppermute(value, AXES, pairs)  3.18 us
    unnamed x8, local copies, waits for them, and re-layouts  2.15 us
  transfers between devices with their start and end apart: 10, of which 1 were waited for; matrix products, arithmetic and copies ran while one was open for 0% of the time, Pallas kernels for 27%

profile of v8, /device:TPU:1, one launch (start us, length us, event | category | flops | bytes accessed | tf_op | source)
XLA Modules:
  0.0 66.8 jit_solution(2670775568350398439)
XLA Ops:
  0.6 0.0 copy-start
  0.6 0.8 %copy-done = f32[12,6,128]{2,1,0:T(8,128)S(1)} copy-done((f32[12,6,128]{2,1,0:T(8,128)S(1)}, f32[12,6,128]{2,1,0:T(8,128)}, u32[]{:S(2)}) %copy-start) | copy-done | bytes 36888
  1.4 0.0 copy-start.1
  1.4 0.7 %copy-done.1 = s32[12,16]{1,0:T(8,128)S(1)} copy-done((s32[12,16]{1,0:T(8,128)S(1)}, s32[12,16]{1,0:T(8,128)}, u32[]{:S(2)}) %copy-start.1) | copy-done | bytes 792
  2.1 0.0 copy-start.3
  2.1 0.7 copy-done.3
  2.8 0.6 pack.1
  3.4 0.1 collective-permute-start.3
  3.5 6.7 %collective-permute-start.2 = (f32[48,128]{1,0:T(8,128)S(1)}, f32[48,128]{1,0:T(8,128)S(1)}, u32[]{:S(2)}, u32[]{:S(2)}) collective-permute-start(f32[48,128]{1,0:T(8,128)S(1)} %get-tuple-element.20.refs_0_.own_ref), channel_id=1, source_target_pairs={{0,30},{1,31},{2,0},{3,1},{4,2},{5,3},{6,4},{7,5},{8,6},{9,7},{10,... | collective-permute-start | bytes 73736 | tf_op jit(solution)/shard_map/ppermute | solution.py:27
  10.1 0.0 collective-permute-start.1
  10.1 0.0 collective-permute-start
  10.1 0.0 collective-permute-done.3.refs_1_
  10.1 9.5 %first_near.1 = (f32[13,4,128,128]{3,2,1,0:T(8,128)S(1)}, bf16[13,128,32]{2,1,0:T(8,128)(2,1)S(1)}, s32[16,128]{1,0:T(8,128)S(1)}, f32[32,128]{1,0:T(8,128)S(1)}) custom-call(f32[48,128]{1,0:T(8,128)S(1)} %get-tuple-element.20.refs_0_.own_ref, f32[48,128]{1,0:T(8,128)S(1)} %collective-permute-done.3.refs_1_), custom_call_target="tpu_custom_call" | custom-call | flops 4294967296 | bytes 1048576 | tf_op jit(solution)/shard_map/first_near/pallas_call | solution.py:426
  19.6 0.0 collective-permute-done.2.above
  19.6 0.0 collective-permute-done.1.beside
  19.6 0.0 collective-permute-done.below
  19.7 10.3 %first_far.1 = (f32[13,4,128,128]{3,2,1,0:T(8,128)S(1)}, s32[16,128]{1,0:T(8,128)S(1)}, f32[40,128]{1,0:T(8,128)S(1)}, f32[36,128]{1,0:T(8,128)S(1)}, f32[36,128...) custom-call(f32[48,128]{1,0:T(8,128)S(1)} %get-tuple-element.20.refs_0_.own_ref,, ...), custom_call_target="tpu_custom_call", output_to_operand_aliasing={{0}: (4, {})} | custom-call | flops 4294967296 | bytes 1048576 | tf_op jit(solution)/shard_map/first_far/pallas_call | solution.py:426
  29.9 2.2 %collective-permute-start.7 = (f32[54,128]{1,0:T(8,128)S(1)}, f32[54,128]{1,0:T(8,128)S(1)}, u32[]{:S(2)}, u32[]{:S(2)}) collective-permute-start(f32[54,128]{1,0:T(8,128)S(1)} %get-tuple-element.27), channel_id=1, source_target_pairs={{0,1},{1,0},{2,3},{3,2},{4,5},{5,4},{6,7},{7,6},{8,9},{9,8},{10,11... | collective-permute-start | bytes 82952 | tf_op jit(solution)/shard_map/ppermute | solution.py:37
  32.1 3.8 %collective-permute-start.6 = (f32[36,128]{1,0:T(8,128)S(1)}, f32[36,128]{1,0:T(8,128)S(1)}, u32[]{:S(2)}, u32[]{:S(2)}) collective-permute-start(f32[36,128]{1,0:T(8,128)S(1)} %get-tuple-element.25.refs_0_.own_ref), channel_id=1, source_target_pairs={{0,30},{1,31},{2,0},{3,1},{4,2},{5,3},{6,4},{7,5},{8,6},{9,7},{10,... | collective-permute-start | bytes 55304 | tf_op jit(solution)/shard_map/ppermute | solution.py:27
  36.0 0.0 collective-permute-start.4
  36.0 0.0 collective-permute-start.5
  36.0 0.0 collective-permute-done.7.refs_1_.sibling_ref
  36.0 0.0 copy-start.2
  36.0 8.6 %second_near.1 = (f32[13,4,128,128]{3,2,1,0:T(8,128)S(1)}, bf16[13,128,32]{2,1,0:T(8,128)(2,1)S(1)}) custom-call(f32[36,128]{1,0:T(8,128)S(1)} %get-tuple-element.25.refs_0_.own_ref, f32[54,128]{1,0:T(8,128)S(1)} %collective-permute-done.7.refs_1_.sibling_ref, s32[16,128]{1,0:T(8,128)S(1)} %get-tuple-element.28.refs_2_, ...), custom_call_target="tpu_custom_call" | custom-call | flops 4294967296 | bytes 1048576 | tf_op jit(solution)/shard_map/second_near/pallas_call | solution.py:426
  44.6 0.0 collective-permute-done.6.above
  44.6 0.0 collective-permute-done.4.below
  44.6 0.0 collective-permute-done.5.beside
  44.7 0.0 copy-done.2
  44.7 10.3 %second_far.1 = (f32[13,4,128,128]{3,2,1,0:T(8,128)S(1)}, f32[6,12,128]{2,1,0:T(8,128)S(1)}, f32[36,128]{1,0:T(8,128)S(1)}, f32[36,128]{1,0:T(8,128)S(1)}, f32[6,24,128]{2,1,0:T(8,128)}) custom-call(s32[2,32]{1,0:T(2,128)S(1)} %copy-done.2, f32[36,128]{1,0:T(8,128)S(1)} %get-tuple-element.25.refs_0_.own_ref, ...), custom_call_target="tpu_custom_call", output_to_operand_aliasing={{0}: (5, {})} | custom-call | flops 4294967296 | bytes 1048576 | tf_op jit(solution)/shard_map/second_far/pallas_call | solution.py:426
  55.0 5.5 %collective-permute-start.8 = (f32[36,128]{1,0:T(8,128)S(1)}, f32[36,128]{1,0:T(8,128)S(1)}, u32[]{:S(2)}, u32[]{:S(2)}) collective-permute-start(f32[36,128]{1,0:T(8,128)S(1)} %get-tuple-element.35), channel_id=1, source_target_pairs={{0,1},{1,0},{2,3},{3,2},{4,5},{5,4},{6,7},{7,6},{8,9},{9,8},{10,11... | collective-permute-start | bytes 55304 | tf_op jit(solution)/shard_map/ppermute | solution.py:37
  60.5 1.9 %collective-permute-start.9 = (f32[36,128]{1,0:T(8,128)S(1)}, f32[36,128]{1,0:T(8,128)S(1)}, u32[]{:S(2)}, u32[]{:S(2)}) collective-permute-start(f32[36,128]{1,0:T(8,128)S(1)} %get-tuple-element.37), channel_id=1, source_target_pairs={{1,2},{2,1},{3,4},{4,3},{5,6},{6,5},{7,8},{8,7},{9,10},{10,9},{11,... | collective-permute-start | bytes 55304 | tf_op jit(solution)/shard_map/ppermute | solution.py:37
  62.4 0.0 collective-permute-done.8.sibling_ref
  62.4 3.2 %collective-permute-done.9.beside_ref = f32[36,128]{1,0:T(8,128)S(1)} collective-permute-done((f32[36,128]{1,0:T(8,128)S(1)}, f32[36,128]{1,0:T(8,128)S(1)}, u32[]{:S(2)}, u32[]{:S(2)}) %collective-permute-start.9) | collective-permute-done | bytes 18464 | tf_op jit(solution)/shard_map/ppermute | solution.py:37
  65.6 1.2 %place.1 = f32[6,24,128]{2,1,0:T(8,128)} custom-call(s32[2,32]{1,0:T(2,128)S(1)} %copy-done.2, f32[36,128]{1,0:T(8,128)S(1)} %collective-permute-done.8.sibling_ref, f32[6,12,128]{2,1,0:T(8,128)S(1)} %get-tuple-element.36.own_ref, f32[36,128]{1,0:T(8,128)S(1)} %collective-permute-done.9.beside_ref), custom_call_target="tpu_custom_call" | custom-call | bytes 1048576 | tf_op jit(solution)/shard_map/place/pallas_call | solution.py:426
Async XLA Ops:
  0.6 0.8 %copy-start = (f32[12,6,128]{2,1,0:T(8,128)S(1)}, f32[12,6,128]{2,1,0:T(8,128)}, u32[]{:S(2)}) copy-start(f32[12,6,128]{2,1,0:T(8,128)} %particles_ref.1) | copy-start | bytes 110596
  1.4 0.7 %copy-start.1 = (s32[12,16]{1,0:T(8,128)S(1)}, s32[12,16]{1,0:T(8,128)}, u32[]{:S(2)}) copy-start(s32[12,16]{1,0:T(8,128)} %neighbours_ref.1) | copy-start | bytes 2308
  2.1 0.7 copy-start.3
  3.4 6.8 %collective-permute-start.3 = (f32[48,128]{1,0:T(8,128)S(1)}, f32[48,128]{1,0:T(8,128)S(1)}, u32[]{:S(2)}, u32[]{:S(2)}) collective-permute-start(f32[48,128]{1,0:T(8,128)S(1)} %get-tuple-element.20.refs_0_.own_ref), channel_id=1, source_target_pairs={{0,1},{1,0},{2,3},{3,2},{4,5},{5,4},{6,7},{7,6},{8,9},{9,8},{10,11... | collective-permute-start | bytes 73736 | tf_op jit(solution)/shard_map/ppermute | solution.py:37
  3.5 16.1 %collective-permute-start.2 = (f32[48,128]{1,0:T(8,128)S(1)}, f32[48,128]{1,0:T(8,128)S(1)}, u32[]{:S(2)}, u32[]{:S(2)}) collective-permute-start(f32[48,128]{1,0:T(8,128)S(1)} %get-tuple-element.20.refs_0_.own_ref), channel_id=1, source_target_pairs={{0,30},{1,31},{2,0},{3,1},{4,2},{5,3},{6,4},{7,5},{8,6},{9,7},{10,... | collective-permute-start | bytes 73736 | tf_op jit(solution)/shard_map/ppermute | solution.py:27
  10.1 9.5 %collective-permute-start.1 = (f32[48,128]{1,0:T(8,128)S(1)}, f32[48,128]{1,0:T(8,128)S(1)}, u32[]{:S(2)}, u32[]{:S(2)}) collective-permute-start(f32[48,128]{1,0:T(8,128)S(1)} %get-tuple-element.20.refs_0_.own_ref), channel_id=1, source_target_pairs={{1,2},{2,1},{3,4},{4,3},{5,6},{6,5},{7,8},{8,7},{9,10},{10,9},{11,... | collective-permute-start | bytes 73736 | tf_op jit(solution)/shard_map/ppermute | solution.py:37
  10.1 9.5 %collective-permute-start = (f32[48,128]{1,0:T(8,128)S(1)}, f32[48,128]{1,0:T(8,128)S(1)}, u32[]{:S(2)}, u32[]{:S(2)}) collective-permute-start(f32[48,128]{1,0:T(8,128)S(1)} %get-tuple-element.20.refs_0_.own_ref), channel_id=1, source_target_pairs={{0,2},{1,3},{2,4},{3,5},{4,6},{5,7},{6,8},{7,9},{8,10},{9,11},{10,... | collective-permute-start | bytes 73736 | tf_op jit(solution)/shard_map/ppermute | solution.py:27
  29.9 6.0 %collective-permute-start.7 = (f32[54,128]{1,0:T(8,128)S(1)}, f32[54,128]{1,0:T(8,128)S(1)}, u32[]{:S(2)}, u32[]{:S(2)}) collective-permute-start(f32[54,128]{1,0:T(8,128)S(1)} %get-tuple-element.27), channel_id=1, source_target_pairs={{0,1},{1,0},{2,3},{3,2},{4,5},{5,4},{6,7},{7,6},{8,9},{9,8},{10,11... | collective-permute-start | bytes 82952 | tf_op jit(solution)/shard_map/ppermute | solution.py:37
  32.1 12.5 %collective-permute-start.6 = (f32[36,128]{1,0:T(8,128)S(1)}, f32[36,128]{1,0:T(8,128)S(1)}, u32[]{:S(2)}, u32[]{:S(2)}) collective-permute-start(f32[36,128]{1,0:T(8,128)S(1)} %get-tuple-element.25.refs_0_.own_ref), channel_id=1, source_target_pairs={{0,30},{1,31},{2,0},{3,1},{4,2},{5,3},{6,4},{7,5},{8,6},{9,7},{10,... | collective-permute-start | bytes 55304 | tf_op jit(solution)/shard_map/ppermute | solution.py:27
  36.0 8.7 %collective-permute-start.4 = (f32[36,128]{1,0:T(8,128)S(1)}, f32[36,128]{1,0:T(8,128)S(1)}, u32[]{:S(2)}, u32[]{:S(2)}) collective-permute-start(f32[36,128]{1,0:T(8,128)S(1)} %get-tuple-element.25.refs_0_.own_ref), channel_id=1, source_target_pairs={{0,2},{1,3},{2,4},{3,5},{4,6},{5,7},{6,8},{7,9},{8,10},{9,11},{10,... | collective-permute-start | bytes 55304 | tf_op jit(solution)/shard_map/ppermute | solution.py:27
  36.0 8.7 %collective-permute-start.5 = (f32[54,128]{1,0:T(8,128)S(1)}, f32[54,128]{1,0:T(8,128)S(1)}, u32[]{:S(2)}, u32[]{:S(2)}) collective-permute-start(f32[54,128]{1,0:T(8,128)S(1)} %get-tuple-element.26), channel_id=1, source_target_pairs={{1,2},{2,1},{3,4},{4,3},{5,6},{6,5},{7,8},{8,7},{9,10},{10,9},{11,... | collective-permute-start | bytes 82952 | tf_op jit(solution)/shard_map/ppermute | solution.py:37
  36.0 8.7 %copy-start.2 = (s32[2,32]{1,0:T(2,128)S(1)}, s32[2,32]{1,0:T(2,128)}, u32[]{:S(2)}) copy-start(s32[2,32]{1,0:T(2,128)} %cuts_ref.3) | copy-start | bytes 772
  55.0 7.4 %collective-permute-start.8 = (f32[36,128]{1,0:T(8,128)S(1)}, f32[36,128]{1,0:T(8,128)S(1)}, u32[]{:S(2)}, u32[]{:S(2)}) collective-permute-start(f32[36,128]{1,0:T(8,128)S(1)} %get-tuple-element.35), channel_id=1, source_target_pairs={{0,1},{1,0},{2,3},{3,2},{4,5},{5,4},{6,7},{7,6},{8,9},{9,8},{10,11... | collective-permute-start | bytes 55304 | tf_op jit(solution)/shard_map/ppermute | solution.py:37
  60.5 5.1 %collective-permute-start.9 = (f32[36,128]{1,0:T(8,128)S(1)}, f32[36,128]{1,0:T(8,128)S(1)}, u32[]{:S(2)}, u32[]{:S(2)}) collective-permute-start(f32[36,128]{1,0:T(8,128)S(1)} %get-tuple-element.37), channel_id=1, source_target_pairs={{1,2},{2,1},{3,4},{4,3},{5,6},{6,5},{7,8},{8,7},{9,10},{10,9},{11,... | collective-permute-start | bytes 55304 | tf_op jit(solution)/shard_map/ppermute | solution.py:37

commit v9 on v6

--- a/solution.py
+++ b/solution.py
@@ -14,6 +14,7 @@
 time_step = 0.5
 reach = 2
 chunk = 4
+units = 4
 feature_rows = 32
 moment_rows = 16
 far_norm = 1e36
@@ -178,56 +179,48 @@
     target_ref[tiles] = target_ref[0]
 
 
-def accumulate(tiles, lists_ref, source_ref, target_ref, moments_ref, buffers, total_ref):
+def accumulate(tiles, lists_ref, source_ref, target_ref, moments_ref, total_ref):
     chunk_counts = [(lists_ref[tiles + 1, tile] + chunk - 1) // chunk for tile in range(tiles)]
     chunk_total = functools.reduce(lambda left, right: left + right, [jnp.maximum(count, 1) for count in chunk_counts])
-    distance_refs, kernel_refs = (buffers[:2], buffers[2:])
 
     def following(tile, part):
         more = (part + 1) * chunk < lists_ref[tiles + 1, tile]
         return (jnp.where(more, tile, jnp.minimum(tile + 1, tiles)), jnp.where(more, part + 1, 0))
 
-    def sources_of(tile, part):
-        return [lists_ref[tile, part * chunk + entry] for entry in range(chunk)]
-
-    def distances(tile, part, distance_ref):
-        features = [source_ref[source] for source in sources_of(tile, part)]
+    def distances(tile, sources):
+        features = [source_ref[source] for source in sources]
         pairs = [jnp.concatenate(features[first : first + 2], axis=1) for first in range(0, chunk, 2)]
-        distance_ref[...] = jnp.dot(target_ref[tile], jnp.concatenate(pairs, axis=0), preferred_element_type=jnp.float32)
-
-    def kernels(distance_ref, kernel_ref):
+        return jnp.dot(target_ref[tile], jnp.concatenate(pairs, axis=0), preferred_element_type=jnp.float32)
+
+    def sums(squares, moments):
+        total = None
         for pair in range(chunk // 2):
-            columns = slice(pair * 2 * lanes, (pair + 1) * 2 * lanes)
-            for first in range(0, lanes, 16):
-                inverse = lax.rsqrt(distance_ref[pair * lanes + first : pair * lanes + first + 16, :])
-                kernel = inverse * inverse * inverse
-                high = kernel.astype(jnp.bfloat16)
-                kernel_ref[first : first + 16, columns] = high
-                kernel_ref[lanes + first : lanes + first + 16, columns] = (kernel - high.astype(jnp.float32)).astype(
-                    jnp.bfloat16
-                )
-
-    def sums(tile, part, kernel_ref):
-        moments = jnp.concatenate([moments_ref[source] for source in sources_of(tile, part)], axis=0)
-        both = jnp.dot(kernel_ref[...], moments, preferred_element_type=jnp.float32)
-        total_ref[tile] += both[:lanes] + both[lanes:]
+            inverse = lax.rsqrt(squares[pair * lanes : (pair + 1) * lanes])
+            kernel = inverse * inverse * inverse
+            high = kernel.astype(jnp.bfloat16)
+            low = (kernel - high.astype(jnp.float32)).astype(jnp.bfloat16)
+            both = jnp.dot(
+                jnp.concatenate([high, low], axis=0),
+                jnp.concatenate(moments[2 * pair : 2 * pair + 2], axis=0),
+                preferred_element_type=jnp.float32,
+            )
+            part = both[:lanes] + both[lanes:]
+            total = part if total is None else total + part
+        return total
 
     def step(_, carry):
-        (tile_0, part_0), (tile_1, part_1) = carry
-        tile_2, part_2 = following(tile_1, part_1)
-        tile_3, part_3 = following(tile_2, part_2)
-        sums(tile_0, part_0, kernel_refs[1])
-        kernels(distance_refs[0], kernel_refs[0])
-        distances(tile_2, part_2, distance_refs[1])
-        sums(tile_1, part_1, kernel_refs[0])
-        kernels(distance_refs[1], kernel_refs[1])
-        distances(tile_3, part_3, distance_refs[0])
-        return ((tile_2, part_2), (tile_3, part_3))
+        tile, part = carry
+        work = []
+        for _ in range(units):
+            sources = [lists_ref[tile, part * chunk + entry] for entry in range(chunk)]
+            work.append((tile, distances(tile, sources), [moments_ref[source] for source in sources]))
+            tile, part = following(tile, part)
+        for item, total in [(item, sums(squares, moments)) for item, squares, moments in work]:
+            total_ref[item] += total
+        return (tile, part)
 
     zero = jnp.int32(0)
-    spare = jnp.int32(tiles)
-    distances(zero, zero, distance_refs[0])
-    lax.fori_loop(0, (chunk_total + 2) // 2, step, ((spare, zero), (zero, zero)))
+    lax.fori_loop(0, (chunk_total + units - 1) // units, step, (zero, zero))
 
 
 def advance(middle, place_own, speed_own, weight_own, total_ref, sums_ref):
@@ -300,13 +293,13 @@
         own_ref, sibling_ref, total_ref, target_ref, lists_ref, weight_ref, *scratch = refs
     else:
         own_ref, sibling_ref, lists_ref, weight_ref, total_ref, target_ref, *scratch = refs
-    tools, buffers = (scratch[:7], scratch[7:])
+    tools = scratch
     tiles = own_ref.shape[0] // tools[0].shape[0]
     middle, copy = prepare(first, True, listed, own_ref, (own_ref, sibling_ref), lists_ref, weight_ref, tools)
     build_targets([part_of(own_ref, tiles, axis) for axis in range(3)], middle, tools[3], target_ref)
     total_ref[...] = jnp.zeros(total_ref.shape, jnp.float32)
     copy.wait()
-    accumulate(tiles, tools[1], tools[5], target_ref, tools[6], buffers, total_ref)
+    accumulate(tiles, tools[1], tools[5], target_ref, tools[6], total_ref)
 
 
 def halves(speed, even, half):
@@ -318,13 +311,12 @@
     listed, own_ref, below, beside, above, total_in, target_ref, weight_own_ref, speed_ref, *refs
 ):
     total_ref, lists_ref, weight_ref, place_out, speed_out, sibling_out, beside_out, *scratch = refs
-    *rest, sums_ref = scratch
-    tools, buffers = (rest[:7], rest[7:])
+    *tools, sums_ref = scratch
     tiles = own_ref.shape[0] // tools[0].shape[0]
     half = tiles // 2
     middle, copy = prepare(True, False, listed, own_ref, (below, beside, above), lists_ref, weight_ref, tools)
     copy.wait()
-    accumulate(tiles, tools[1], tools[5], target_ref, tools[6], buffers, total_ref)
+    accumulate(tiles, tools[1], tools[5], target_ref, tools[6], total_ref)
     places, speeds = advance(
         middle,
         [part_of(own_ref, tiles, axis) for axis in range(3)],
@@ -365,13 +357,12 @@
     out_ref,
     *scratch
 ):
-    *rest, sums_ref, pool_ref = scratch
-    tools, buffers = (rest[:7], rest[7:])
+    *tools, sums_ref, pool_ref = scratch
     tiles = own_ref.shape[0] // 3
     half = tiles // 2
     middle, copy = prepare(False, False, None, own_ref, (below, beside, above), lists_ref, weight_ref, tools)
     copy.wait()
-    accumulate(tiles, tools[1], tools[5], target_ref, tools[6], buffers, total_ref)
+    accumulate(tiles, tools[1], tools[5], target_ref, tools[6], total_ref)
     place_own = [part_of(own_ref, tiles, axis) for axis in range(3)]
     speed_own = [part_of(speed_ref, tiles, axis) for axis in range(3)]
     places, speeds = advance(middle, place_own, speed_own, weight_own_ref[:tiles, :], total_ref, sums_ref)
@@ -465,10 +456,6 @@
             pltpu.VMEM((rows, moment_rows, lanes), jnp.float32),
             pltpu.VMEM((rows, feature_rows, lanes), jnp.bfloat16),
             pltpu.VMEM((rows, lanes, lanes), jnp.bfloat16),
-            pltpu.VMEM((chunk // 2 * lanes, 2 * lanes), jnp.float32),
-            pltpu.VMEM((chunk // 2 * lanes, 2 * lanes), jnp.float32),
-            pltpu.VMEM((2 * lanes, chunk * lanes), jnp.bfloat16),
-            pltpu.VMEM((2 * lanes, chunk * lanes), jnp.bfloat16),
         ]
 
     packed, speed = pl.pallas_call(

time: 78.8 us -> 70.9 us (0.90)
  Pallas kernels: 50.3 us -> 42.8 us
    pallas_call x5, Pallas kernels: 49.7 us -> 42.2 us  [call(): pl.pallas_call(kernel, out_shape=outs, in_specs=[kind for kind, _ in ins]...]
    ppermute x4, starting transfers between devices: 10.6 us -> 9.32 us  [shifted(): return lax.ppermute(value, AXES, pairs)]
    ppermute x6, starting transfers between devices: 11.2 us -> 12.1 us  [swapped(): return lax.ppermute(value, AXES, pairs)]
where the time goes in v9:
time: 70.9 us; the launch traced here: 71 us
  Pallas kernels  42.8 us (60%)
  starting transfers between devices  21.5 us (30%)
  waiting for transfers between devices  3.19 us (4%)
  local copies, waits for them, and re-layouts  2.82 us (4%)
  between operations  0.76 us (1%)
    pallas_call x5, Pallas kernels, call(): pl.pallas_call(kernel, out_shape=outs, in_specs=[kind for kind, _ in ins]...  42.2 us
    ppermute x6, starting transfers between devices, swapped(): return lax.ppermute(value, AXES, pairs)  12.1 us
    ppermute x4, starting transfers between devices, shifted(): return lax.ppermute(value, AXES, pairs)  9.32 us
    ppermute x6, waiting for transfers between devices, swapped(): return lax.ppermute(value, AXES, pairs)  3.18 us
    unnamed x8, local copies, waits for them, and re-layouts  2.82 us
  transfers between devices with their start and end apart: 10, of which 1 were waited for; matrix products, arithmetic and copies ran while one was open for 0% of the time, Pallas kernels for 29%

profile of v9, /device:TPU:1, one launch (start us, length us, event | category | flops | bytes accessed | tf_op | source)
XLA Modules:
  0.0 71.0 jit_solution(7346506374096854309)
XLA Ops:
  0.6 0.0 copy-start
  0.6 0.8 %copy-done = f32[12,6,128]{2,1,0:T(8,128)S(1)} copy-done((f32[12,6,128]{2,1,0:T(8,128)S(1)}, f32[12,6,128]{2,1,0:T(8,128)}, u32[]{:S(2)}) %copy-start) | copy-done | bytes 36888
  1.4 0.0 copy-start.1
  1.4 0.7 copy-done.1
  2.1 0.0 copy-start.3
  2.1 0.7 copy-done.3
  2.8 0.6 pack.1
  3.4 0.1 collective-permute-start.3
  3.5 6.7 %collective-permute-start.2 = (f32[48,128]{1,0:T(8,128)S(1)}, f32[48,128]{1,0:T(8,128)S(1)}, u32[]{:S(2)}, u32[]{:S(2)}) collective-permute-start(f32[48,128]{1,0:T(8,128)S(1)} %get-tuple-element.20.refs_0_.own_ref), channel_id=1, source_target_pairs={{0,30},{1,31},{2,0},{3,1},{4,2},{5,3},{6,4},{7,5},{8,6},{9,7},{10,... | collective-permute-start | bytes 73736 | tf_op jit(solution)/shard_map/ppermute | solution.py:28
  10.1 0.0 collective-permute-start.1
  10.1 0.0 collective-permute-start
  10.1 0.0 collective-permute-done.3.refs_1_
  10.1 10.6 %first_near.1 = (f32[13,128,128]{2,1,0:T(8,128)S(1)}, bf16[13,256,64]{2,1,0:T(8,128)(2,1)S(1)}, s32[16,128]{1,0:T(8,128)S(1)}, f32[32,128]{1,0:T(8,128)S(1)}) custom-call(f32[48,128]{1,0:T(8,128)S(1)} %get-tuple-element.20.refs_0_.own_ref, f32[48,128]{1,0:T(8,128)S(1)} %collective-permute-done.3.refs_1_), custom_call_target="tpu_custom_call" | custom-call | flops 4294967296 | bytes 1048576 | tf_op jit(solution)/shard_map/first_near/pallas_call | solution.py:438
  20.7 0.0 collective-permute-done.2.above
  20.7 0.0 collective-permute-done.1.beside
  20.7 0.0 collective-permute-done.below
  20.8 10.4 %first_far.1 = (f32[13,128,128]{2,1,0:T(8,128)S(1)}, s32[16,128]{1,0:T(8,128)S(1)}, f32[40,128]{1,0:T(8,128)S(1)}, f32[36,128]{1,0:T(8,128)S(1)}, f32[36,128]{1,...) custom-call(f32[48,128]{1,0:T(8,128)S(1)} %get-tuple-element.20.refs_0_.own_ref, ...), custom_call_target="tpu_custom_call", output_to_operand_aliasing={{0}: (4, {})} | custom-call | flops 4294967296 | bytes 1048576 | tf_op jit(solution)/shard_map/first_far/pallas_call | solution.py:438
  31.2 3.4 %collective-permute-start.7 = (f32[54,128]{1,0:T(8,128)S(1)}, f32[54,128]{1,0:T(8,128)S(1)}, u32[]{:S(2)}, u32[]{:S(2)}) collective-permute-start(f32[54,128]{1,0:T(8,128)S(1)} %get-tuple-element.27), channel_id=1, source_target_pairs={{0,1},{1,0},{2,3},{3,2},{4,5},{5,4},{6,7},{7,6},{8,9},{9,8},{10,11... | collective-permute-start | bytes 82952 | tf_op jit(solution)/shard_map/ppermute | solution.py:38
  34.6 2.7 %collective-permute-start.6 = (f32[36,128]{1,0:T(8,128)S(1)}, f32[36,128]{1,0:T(8,128)S(1)}, u32[]{:S(2)}, u32[]{:S(2)}) collective-permute-start(f32[36,128]{1,0:T(8,128)S(1)} %get-tuple-element.25.refs_0_.own_ref), channel_id=1, source_target_pairs={{0,30},{1,31},{2,0},{3,1},{4,2},{5,3},{6,4},{7,5},{8,6},{9,7},{10,... | collective-permute-start | bytes 55304 | tf_op jit(solution)/shard_map/ppermute | solution.py:28
  37.2 0.0 collective-permute-start.4
  37.2 0.0 collective-permute-start.5
  37.2 0.0 collective-permute-done.7.refs_1_.sibling_ref
  37.2 9.7 %second_near.1 = (f32[13,128,128]{2,1,0:T(8,128)S(1)}, bf16[13,256,64]{2,1,0:T(8,128)(2,1)S(1)}) custom-call(f32[36,128]{1,0:T(8,128)S(1)} %get-tuple-element.25.refs_0_.own_ref, f32[54,128]{1,0:T(8,128)S(1)} %collective-permute-done.7.refs_1_.sibling_ref, s32[16,128]{1,0:T(8,128)S(1)} %get-tuple-element.28.refs_2_, ...), custom_call_target="tpu_custom_call" | custom-call | flops 4294967296 | bytes 1048576 | tf_op jit(solution)/shard_map/second_near/pallas_call | solution.py:438
  46.9 0.0 collective-permute-done.6.above
  46.9 0.0 collective-permute-done.4.below
  46.9 0.0 collective-permute-done.5.beside
  46.9 0.0 copy-start.2
  47.0 0.7 copy-done.2
  47.6 10.3 %second_far.1 = (f32[13,128,128]{2,1,0:T(8,128)S(1)}, f32[6,12,128]{2,1,0:T(8,128)S(1)}, f32[36,128]{1,0:T(8,128)S(1)}, f32[36,128]{1,0:T(8,128)S(1)}, f32[6,24,128]{2,1,0:T(8,128)}) custom-call(s32[2,32]{1,0:T(2,128)S(1)} %copy-done.2, f32[36,128]{1,0:T(8,128)S(1)} %get-tuple-element.25.refs_0_.own_ref, ...), custom_call_target="tpu_custom_call", output_to_operand_aliasing={{0}: (5, {})} | custom-call | flops 4294967296 | bytes 1048576 | tf_op jit(solution)/shard_map/second_far/pallas_call | solution.py:438
  58.0 6.7 %collective-permute-start.8 = (f32[36,128]{1,0:T(8,128)S(1)}, f32[36,128]{1,0:T(8,128)S(1)}, u32[]{:S(2)}, u32[]{:S(2)}) collective-permute-start(f32[36,128]{1,0:T(8,128)S(1)} %get-tuple-element.35), channel_id=1, source_target_pairs={{0,1},{1,0},{2,3},{3,2},{4,5},{5,4},{6,7},{7,6},{8,9},{9,8},{10,11... | collective-permute-start | bytes 55304 | tf_op jit(solution)/shard_map/ppermute | solution.py:38
  64.7 1.9 %collective-permute-start.9 = (f32[36,128]{1,0:T(8,128)S(1)}, f32[36,128]{1,0:T(8,128)S(1)}, u32[]{:S(2)}, u32[]{:S(2)}) collective-permute-start(f32[36,128]{1,0:T(8,128)S(1)} %get-tuple-element.37), channel_id=1, source_target_pairs={{1,2},{2,1},{3,4},{4,3},{5,6},{6,5},{7,8},{8,7},{9,10},{10,9},{11,... | collective-permute-start | bytes 55304 | tf_op jit(solution)/shard_map/ppermute | solution.py:38
  66.6 0.0 collective-permute-done.8.sibling_ref
  66.6 3.2 %collective-permute-done.9.beside_ref = f32[36,128]{1,0:T(8,128)S(1)} collective-permute-done((f32[36,128]{1,0:T(8,128)S(1)}, f32[36,128]{1,0:T(8,128)S(1)}, u32[]{:S(2)}, u32[]{:S(2)}) %collective-permute-start.9) | collective-permute-done | bytes 18464 | tf_op jit(solution)/shard_map/ppermute | solution.py:38
  69.8 1.2 %place.1 = f32[6,24,128]{2,1,0:T(8,128)} custom-call(s32[2,32]{1,0:T(2,128)S(1)} %copy-done.2, f32[36,128]{1,0:T(8,128)S(1)} %collective-permute-done.8.sibling_ref, f32[6,12,128]{2,1,0:T(8,128)S(1)} %get-tuple-element.36.own_ref, f32[36,128]{1,0:T(8,128)S(1)} %collective-permute-done.9.beside_ref), custom_call_target="tpu_custom_call" | custom-call | bytes 1048576 | tf_op jit(solution)/shard_map/place/pallas_call | solution.py:438
Async XLA Ops:
  0.6 0.8 %copy-start = (f32[12,6,128]{2,1,0:T(8,128)S(1)}, f32[12,6,128]{2,1,0:T(8,128)}, u32[]{:S(2)}) copy-start(f32[12,6,128]{2,1,0:T(8,128)} %particles_ref.1) | copy-start | bytes 110596
  1.4 0.7 copy-start.1
  2.1 0.7 copy-start.3
  3.4 6.8 %collective-permute-start.3 = (f32[48,128]{1,0:T(8,128)S(1)}, f32[48,128]{1,0:T(8,128)S(1)}, u32[]{:S(2)}, u32[]{:S(2)}) collective-permute-start(f32[48,128]{1,0:T(8,128)S(1)} %get-tuple-element.20.refs_0_.own_ref), channel_id=1, source_target_pairs={{0,1},{1,0},{2,3},{3,2},{4,5},{5,4},{6,7},{7,6},{8,9},{9,8},{10,11... | collective-permute-start | bytes 73736 | tf_op jit(solution)/shard_map/ppermute | solution.py:38
  3.5 17.2 %collective-permute-start.2 = (f32[48,128]{1,0:T(8,128)S(1)}, f32[48,128]{1,0:T(8,128)S(1)}, u32[]{:S(2)}, u32[]{:S(2)}) collective-permute-start(f32[48,128]{1,0:T(8,128)S(1)} %get-tuple-element.20.refs_0_.own_ref), channel_id=1, source_target_pairs={{0,30},{1,31},{2,0},{3,1},{4,2},{5,3},{6,4},{7,5},{8,6},{9,7},{10,... | collective-permute-start | bytes 73736 | tf_op jit(solution)/shard_map/ppermute | solution.py:28
  10.1 10.6 %collective-permute-start.1 = (f32[48,128]{1,0:T(8,128)S(1)}, f32[48,128]{1,0:T(8,128)S(1)}, u32[]{:S(2)}, u32[]{:S(2)}) collective-permute-start(f32[48,128]{1,0:T(8,128)S(1)} %get-tuple-element.20.refs_0_.own_ref), channel_id=1, source_target_pairs={{1,2},{2,1},{3,4},{4,3},{5,6},{6,5},{7,8},{8,7},{9,10},{10,9},{11,... | collective-permute-start | bytes 73736 | tf_op jit(solution)/shard_map/ppermute | solution.py:38
  10.1 10.6 %collective-permute-start = (f32[48,128]{1,0:T(8,128)S(1)}, f32[48,128]{1,0:T(8,128)S(1)}, u32[]{:S(2)}, u32[]{:S(2)}) collective-permute-start(f32[48,128]{1,0:T(8,128)S(1)} %get-tuple-element.20.refs_0_.own_ref), channel_id=1, source_target_pairs={{0,2},{1,3},{2,4},{3,5},{4,6},{5,7},{6,8},{7,9},{8,10},{9,11},{10,... | collective-permute-start | bytes 73736 | tf_op jit(solution)/shard_map/ppermute | solution.py:28
  31.2 6.1 %collective-permute-start.7 = (f32[54,128]{1,0:T(8,128)S(1)}, f32[54,128]{1,0:T(8,128)S(1)}, u32[]{:S(2)}, u32[]{:S(2)}) collective-permute-start(f32[54,128]{1,0:T(8,128)S(1)} %get-tuple-element.27), channel_id=1, source_target_pairs={{0,1},{1,0},{2,3},{3,2},{4,5},{5,4},{6,7},{7,6},{8,9},{9,8},{10,11... | collective-permute-start | bytes 82952 | tf_op jit(solution)/shard_map/ppermute | solution.py:38
  34.6 12.3 %collective-permute-start.6 = (f32[36,128]{1,0:T(8,128)S(1)}, f32[36,128]{1,0:T(8,128)S(1)}, u32[]{:S(2)}, u32[]{:S(2)}) collective-permute-start(f32[36,128]{1,0:T(8,128)S(1)} %get-tuple-element.25.refs_0_.own_ref), channel_id=1, source_target_pairs={{0,30},{1,31},{2,0},{3,1},{4,2},{5,3},{6,4},{7,5},{8,6},{9,7},{10,... | collective-permute-start | bytes 55304 | tf_op jit(solution)/shard_map/ppermute | solution.py:28
  37.2 9.7 %collective-permute-start.4 = (f32[36,128]{1,0:T(8,128)S(1)}, f32[36,128]{1,0:T(8,128)S(1)}, u32[]{:S(2)}, u32[]{:S(2)}) collective-permute-start(f32[36,128]{1,0:T(8,128)S(1)} %get-tuple-element.25.refs_0_.own_ref), channel_id=1, source_target_pairs={{0,2},{1,3},{2,4},{3,5},{4,6},{5,7},{6,8},{7,9},{8,10},{9,11},{10,... | collective-permute-start | bytes 55304 | tf_op jit(solution)/shard_map/ppermute | solution.py:28
  37.2 9.7 %collective-permute-start.5 = (f32[54,128]{1,0:T(8,128)S(1)}, f32[54,128]{1,0:T(8,128)S(1)}, u32[]{:S(2)}, u32[]{:S(2)}) collective-permute-start(f32[54,128]{1,0:T(8,128)S(1)} %get-tuple-element.26), channel_id=1, source_target_pairs={{1,2},{2,1},{3,4},{4,3},{5,6},{6,5},{7,8},{8,7},{9,10},{10,9},{11,... | collective-permute-start | bytes 82952 | tf_op jit(solution)/shard_map/ppermute | solution.py:38
  46.9 0.7 copy-start.2
  58.0 8.6 %collective-permute-start.8 = (f32[36,128]{1,0:T(8,128)S(1)}, f32[36,128]{1,0:T(8,128)S(1)}, u32[]{:S(2)}, u32[]{:S(2)}) collective-permute-start(f32[36,128]{1,0:T(8,128)S(1)} %get-tuple-element.35), channel_id=1, source_target_pairs={{0,1},{1,0},{2,3},{3,2},{4,5},{5,4},{6,7},{7,6},{8,9},{9,8},{10,11... | collective-permute-start | bytes 55304 | tf_op jit(solution)/shard_map/ppermute | solution.py:38
  64.7 5.1 %collective-permute-start.9 = (f32[36,128]{1,0:T(8,128)S(1)}, f32[36,128]{1,0:T(8,128)S(1)}, u32[]{:S(2)}, u32[]{:S(2)}) collective-permute-start(f32[36,128]{1,0:T(8,128)S(1)} %get-tuple-element.37), channel_id=1, source_target_pairs={{1,2},{2,1},{3,4},{4,3},{5,6},{6,5},{7,8},{8,7},{9,10},{10,9},{11,... | collective-permute-start | bytes 55304 | tf_op jit(solution)/shard_map/ppermute | solution.py:38

commit v10 on v8

--- a/solution.py
+++ b/solution.py
@@ -21,10 +21,21 @@
 vmem_limit = 16 << 20
 
 
-def shifted(value, steps):
+def gathered(value):
     count = lax.axis_size(AXES)
-    pairs = [(source, (source + steps) % count) for source in range(count)]
-    return lax.ppermute(value, AXES, pairs)
+    groups = [[(first + step) % count for step in range(4)] for first in range(0, count, 2)]
+    return [lax.all_gather(value, AXES, axis_index_groups=groups[half::2]) for half in range(2)]
+
+
+def far_blocks(aligned, offset):
+    spot = device_index() % 4
+    low = spot < 2
+    side = spot % 2
+    below = jnp.where(low, offset[side], aligned[side])
+    above = jnp.where(low, aligned[side + 2], offset[side + 2])
+    inner = (spot == 1) | (spot == 2)
+    beside = jnp.where(inner, aligned[jnp.where(spot == 1, 2, 1)], offset[jnp.where(spot == 0, 1, 2)])
+    return (below, beside, above)
 
 
 def swapped(value, first, wrap=True):
@@ -156,10 +167,14 @@
     features += [zeros] * (feature_rows - len(features))
     for row, value in enumerate(features):
         feature_ref[:tiles, row, :] = value
-    blank = jnp.zeros((lanes - feature_rows, lanes), jnp.float32)
+    lane_group = lax.broadcasted_iota(jnp.int32, (lanes, lanes), 1) // feature_rows
+    pairs = chunk // 2
     for tile in range(tiles):
-        block = jnp.concatenate([feature_ref[tile], blank], axis=0)
-        target_ref[tile] = jnp.transpose(block)[:, :feature_rows].astype(jnp.bfloat16)
+        feature = feature_ref[tile]
+        block = jnp.transpose(jnp.concatenate([feature] * (lanes // feature_rows), axis=0))
+        for pair in range(pairs):
+            part = jnp.where(lane_group == pair, block, 0.0)[:, : pairs * feature_rows]
+            target_ref[tile, pair * lanes : (pair + 1) * lanes, :] = part.astype(jnp.bfloat16)
     target_ref[tiles] = target_ref[0]
 
 
@@ -175,20 +190,17 @@
         return [lists_ref[tile, part * chunk + entry] for entry in range(chunk)]
 
     def distances(tile, sources):
-        target = target_ref[tile]
         features = [source_ref[source] for source in sources]
-        return [
-            jnp.dot(target, jnp.concatenate(features[first : first + 2], axis=1), preferred_element_type=jnp.float32)
-            for first in range(0, chunk, 2)
-        ]
+        pairs = [jnp.concatenate(features[first : first + 2], axis=1) for first in range(0, chunk, 2)]
+        return jnp.dot(target_ref[tile], jnp.concatenate(pairs, axis=0), preferred_element_type=jnp.float32)
 
     def kernels(tile, places, squares):
         for first in range(0, lanes, 8):
             strip = slice(first, first + 8)
             sums = [total_ref[tile, row, strip, :] for row in range(4)]
             for entry in range(chunk):
-                column = (entry % 2) * lanes
-                inverse = lax.rsqrt(squares[entry // 2][strip, column : column + lanes])
+                row, column = (entry // 2 * lanes + first, entry % 2 * lanes)
+                inverse = lax.rsqrt(squares[row : row + 8, column : column + lanes])
                 kernel = inverse * inverse * inverse
                 for axis in range(3):
                     sums[axis] = sums[axis] + kernel * places[entry][axis]
@@ -296,13 +308,13 @@
 
 
 def first_finish(
-    listed, own_ref, below, beside, above, total_in, target_ref, weight_own_ref, speed_ref, *refs
+    listed, own_ref, aligned, offset, total_in, target_ref, weight_own_ref, speed_ref, *refs
 ):
     total_ref, lists_ref, weight_ref, place_out, speed_out, sibling_out, beside_out, *scratch = refs
     *tools, sums_ref = scratch
     tiles = own_ref.shape[0] // tools[0].shape[0]
     half = tiles // 2
-    middle, copy = prepare(True, False, listed, own_ref, (below, beside, above), lists_ref, weight_ref, tools)
+    middle, copy = prepare(True, False, listed, own_ref, far_blocks(aligned, offset), lists_ref, weight_ref, tools)
     copy.wait()
     accumulate(tiles, tools[1], tools[5], target_ref, tools[4], total_ref)
     places, speeds = advance(
@@ -328,9 +340,8 @@
     total_tiles,
     cuts_ref,
     own_ref,
-    below,
-    beside,
-    above,
+    aligned,
+    offset,
     total_in,
     target_ref,
     weight_own_ref,
@@ -348,6 +359,7 @@
     *tools, sums_ref, pool_ref = scratch
     tiles = own_ref.shape[0] // 3
     half = tiles // 2
+    below, beside, above = far_blocks(aligned, offset)
     middle, copy = prepare(False, False, None, own_ref, (below, beside, above), lists_ref, weight_ref, tools)
     copy.wait()
     accumulate(tiles, tools[1], tools[5], target_ref, tools[4], total_ref)
@@ -402,6 +414,10 @@
     place_rows(1, total_tiles, cuts_ref, lower, [own_ref[row] for row in range(6)], upper, pool_ref, out_ref)
 
 
+def far(value):
+    return pltpu.with_memory_space_constraint(value, pltpu.HBM)
+
+
 def near(value):
     return pltpu.with_memory_space_constraint(value, pltpu.VMEM)
 
@@ -417,16 +433,17 @@
     list_rows = round_up(tiles + 2, 8)
     vmem = pl.BlockSpec(memory_space=pltpu.VMEM)
     smem = pl.BlockSpec(memory_space=pltpu.SMEM)
+    fetched = "fetched"
 
     def held(*sizes, dtype=jnp.float32):
         return pltpu.VMEM(sizes, dtype)
 
     def call(kernel, name, outs, ins, scratch, flops=0, aliases=None):
-        held_ins = [value if kind is smem else near(value) for kind, value in ins]
+        held_ins = [far(value) if kind in (smem, fetched) else near(value) for kind, value in ins]
         return pl.pallas_call(
             kernel,
             out_shape=outs,
-            in_specs=[kind for kind, _ in ins],
+            in_specs=[vmem if kind is fetched else kind for kind, _ in ins],
             out_specs=[vmem] * len(outs),
             scratch_shapes=scratch,
             input_output_aliases=aliases or {},
@@ -452,17 +469,17 @@
         out_specs=(vmem, vmem),
         compiler_params=pltpu.CompilerParams(vmem_limit_bytes=vmem_limit),
         name="pack",
-    )(particles, occupancy, neighbours)
+    )(far(particles), far(occupancy), far(neighbours))
     pool_scratch = pltpu.VMEM((6, round_up(capacity + tiles, 8), slots), jnp.float32)
     sums_scratch = pltpu.VMEM((4, round_up(tiles, 8), lanes), jnp.float32)
     totals = held(tiles + 1, 4, lanes, lanes)
-    targets = held(tiles + 1, lanes, feature_rows, dtype=jnp.bfloat16)
+    targets = held(tiles + 1, chunk // 2 * lanes, chunk // 2 * feature_rows, dtype=jnp.bfloat16)
     lists = held(list_rows, lanes, dtype=jnp.int32)
     edge = 3 * tiles + 3 * half
     work = 1 << 32
 
     sibling = swapped(packed, 0)
-    beside, below, above = (swapped(packed, 1), shifted(packed, reach), shifted(packed, -reach))
+    aligned, offset = gathered(packed)
     total, target, near_lists, near_weight = call(
         functools.partial(begin, listed, True),
         "first_near",
@@ -475,13 +492,14 @@
         functools.partial(first_finish, listed),
         "first_far",
         [totals, lists, held(far_rows, slots), held(3 * tiles, slots), held(3 * tiles, slots), held(edge, slots), held(edge, slots)],
-        [(vmem, value) for value in (packed, below, beside, above, total, target, near_weight, speed)],
+        [(vmem, packed), (fetched, aligned), (fetched, offset)]
+        + [(vmem, value) for value in (total, target, near_weight, speed)],
         tools(far_rows, 4) + [sums_scratch],
         work,
-        {4: 0},
+        {3: 0},
     )
     sibling = swapped(sibling, 0)
-    beside, below, above = (swapped(beside, 1), shifted(place, reach), shifted(place, -reach))
+    aligned, offset = gathered(beside)
     total, target = call(
         functools.partial(begin, listed, False),
         "second_near",
@@ -500,14 +518,11 @@
             held(6 * half, slots),
             jax.ShapeDtypeStruct((6, capacity, slots), jnp.float32),
         ],
-        [(smem, curve_cuts)]
-        + [
-            (vmem, value)
-            for value in (place, below, beside, above, total, target, near_weight, speed, sibling, far_lists, far_weight)
-        ],
+        [(smem, curve_cuts), (vmem, place), (fetched, aligned), (fetched, offset)]
+        + [(vmem, value) for value in (total, target, near_weight, speed, sibling, far_lists, far_weight)],
         tools(far_rows, 3) + [sums_scratch, pool_scratch],
         work,
-        {5: 0},
+        {4: 0},
     )
     (after_second,) = call(
         functools.partial(third_kernel, total_tiles),

time: 67 us -> 84.4 us (1.26)
  blocking collectives: 0 us -> 31.8 us
  starting transfers between devices: 20.2 us -> 3.94 us
  Pallas kernels: 40.5 us -> 44.4 us
  local copies, waits for them, and re-layouts: 2.15 us -> 0 us
    all_gather x0 -> x4, blocking collectives: none -> 31.8 us  [gathered(): lax.all_gather(value, AXES, axis_index_groups=groups[half::2])]
    ppermute x4 -> x0, starting transfers between devices: 10.5 us -> none  [shifted(): return lax.ppermute(value, AXES, pairs)]
    ppermute x6 -> x4, starting transfers between devices: 9.71 us -> 3.94 us  [swapped(): return lax.ppermute(value, AXES, pairs)]
    pallas_call x5, Pallas kernels: 39.9 us -> 43.6 us  [call(): pl.pallas_call(kernel, out_shape=outs, in_specs=[vmem if kind is fetched...]
    unnamed x8 -> x0, local copies, waits for them, and re-layouts: 2.15 us -> none
    ppermute x6 -> x4, waiting for transfers between devices: 3.18 us -> 2.94 us  [swapped(): return lax.ppermute(value, AXES, pairs)]
  transfers between devices with their start and end apart: 10 -> 4, of which waited for: 1 -> 1; matrix products, arithmetic and copies ran while one was open for 0% -> 0% of each run, Pallas kernels for 27% -> 0%
where the time goes in v10:
time: 84.4 us; the launch traced here: 83.8 us
  Pallas kernels  44.4 us (53%)
  blocking collectives  31.8 us (38%)
  starting transfers between devices  3.94 us (5%)
  waiting for transfers between devices  2.94 us (3%)
    pallas_call x5, Pallas kernels, call(): pl.pallas_call(kernel, out_shape=outs, in_specs=[vmem if kind is fetched...  43.6 us
    all_gather x4, blocking collectives, gathered(): lax.all_gather(value, AXES, axis_index_groups=groups[half::2])  31.8 us
    ppermute x4, starting transfers between devices, swapped(): return lax.ppermute(value, AXES, pairs)  3.94 us
    ppermute x4, waiting for transfers between devices, swapped(): return lax.ppermute(value, AXES, pairs)  2.94 us
  transfers between devices with their start and end apart: 4, of which 1 were waited for; matrix products, arithmetic and copies ran while one was open for 0% of the time, Pallas kernels for 0%

profile of v10, /device:TPU:1, one launch (start us, length us, event | category | flops | bytes accessed | tf_op | source)
XLA Modules:
  0.0 83.8 jit_solution(2892393175446710756)
XLA Ops:
  0.6 0.8 %pack.1 = (f32[48,128]{1,0:T(8,128)S(1)}, f32[36,128]{1,0:T(8,128)S(1)}) custom-call(f32[12,6,128]{2,1,0:T(8,128)} %particles_ref.1, s32[12]{0:T(128)} %occupancy_ref.1, s32[12,16]{1,0:T(8,128)} %neighbours_ref.1), custom_call_target="tpu_custom_call" | custom-call | tf_op jit(solution)/shard_map/pack/pallas_call | solution.py:465
  1.5 0.1 collective-permute-start
  1.6 7.0 %all-gather = f32[192,128]{1,0:T(8,128)} all-gather(f32[48,128]{1,0:T(8,128)S(1)} %get-tuple-element.20.refs_0_.own_ref), channel_id=2, replica_groups={{0,1,2,3},{4,5,6,7},{8,9,10,11},{12,13,14,15},{16,17,18,19},{20,21,22,2..., dimensions={0}, use_global_device_ids=true | all-gather | bytes 122880 | tf_op jit(solution)/shard_map/all_gather | solution.py:27
  8.6 9.6 %all-gather.1 = f32[192,128]{1,0:T(8,128)} all-gather(f32[48,128]{1,0:T(8,128)S(1)} %get-tuple-element.20.refs_0_.own_ref), channel_id=3, replica_groups={{2,3,4,5},{6,7,8,9},{10,11,12,13},{14,15,16,17},{18,19,20,21},{22,23,24..., dimensions={0}, use_global_device_ids=true | all-gather | bytes 122880 | tf_op jit(solution)/shard_map/all_gather | solution.py:27
  18.2 0.0 collective-permute-done.refs_1_
  18.2 10.3 %first_near.1 = (f32[13,4,128,128]{3,2,1,0:T(8,128)S(1)}, bf16[13,256,64]{2,1,0:T(8,128)(2,1)S(1)}, s32[16,128]{1,0:T(8,128)S(1)}, f32[32,128]{1,0:T(8,128)S(1)}) custom-call(f32[48,128]{1,0:T(8,128)S(1)} %get-tuple-element.20.refs_0_.own_ref, f32[48,128]{1,0:T(8,128)S(1)} %collective-permute-done.refs_1_), custom_call_target="tpu_custom_call" | custom-call | flops 4294967296 | bytes 1048576 | tf_op jit(solution)/shard_map/first_near/pallas_call | solution.py:443
  28.5 11.5 %first_far.1 = (f32[13,4,128,128]{3,2,1,0:T(8,128)S(1)}, s32[16,128]{1,0:T(8,128)S(1)}, f32[40,128]{1,0:T(8,128)S(1)}, f32[36,128]{1,0:T(8,128)S(1)}, f32[36,128...) custom-call(f32[48,128]{1,0:T(8,128)S(1)} %get-tuple-element.20.refs_0_.own_ref,, ...), custom_call_target="tpu_custom_call", output_to_operand_aliasing={{0}: (3, {})} | custom-call | flops 4294967296 | bytes 1048576 | tf_op jit(solution)/shard_map/first_far/pallas_call | solution.py:443
  40.0 0.8 collective-permute-start.1
  40.9 9.4 %all-gather.5.offset = f32[4,54,128]{2,1,0:T(8,128)} all-gather(f32[1,54,128]{2,1,0:T(8,128)S(1)} %bitcast.5), channel_id=5, replica_groups={{2,3,4,5},{6,7,8,9},{10,11,12,13},{14,15,16,17},{18,19,20,21},{22,23,24..., dimensions={0}, use_global_device_ids=true | all-gather | bytes 138240 | tf_op jit(solution)/shard_map/all_gather | solution.py:27
  50.3 5.8 %all-gather.4.aligned = f32[4,54,128]{2,1,0:T(8,128)} all-gather(f32[1,54,128]{2,1,0:T(8,128)S(1)} %bitcast.6), channel_id=4, replica_groups={{0,1,2,3},{4,5,6,7},{8,9,10,11},{12,13,14,15},{16,17,18,19},{20,21,22,2..., dimensions={0}, use_global_device_ids=true | all-gather | bytes 138240 | tf_op jit(solution)/shard_map/all_gather | solution.py:27
  56.1 0.0 collective-permute-done.1.refs_1_.sibling_ref
  56.1 9.5 %second_near.1 = (f32[13,4,128,128]{3,2,1,0:T(8,128)S(1)}, bf16[13,256,64]{2,1,0:T(8,128)(2,1)S(1)}) custom-call(f32[36,128]{1,0:T(8,128)S(1)} %get-tuple-element.25.refs_0_.own_ref, f32[54,128]{1,0:T(8,128)S(1)} %collective-permute-done.1.refs_1_.sibling_ref, s32[16,128]{1,0:T(8,128)S(1)} %get-tuple-element.28.refs_2_, ...), custom_call_target="tpu_custom_call" | custom-call | flops 4294967296 | bytes 1048576 | tf_op jit(solution)/shard_map/second_near/pallas_call | solution.py:443
  65.5 11.0 %second_far.1 = (f32[13,4,128,128]{3,2,1,0:T(8,128)S(1)}, f32[6,12,128]{2,1,0:T(8,128)S(1)}, f32[36,128]{1,0:T(8,128)S(1)}, f32[36,128]{1,0:T(8,128)S(1)}, f32[6,24,128]{2,1,0:T(8,128)}) custom-call(s32[2,32]{1,0:T(2,128)} %cuts_ref.3, f32[36,128]{1,0:T(8,128)S(1)} %get-tuple-element.25.refs_0_.own_ref, ...), custom_call_target="tpu_custom_call", output_to_operand_aliasing={{0}: (4, {})} | custom-call | flops 4294967296 | bytes 1048576 | tf_op jit(solution)/shard_map/second_far/pallas_call | solution.py:443
  76.5 0.8 %collective-permute-start.2 = (f32[36,128]{1,0:T(8,128)S(1)}, f32[36,128]{1,0:T(8,128)S(1)}, u32[]{:S(2)}, u32[]{:S(2)}) collective-permute-start(f32[36,128]{1,0:T(8,128)S(1)} %get-tuple-element.35), channel_id=1, source_target_pairs={{0,1},{1,0},{2,3},{3,2},{4,5},{5,4},{6,7},{7,6},{8,9},{9,8},{10,11... | collective-permute-start | bytes 55304 | tf_op jit(solution)/shard_map/ppermute | solution.py:48
  77.4 2.1 %collective-permute-start.3 = (f32[36,128]{1,0:T(8,128)S(1)}, f32[36,128]{1,0:T(8,128)S(1)}, u32[]{:S(2)}, u32[]{:S(2)}) collective-permute-start(f32[36,128]{1,0:T(8,128)S(1)} %get-tuple-element.37), channel_id=1, source_target_pairs={{1,2},{2,1},{3,4},{4,3},{5,6},{6,5},{7,8},{8,7},{9,10},{10,9},{11,... | collective-permute-start | bytes 55304 | tf_op jit(solution)/shard_map/ppermute | solution.py:48
  79.5 0.0 collective-permute-done.2.sibling_ref
  79.5 2.9 %collective-permute-done.3.beside_ref = f32[36,128]{1,0:T(8,128)S(1)} collective-permute-done((f32[36,128]{1,0:T(8,128)S(1)}, f32[36,128]{1,0:T(8,128)S(1)}, u32[]{:S(2)}, u32[]{:S(2)}) %collective-permute-start.3) | collective-permute-done | bytes 18464 | tf_op jit(solution)/shard_map/ppermute | solution.py:48
  82.5 1.3 %place.1 = f32[6,24,128]{2,1,0:T(8,128)} custom-call(s32[2,32]{1,0:T(2,128)} %cuts_ref.3, f32[36,128]{1,0:T(8,128)S(1)} %collective-permute-done.2.sibling_ref, f32[6,12,128]{2,1,0:T(8,128)S(1)} %get-tuple-element.36.own_ref, f32[36,128]{1,0:T(8,128)S(1)} %collective-permute-done.3.beside_ref), custom_call_target="tpu_custom_call" | custom-call | bytes 1048576 | tf_op jit(solution)/shard_map/place/pallas_call | solution.py:443
Async XLA Ops:
  1.5 16.7 %collective-permute-start = (f32[48,128]{1,0:T(8,128)S(1)}, f32[48,128]{1,0:T(8,128)S(1)}, u32[]{:S(2)}, u32[]{:S(2)}) collective-permute-start(f32[48,128]{1,0:T(8,128)S(1)} %get-tuple-element.20.refs_0_.own_ref), channel_id=1, source_target_pairs={{0,1},{1,0},{2,3},{3,2},{4,5},{5,4},{6,7},{7,6},{8,9},{9,8},{10,11... | collective-permute-start | bytes 73736 | tf_op jit(solution)/shard_map/ppermute | solution.py:48
  40.0 16.0 %collective-permute-start.1 = (f32[54,128]{1,0:T(8,128)S(1)}, f32[54,128]{1,0:T(8,128)S(1)}, u32[]{:S(2)}, u32[]{:S(2)}) collective-permute-start(f32[54,128]{1,0:T(8,128)S(1)} %get-tuple-element.27), channel_id=1, source_target_pairs={{0,1},{1,0},{2,3},{3,2},{4,5},{5,4},{6,7},{7,6},{8,9},{9,8},{10,11... | collective-permute-start | bytes 82952 | tf_op jit(solution)/shard_map/ppermute | solution.py:48
  76.5 3.0 %collective-permute-start.2 = (f32[36,128]{1,0:T(8,128)S(1)}, f32[36,128]{1,0:T(8,128)S(1)}, u32[]{:S(2)}, u32[]{:S(2)}) collective-permute-start(f32[36,128]{1,0:T(8,128)S(1)} %get-tuple-element.35), channel_id=1, source_target_pairs={{0,1},{1,0},{2,3},{3,2},{4,5},{5,4},{6,7},{7,6},{8,9},{9,8},{10,11... | collective-permute-start | bytes 55304 | tf_op jit(solution)/shard_map/ppermute | solution.py:48
  77.4 5.1 %collective-permute-start.3 = (f32[36,128]{1,0:T(8,128)S(1)}, f32[36,128]{1,0:T(8,128)S(1)}, u32[]{:S(2)}, u32[]{:S(2)}) collective-permute-start(f32[36,128]{1,0:T(8,128)S(1)} %get-tuple-element.37), channel_id=1, source_target_pairs={{1,2},{2,1},{3,4},{4,3},{5,6},{6,5},{7,8},{8,7},{9,10},{10,9},{11,... | collective-permute-start | bytes 55304 | tf_op jit(solution)/shard_map/ppermute | solution.py:48

commit v11 on v8

--- a/solution.py
+++ b/solution.py
@@ -21,19 +21,14 @@
 vmem_limit = 16 << 20
 
 
-def shifted(value, steps):
-    count = lax.axis_size(AXES)
-    pairs = [(source, (source + steps) % count) for source in range(count)]
-    return lax.ppermute(value, AXES, pairs)
-
-
-def swapped(value, first, wrap=True):
+def swapped(value, first, stride=1, wrap=True):
     count = lax.axis_size(AXES)
     pairs = []
-    for lower in range(first, count, 2):
-        if wrap or lower + 1 < count:
-            upper = (lower + 1) % count
-            pairs += [(lower, upper), (upper, lower)]
+    for start in range(first, count, 2 * stride):
+        for lower in range(start, start + stride):
+            if wrap or lower + stride < count:
+                upper = (lower + stride) % count
+                pairs += [(lower, upper), (upper, lower)]
     return lax.ppermute(value, AXES, pairs)
 
 
@@ -198,17 +193,19 @@
 
     def step(_, carry):
         tile, part = carry
-        work = []
+        waiting = None
         for _ in range(units):
             sources = sources_of(tile, part)
             places = [
                 [jnp.broadcast_to(moment_ref[source, axis : axis + 1, :], (8, lanes)) for axis in range(3)]
                 for source in sources
             ]
-            work.append((tile, places, distances(tile, sources)))
+            item = (tile, places, distances(tile, sources))
+            if waiting is not None:
+                kernels(*waiting)
+            waiting = item
             tile, part = following(tile, part)
-        for item in work:
-            kernels(*item)
+        kernels(*waiting)
         return (tile, part)
 
     zero = jnp.int32(0)
@@ -248,10 +245,12 @@
 
 
 def offsets_of(tiles, near_pair):
-    toward = jnp.where(device_index() % 2 == 0, 1.0, -1.0) * float(tiles)
+    device = device_index()
+    toward = jnp.where(device % 2 == 0, 1.0, -1.0) * float(tiles)
     if near_pair:
         return [0.0, toward]
-    return [-float(reach * tiles), -toward, float(reach * tiles)]
+    across = jnp.where(device % (2 * reach) < reach, 1.0, -1.0) * float(reach * tiles)
+    return [across, -toward, -across]
 
 
 def prepare(first, near_pair, listed, own_ref, blocks, lists_ref, weight_ref, tools):
@@ -296,13 +295,13 @@
 
 
 def first_finish(
-    listed, own_ref, below, beside, above, total_in, target_ref, weight_own_ref, speed_ref, *refs
+    listed, own_ref, aligned, beside, offset, total_in, target_ref, weight_own_ref, speed_ref, *refs
 ):
     total_ref, lists_ref, weight_ref, place_out, speed_out, sibling_out, beside_out, *scratch = refs
     *tools, sums_ref = scratch
     tiles = own_ref.shape[0] // tools[0].shape[0]
     half = tiles // 2
-    middle, copy = prepare(True, False, listed, own_ref, (below, beside, above), lists_ref, weight_ref, tools)
+    middle, copy = prepare(True, False, listed, own_ref, (aligned, beside, offset), lists_ref, weight_ref, tools)
     copy.wait()
     accumulate(tiles, tools[1], tools[5], target_ref, tools[4], total_ref)
     places, speeds = advance(
@@ -328,9 +327,9 @@
     total_tiles,
     cuts_ref,
     own_ref,
-    below,
+    aligned,
     beside,
-    above,
+    offset,
     total_in,
     target_ref,
     weight_own_ref,
@@ -348,7 +347,7 @@
     *tools, sums_ref, pool_ref = scratch
     tiles = own_ref.shape[0] // 3
     half = tiles // 2
-    middle, copy = prepare(False, False, None, own_ref, (below, beside, above), lists_ref, weight_ref, tools)
+    middle, copy = prepare(False, False, None, own_ref, (aligned, beside, offset), lists_ref, weight_ref, tools)
     copy.wait()
     accumulate(tiles, tools[1], tools[5], target_ref, tools[4], total_ref)
     place_own = [part_of(own_ref, tiles, axis) for axis in range(3)]
@@ -402,6 +401,10 @@
     place_rows(1, total_tiles, cuts_ref, lower, [own_ref[row] for row in range(6)], upper, pool_ref, out_ref)
 
 
+def far(value):
+    return pltpu.with_memory_space_constraint(value, pltpu.HBM)
+
+
 def near(value):
     return pltpu.with_memory_space_constraint(value, pltpu.VMEM)
 
@@ -422,7 +425,7 @@
         return pltpu.VMEM(sizes, dtype)
 
     def call(kernel, name, outs, ins, scratch, flops=0, aliases=None):
-        held_ins = [value if kind is smem else near(value) for kind, value in ins]
+        held_ins = [far(value) if kind is smem else near(value) for kind, value in ins]
         return pl.pallas_call(
             kernel,
             out_shape=outs,
@@ -452,7 +455,7 @@
         out_specs=(vmem, vmem),
         compiler_params=pltpu.CompilerParams(vmem_limit_bytes=vmem_limit),
         name="pack",
-    )(particles, occupancy, neighbours)
+    )(far(particles), far(occupancy), far(neighbours))
     pool_scratch = pltpu.VMEM((6, round_up(capacity + tiles, 8), slots), jnp.float32)
     sums_scratch = pltpu.VMEM((4, round_up(tiles, 8), lanes), jnp.float32)
     totals = held(tiles + 1, 4, lanes, lanes)
@@ -462,7 +465,7 @@
     work = 1 << 32
 
     sibling = swapped(packed, 0)
-    beside, below, above = (swapped(packed, 1), shifted(packed, reach), shifted(packed, -reach))
+    beside, aligned, offset = (swapped(packed, 1), swapped(packed, 0, reach), swapped(packed, reach, reach))
     total, target, near_lists, near_weight = call(
         functools.partial(begin, listed, True),
         "first_near",
@@ -475,13 +478,13 @@
         functools.partial(first_finish, listed),
         "first_far",
         [totals, lists, held(far_rows, slots), held(3 * tiles, slots), held(3 * tiles, slots), held(edge, slots), held(edge, slots)],
-        [(vmem, value) for value in (packed, below, beside, above, total, target, near_weight, speed)],
+        [(vmem, value) for value in (packed, aligned, beside, offset, total, target, near_weight, speed)],
         tools(far_rows, 4) + [sums_scratch],
         work,
         {4: 0},
     )
     sibling = swapped(sibling, 0)
-    beside, below, above = (swapped(beside, 1), shifted(place, reach), shifted(place, -reach))
+    beside, aligned, offset = (swapped(beside, 1), swapped(place, 0, reach), swapped(place, reach, reach))
     total, target = call(
         functools.partial(begin, listed, False),
         "second_near",
@@ -503,7 +506,7 @@
         [(smem, curve_cuts)]
         + [
             (vmem, value)
-            for value in (place, below, beside, above, total, target, near_weight, speed, sibling, far_lists, far_weight)
+            for value in (place, aligned, beside, offset, total, target, near_weight, speed, sibling, far_lists, far_weight)
         ],
         tools(far_rows, 3) + [sums_scratch, pool_scratch],
         work,

time: 67 us -> 61.5 us (0.918)
  starting transfers between devices: 20.2 us -> 17.7 us
  local copies, waits for them, and re-layouts: 2.15 us -> 0 us
    ppermute x4 -> x0, starting transfers between devices: 10.5 us -> none  [shifted(): return lax.ppermute(value, AXES, pairs)]
    ppermute x6 -> x10, starting transfers between devices: 9.71 us -> 17.7 us  [swapped(): return lax.ppermute(value, AXES, pairs)]
    unnamed x8 -> x0, local copies, waits for them, and re-layouts: 2.15 us -> none
    pallas_call x5, Pallas kernels: 39.9 us -> 39.1 us  [call(): pl.pallas_call(kernel, out_shape=outs, in_specs=[kind for kind, _ in ins]...]
    ppermute x6 -> x10, waiting for transfers between devices: 3.18 us -> 2.6 us  [swapped(): return lax.ppermute(value, AXES, pairs)]
  transfers between devices with their start and end apart: 10 -> 10, of which waited for: 1 -> 1; matrix products, arithmetic and copies ran while one was open for 0% -> 0% of each run, Pallas kernels for 27% -> 28%
where the time goes in v11:
time: 61.5 us; the launch traced here: 61 us
  Pallas kernels  40 us (65%)
  starting transfers between devices  17.7 us (29%)
  waiting for transfers between devices  2.6 us (4%)
  between operations  0.75 us (1%)
    pallas_call x5, Pallas kernels, call(): pl.pallas_call(kernel, out_shape=outs, in_specs=[kind for kind, _ in ins]...  39.1 us
    ppermute x10, starting transfers between devices, swapped(): return lax.ppermute(value, AXES, pairs)  17.7 us
    ppermute x10, waiting for transfers between devices, swapped(): return lax.ppermute(value, AXES, pairs)  2.6 us
  transfers between devices with their start and end apart: 10, of which 1 were waited for; matrix products, arithmetic and copies ran while one was open for 0% of the time, Pallas kernels for 28%

profile of v11, /device:TPU:1, one launch (start us, length us, event | category | flops | bytes accessed | tf_op | source)
XLA Modules:
  0.0 61.0 jit_solution(13565934438442156171)
XLA Ops:
  0.6 0.8 %pack.1 = (f32[48,128]{1,0:T(8,128)S(1)}, f32[36,128]{1,0:T(8,128)S(1)}) custom-call(f32[12,6,128]{2,1,0:T(8,128)} %particles_ref.1, s32[12]{0:T(128)} %occupancy_ref.1, s32[12,16]{1,0:T(8,128)} %neighbours_ref.1), custom_call_target="tpu_custom_call" | custom-call | tf_op jit(solution)/shard_map/pack/pallas_call | solution.py:451
  1.5 0.1 collective-permute-start.3
  1.6 6.7 %collective-permute-start.2 = (f32[48,128]{1,0:T(8,128)S(1)}, f32[48,128]{1,0:T(8,128)S(1)}, u32[]{:S(2)}, u32[]{:S(2)}) collective-permute-start(f32[48,128]{1,0:T(8,128)S(1)} %get-tuple-element.20.refs_0_.own_ref), channel_id=1, source_target_pairs={{2,4},{4,2},{3,5},{5,3},{6,8},{8,6},{7,9},{9,7},{10,12},{12,10},{1... | collective-permute-start | bytes 73736 | tf_op jit(solution)/shard_map/ppermute | solution.py:32
  8.3 0.0 collective-permute-start.1
  8.3 0.0 collective-permute-start
  8.3 0.0 collective-permute-done.3.refs_1_
  8.3 9.0 %first_near.1 = (f32[13,4,128,128]{3,2,1,0:T(8,128)S(1)}, bf16[13,128,32]{2,1,0:T(8,128)(2,1)S(1)}, s32[16,128]{1,0:T(8,128)S(1)}, f32[32,128]{1,0:T(8,128)S(1)}) custom-call(f32[48,128]{1,0:T(8,128)S(1)} %get-tuple-element.20.refs_0_.own_ref, f32[48,128]{1,0:T(8,128)S(1)} %collective-permute-done.3.refs_1_), custom_call_target="tpu_custom_call" | custom-call | flops 4294967296 | bytes 1048576 | tf_op jit(solution)/shard_map/first_near/pallas_call | solution.py:429
  17.2 0.0 collective-permute-done.2.offset
  17.2 0.0 collective-permute-done.1.beside
  17.3 0.0 collective-permute-done.aligned
  17.3 10.3 %first_far.1 = (f32[13,4,128,128]{3,2,1,0:T(8,128)S(1)}, s32[16,128]{1,0:T(8,128)S(1)}, f32[40,128]{1,0:T(8,128)S(1)}, f32[36,128]{1,0:T(8,128)S(1)}, f32[36,128...) custom-call(f32[48,128]{1,0:T(8,128)S(1)} %get-tuple-element.20.refs_0_.own_ref,, ...), custom_call_target="tpu_custom_call", output_to_operand_aliasing={{0}: (4, {})} | custom-call | flops 4294967296 | bytes 1048576 | tf_op jit(solution)/shard_map/first_far/pallas_call | solution.py:429
  27.5 1.7 %collective-permute-start.7 = (f32[54,128]{1,0:T(8,128)S(1)}, f32[54,128]{1,0:T(8,128)S(1)}, u32[]{:S(2)}, u32[]{:S(2)}) collective-permute-start(f32[54,128]{1,0:T(8,128)S(1)} %get-tuple-element.27), channel_id=1, source_target_pairs={{0,1},{1,0},{2,3},{3,2},{4,5},{5,4},{6,7},{7,6},{8,9},{9,8},{10,11... | collective-permute-start | bytes 82952 | tf_op jit(solution)/shard_map/ppermute | solution.py:32
  29.2 4.3 %collective-permute-start.6 = (f32[36,128]{1,0:T(8,128)S(1)}, f32[36,128]{1,0:T(8,128)S(1)}, u32[]{:S(2)}, u32[]{:S(2)}) collective-permute-start(f32[36,128]{1,0:T(8,128)S(1)} %get-tuple-element.25.refs_0_.own_ref), channel_id=1, source_target_pairs={{2,4},{4,2},{3,5},{5,3},{6,8},{8,6},{7,9},{9,7},{10,12},{12,10},{1... | collective-permute-start | bytes 55304 | tf_op jit(solution)/shard_map/ppermute | solution.py:32
  33.5 0.0 collective-permute-start.4
  33.5 2.3 %collective-permute-start.5 = (f32[54,128]{1,0:T(8,128)S(1)}, f32[54,128]{1,0:T(8,128)S(1)}, u32[]{:S(2)}, u32[]{:S(2)}) collective-permute-start(f32[54,128]{1,0:T(8,128)S(1)} %get-tuple-element.26), channel_id=1, source_target_pairs={{1,2},{2,1},{3,4},{4,3},{5,6},{6,5},{7,8},{8,7},{9,10},{10,9},{11,... | collective-permute-start | bytes 82952 | tf_op jit(solution)/shard_map/ppermute | solution.py:32
  35.9 0.0 collective-permute-done.7.refs_1_.sibling_ref
  35.9 8.1 %second_near.1 = (f32[13,4,128,128]{3,2,1,0:T(8,128)S(1)}, bf16[13,128,32]{2,1,0:T(8,128)(2,1)S(1)}) custom-call(f32[36,128]{1,0:T(8,128)S(1)} %get-tuple-element.25.refs_0_.own_ref, f32[54,128]{1,0:T(8,128)S(1)} %collective-permute-done.7.refs_1_.sibling_ref, s32[16,128]{1,0:T(8,128)S(1)} %get-tuple-element.28.refs_2_, ...), custom_call_target="tpu_custom_call" | custom-call | flops 4294967296 | bytes 1048576 | tf_op jit(solution)/shard_map/second_near/pallas_call | solution.py:429
  44.0 0.0 collective-permute-done.6.offset
  44.0 0.0 collective-permute-done.4.aligned
  44.0 0.0 collective-permute-done.5.beside
  44.0 10.5 %second_far.1 = (f32[13,4,128,128]{3,2,1,0:T(8,128)S(1)}, f32[6,12,128]{2,1,0:T(8,128)S(1)}, f32[36,128]{1,0:T(8,128)S(1)}, f32[36,128]{1,0:T(8,128)S(1)}, f32[6,24,128]{2,1,0:T(8,128)}) custom-call(s32[2,32]{1,0:T(2,128)} %cuts_ref.3, f32[36,128]{1,0:T(8,128)S(1)} %get-tuple-element.25.refs_0_.own_ref, ...), custom_call_target="tpu_custom_call", output_to_operand_aliasing={{0}: (5, {})} | custom-call | flops 4294967296 | bytes 1048576 | tf_op jit(solution)/shard_map/second_far/pallas_call | solution.py:429
  54.5 0.1 collective-permute-start.8
  54.5 2.5 %collective-permute-start.9 = (f32[36,128]{1,0:T(8,128)S(1)}, f32[36,128]{1,0:T(8,128)S(1)}, u32[]{:S(2)}, u32[]{:S(2)}) collective-permute-start(f32[36,128]{1,0:T(8,128)S(1)} %get-tuple-element.37), channel_id=1, source_target_pairs={{1,2},{2,1},{3,4},{4,3},{5,6},{6,5},{7,8},{8,7},{9,10},{10,9},{11,... | collective-permute-start | bytes 55304 | tf_op jit(solution)/shard_map/ppermute | solution.py:32
  57.1 0.0 collective-permute-done.8.sibling_ref
  57.1 2.6 %collective-permute-done.9.beside_ref = f32[36,128]{1,0:T(8,128)S(1)} collective-permute-done((f32[36,128]{1,0:T(8,128)S(1)}, f32[36,128]{1,0:T(8,128)S(1)}, u32[]{:S(2)}, u32[]{:S(2)}) %collective-permute-start.9) | collective-permute-done | bytes 18464 | tf_op jit(solution)/shard_map/ppermute | solution.py:32
  59.6 1.3 %place.1 = f32[6,24,128]{2,1,0:T(8,128)} custom-call(s32[2,32]{1,0:T(2,128)} %cuts_ref.3, f32[36,128]{1,0:T(8,128)S(1)} %collective-permute-done.8.sibling_ref, f32[6,12,128]{2,1,0:T(8,128)S(1)} %get-tuple-element.36.own_ref, f32[36,128]{1,0:T(8,128)S(1)} %collective-permute-done.9.beside_ref), custom_call_target="tpu_custom_call" | custom-call | bytes 1048576 | tf_op jit(solution)/shard_map/place/pallas_call | solution.py:429
Async XLA Ops:
  1.5 6.8 %collective-permute-start.3 = (f32[48,128]{1,0:T(8,128)S(1)}, f32[48,128]{1,0:T(8,128)S(1)}, u32[]{:S(2)}, u32[]{:S(2)}) collective-permute-start(f32[48,128]{1,0:T(8,128)S(1)} %get-tuple-element.20.refs_0_.own_ref), channel_id=1, source_target_pairs={{0,1},{1,0},{2,3},{3,2},{4,5},{5,4},{6,7},{7,6},{8,9},{9,8},{10,11... | collective-permute-start | bytes 73736 | tf_op jit(solution)/shard_map/ppermute | solution.py:32
  1.6 15.6 %collective-permute-start.2 = (f32[48,128]{1,0:T(8,128)S(1)}, f32[48,128]{1,0:T(8,128)S(1)}, u32[]{:S(2)}, u32[]{:S(2)}) collective-permute-start(f32[48,128]{1,0:T(8,128)S(1)} %get-tuple-element.20.refs_0_.own_ref), channel_id=1, source_target_pairs={{2,4},{4,2},{3,5},{5,3},{6,8},{8,6},{7,9},{9,7},{10,12},{12,10},{1... | collective-permute-start | bytes 73736 | tf_op jit(solution)/shard_map/ppermute | solution.py:32
  8.3 9.0 %collective-permute-start.1 = (f32[48,128]{1,0:T(8,128)S(1)}, f32[48,128]{1,0:T(8,128)S(1)}, u32[]{:S(2)}, u32[]{:S(2)}) collective-permute-start(f32[48,128]{1,0:T(8,128)S(1)} %get-tuple-element.20.refs_0_.own_ref), channel_id=1, source_target_pairs={{1,2},{2,1},{3,4},{4,3},{5,6},{6,5},{7,8},{8,7},{9,10},{10,9},{11,... | collective-permute-start | bytes 73736 | tf_op jit(solution)/shard_map/ppermute | solution.py:32
  8.3 9.0 %collective-permute-start = (f32[48,128]{1,0:T(8,128)S(1)}, f32[48,128]{1,0:T(8,128)S(1)}, u32[]{:S(2)}, u32[]{:S(2)}) collective-permute-start(f32[48,128]{1,0:T(8,128)S(1)} %get-tuple-element.20.refs_0_.own_ref), channel_id=1, source_target_pairs={{0,2},{2,0},{1,3},{3,1},{4,6},{6,4},{5,7},{7,5},{8,10},{10,8},{9,1... | collective-permute-start | bytes 73736 | tf_op jit(solution)/shard_map/ppermute | solution.py:32
  27.5 8.3 %collective-permute-start.7 = (f32[54,128]{1,0:T(8,128)S(1)}, f32[54,128]{1,0:T(8,128)S(1)}, u32[]{:S(2)}, u32[]{:S(2)}) collective-permute-start(f32[54,128]{1,0:T(8,128)S(1)} %get-tuple-element.27), channel_id=1, source_target_pairs={{0,1},{1,0},{2,3},{3,2},{4,5},{5,4},{6,7},{7,6},{8,9},{9,8},{10,11... | collective-permute-start | bytes 82952 | tf_op jit(solution)/shard_map/ppermute | solution.py:32
  29.2 14.7 %collective-permute-start.6 = (f32[36,128]{1,0:T(8,128)S(1)}, f32[36,128]{1,0:T(8,128)S(1)}, u32[]{:S(2)}, u32[]{:S(2)}) collective-permute-start(f32[36,128]{1,0:T(8,128)S(1)} %get-tuple-element.25.refs_0_.own_ref), channel_id=1, source_target_pairs={{2,4},{4,2},{3,5},{5,3},{6,8},{8,6},{7,9},{9,7},{10,12},{12,10},{1... | collective-permute-start | bytes 55304 | tf_op jit(solution)/shard_map/ppermute | solution.py:32
  33.5 10.5 %collective-permute-start.4 = (f32[36,128]{1,0:T(8,128)S(1)}, f32[36,128]{1,0:T(8,128)S(1)}, u32[]{:S(2)}, u32[]{:S(2)}) collective-permute-start(f32[36,128]{1,0:T(8,128)S(1)} %get-tuple-element.25.refs_0_.own_ref), channel_id=1, source_target_pairs={{0,2},{2,0},{1,3},{3,1},{4,6},{6,4},{5,7},{7,5},{8,10},{10,8},{9,1... | collective-permute-start | bytes 55304 | tf_op jit(solution)/shard_map/ppermute | solution.py:32
  33.5 10.5 %collective-permute-start.5 = (f32[54,128]{1,0:T(8,128)S(1)}, f32[54,128]{1,0:T(8,128)S(1)}, u32[]{:S(2)}, u32[]{:S(2)}) collective-permute-start(f32[54,128]{1,0:T(8,128)S(1)} %get-tuple-element.26), channel_id=1, source_target_pairs={{1,2},{2,1},{3,4},{4,3},{5,6},{6,5},{7,8},{8,7},{9,10},{10,9},{11,... | collective-permute-start | bytes 82952 | tf_op jit(solution)/shard_map/ppermute | solution.py:32
  54.5 2.6 %collective-permute-start.8 = (f32[36,128]{1,0:T(8,128)S(1)}, f32[36,128]{1,0:T(8,128)S(1)}, u32[]{:S(2)}, u32[]{:S(2)}) collective-permute-start(f32[36,128]{1,0:T(8,128)S(1)} %get-tuple-element.35), channel_id=1, source_target_pairs={{0,1},{1,0},{2,3},{3,2},{4,5},{5,4},{6,7},{7,6},{8,9},{9,8},{10,11... | collective-permute-start | bytes 55304 | tf_op jit(solution)/shard_map/ppermute | solution.py:32
  54.5 5.1 %collective-permute-start.9 = (f32[36,128]{1,0:T(8,128)S(1)}, f32[36,128]{1,0:T(8,128)S(1)}, u32[]{:S(2)}, u32[]{:S(2)}) collective-permute-start(f32[36,128]{1,0:T(8,128)S(1)} %get-tuple-element.37), channel_id=1, source_target_pairs={{1,2},{2,1},{3,4},{4,3},{5,6},{6,5},{7,8},{8,7},{9,10},{10,9},{11,... | collective-permute-start | bytes 55304 | tf_op jit(solution)/shard_map/ppermute | solution.py:32
